TPU v7x, 32 devices: a whole 2x2x4 slice. The times are simulated.
32 devices in a mesh: mod: 16 (over z, y, core), pair: 2 (over x).
Axes of the slice: x: 2, y: 2, z: 4, core: 2. Of those that a mesh axis runs over, the one named last changes fastest.
Arguments:
- rows_input: bfloat16 [65536, 768], P(('mod', 'pair')), may hold values from -6 to 6
- grad_out: bfloat16 [65536, 768], P(('mod', 'pair')), may hold values from -6 to 6
- w_qkv: bfloat16 [768, 2304], P('pair', 'mod'), may hold values from -0.21875 to 0.21875
- w_out: bfloat16 [768, 768], P('pair', 'mod'), may hold values from -0.625 to 0.625
- w_up: bfloat16 [768, 3072], P('pair', 'mod'), may hold values from -0.21875 to 0.21875
- w_down: bfloat16 [3072, 768], P('pair', 'mod'), may hold values from -0.109375 to 0.109375
- vectors: bfloat16 [8, 768], P('pair', 'mod'), may hold values from -1.6 to 1.6
- b_up: bfloat16 [8, 384], P('pair', 'mod'), may hold values from -3 to 3
- live_rows: int32 [1024], P(('mod', 'pair')), may hold values from 16 to 64, as said below
Outputs:
- rows_output: bfloat16 [65536, 768], P(('mod', 'pair'))
- grad_input: float32 [65536, 768], P(('mod', 'pair'))
- grad_w_qkv: float32 [768, 2304], P('pair', 'mod')
- grad_w_out: float32 [768, 768], P('pair', 'mod')
- grad_w_up: float32 [768, 3072], P('pair', 'mod')
- grad_w_down: float32 [3072, 768], P('pair', 'mod')
- grad_vectors: float32 [8, 768], P('pair', 'mod')
- grad_b_up: float32 [8, 384], P('pair', 'mod')
Inputs may be any that keep to these rules, and one draw needn't show every extreme that they name: `live_rows`: each entry lies between 16 and 64; both ends occur in every draw.
All inputs are finite; a program needn't handle non-finite values.
Results may differ from a plain program's by a relative error of at most 0.019.
Values may be sent and summed in bfloat16 or wider, within the bound.
No kernel may reach another device: no remote copies, remote signals or barrier semaphores. Data moves between devices by JAX's collectives and lax.ppermute only.
A program may use at most 320 MiB of HBM per device.

v0:
```python
import jax
import jax.numpy as jnp
from jax import lax
from jax.sharding import PartitionSpec as P

HEADS = 12
HEAD_DIM = 64
SLOTS = 64
PAIRS_DEV = 8
MICRO = 4


EPS = 1e-05
NEG = -1000000000.0


def shifted(shard, axis, by):
    count = lax.axis_size(axis)
    return lax.ppermute(shard, axis, [(i, (i + by) % count) for i in range(count)])


def norm_rows(values, gain, shift):
    centre = values - jnp.mean(values, -1, keepdims=True)
    spread = jnp.mean(centre * centre, -1, keepdims=True)
    return centre * lax.rsqrt(spread + EPS) * gain + shift


def gelu_exact(values):
    return jax.nn.gelu(values, approximate=False)


def plain_dot(left, right):
    return jnp.dot(left, right, preferred_element_type=jnp.float32)


def left_dot(left, right):
    return lax.dot_general(
        left, right, (((0,), (0,)), ((), ())), preferred_element_type=jnp.float32
    )


def right_dot(left, right):
    return lax.dot_general(
        left, right, (((1,), (1,)), ((), ())), preferred_element_type=jnp.float32
    )


def fetch(w_qkv, w_out, w_up, w_down, vectors, b_up):
    sectioned = (
        lax.all_gather(w_qkv, "pair", axis=0, tiled=True),
        lax.all_gather(w_out, "pair", axis=0, tiled=True),
        lax.all_gather(w_up, "pair", axis=0, tiled=True),
        lax.all_gather(w_down, "pair", axis=0, tiled=True),
        lax.all_gather(vectors, "pair", axis=0, tiled=True),
        lax.all_gather(b_up, "pair", axis=0, tiled=True),
    )
    return (
        lax.all_gather(sectioned[0], "mod", axis=1, tiled=True),
        lax.all_gather(sectioned[1], "mod", axis=1, tiled=True),
        lax.all_gather(sectioned[2], "mod", axis=1, tiled=True),
        lax.all_gather(sectioned[3], "mod", axis=1, tiled=True),
        lax.all_gather(sectioned[4], "mod", axis=1, tiled=True),
        lax.all_gather(sectioned[5], "mod", axis=1, tiled=True),
    )


def reduce_grads(terms):
    sectioned = (
        lax.psum_scatter(
            terms[0].astype(jnp.bfloat16), "mod", scatter_dimension=1, tiled=True
        ).astype(jnp.float32),
        lax.psum_scatter(
            terms[1].astype(jnp.bfloat16), "mod", scatter_dimension=1, tiled=True
        ).astype(jnp.float32),
        lax.psum_scatter(
            terms[2].astype(jnp.bfloat16), "mod", scatter_dimension=1, tiled=True
        ).astype(jnp.float32),
        lax.psum_scatter(
            terms[3].astype(jnp.bfloat16), "mod", scatter_dimension=1, tiled=True
        ).astype(jnp.float32),
        lax.psum_scatter(
            terms[4].astype(jnp.bfloat16), "mod", scatter_dimension=1, tiled=True
        ).astype(jnp.float32),
        lax.psum_scatter(
            terms[5].astype(jnp.bfloat16), "mod", scatter_dimension=1, tiled=True
        ).astype(jnp.float32),
    )
    return (
        lax.psum_scatter(
            sectioned[0].astype(jnp.bfloat16), "pair", scatter_dimension=0, tiled=True
        ).astype(jnp.float32),
        lax.psum_scatter(
            sectioned[1].astype(jnp.bfloat16), "pair", scatter_dimension=0, tiled=True
        ).astype(jnp.float32),
        lax.psum_scatter(
            sectioned[2].astype(jnp.bfloat16), "pair", scatter_dimension=0, tiled=True
        ).astype(jnp.float32),
        lax.psum_scatter(
            sectioned[3].astype(jnp.bfloat16), "pair", scatter_dimension=0, tiled=True
        ).astype(jnp.float32),
        lax.psum_scatter(
            sectioned[4].astype(jnp.bfloat16), "pair", scatter_dimension=0, tiled=True
        ).astype(jnp.float32),
        lax.psum_scatter(
            sectioned[5].astype(jnp.bfloat16), "pair", scatter_dimension=0, tiled=True
        ).astype(jnp.float32),
    )


def key_mask(live, live_other, slots):
    position = jnp.arange(2 * slots)
    valid = jnp.where(
        position[None, :] < slots,
        position[None, :] < live[:, None],
        position[None, :] - slots < live_other[:, None],
    )
    return valid[:, None, None, :]


def forward(rows_in, live, fetched, half):
    wqkv_full, wout_full, wup_full, wdown_full, vec_full, bup_full = fetched
    width = rows_in.shape[1]
    pairs = live.shape[0]
    slots = rows_in.shape[0] // pairs
    scale = HEAD_DIM ** (-0.5)
    vec_wide = vec_full.astype(jnp.float32)
    bias_up = bup_full.astype(jnp.float32).reshape(-1)
    bias_qkv = jnp.concatenate([vec_wide[0], jnp.zeros((width,), jnp.float32), vec_wide[1]])
    projected = (plain_dot(rows_in, wqkv_full) + bias_qkv).astype(jnp.bfloat16)
    key_own = projected[:, width : 2 * width].reshape(pairs, slots, width)
    value_own = projected[:, 2 * width :].reshape(pairs, slots, width)
    key_far, value_far, live_far = shifted(
        (key_own, value_own, live.astype(jnp.bfloat16)), "mod", half
    )
    queries = projected[:, :width].reshape(pairs, slots, HEADS, HEAD_DIM)
    keys_all = jnp.concatenate([key_own, key_far], 1).reshape(pairs, 2 * slots, HEADS, HEAD_DIM)
    values_all = jnp.concatenate([value_own, value_far], 1).reshape(
        pairs, 2 * slots, HEADS, HEAD_DIM
    )
    valid = key_mask(live, live_far.astype(jnp.int32), slots)
    scores = (
        jnp.einsum("pqhd,pkhd->phqk", queries, keys_all, preferred_element_type=jnp.float32) * scale
    )
    scores = jnp.where(valid, scores, NEG)
    peak = jnp.max(scores, -1, keepdims=True)
    expo = jnp.exp(scores - peak)
    total = jnp.sum(expo, -1, keepdims=True)
    attend = expo / total
    log_total = peak + jnp.log(total)
    mixed = jnp.einsum(
        "phqk,pkhd->pqhd",
        attend.astype(jnp.bfloat16),
        values_all,
        preferred_element_type=jnp.float32,
    )
    mixed_low = mixed.reshape(pairs * slots, width).astype(jnp.bfloat16)
    branch = plain_dot(mixed_low, wout_full) + vec_wide[2]
    summed_one = rows_in.astype(jnp.float32) + branch
    first = norm_rows(summed_one, vec_wide[4], vec_wide[5])
    first_low = first.astype(jnp.bfloat16)
    inner = plain_dot(first_low, wup_full) + bias_up
    act_low = gelu_exact(inner).astype(jnp.bfloat16)
    outer = plain_dot(act_low, wdown_full) + vec_wide[3]
    summed_two = first + outer
    result = norm_rows(summed_two, vec_wide[6], vec_wide[7]).astype(jnp.bfloat16)
    kept = (
        rows_in,
        queries,
        keys_all,
        values_all,
        valid,
        log_total,
        mixed_low,
        summed_one,
        first_low,
        inner,
        act_low,
        summed_two,
    )
    return (result, kept)


def backward(kept, grad_rows, fetched, half):
    wqkv_full, wout_full, wup_full, wdown_full, vec_full, bup_full = fetched
    (
        rows_in,
        queries,
        keys_all,
        values_all,
        valid,
        log_total,
        mixed_low,
        summed_one,
        first_low,
        inner,
        act_low,
        summed_two,
    ) = kept
    width = rows_in.shape[1]
    pairs = queries.shape[0]
    slots = queries.shape[1]
    rows_count = pairs * slots
    scale = HEAD_DIM ** (-0.5)
    vec_wide = vec_full.astype(jnp.float32)
    unused, norm_two_back = jax.vjp(norm_rows, summed_two, vec_wide[6], vec_wide[7])
    grad_two, gain_two_grad, shift_two_grad = norm_two_back(grad_rows)
    outer_low = grad_two.astype(jnp.bfloat16)
    down_bias_grad = jnp.sum(outer_low.astype(jnp.float32), 0)
    down_grad = left_dot(act_low, outer_low)
    act_grad = right_dot(outer_low, wdown_full)
    unused_act, gelu_back = jax.vjp(gelu_exact, inner)
    inner_grad = gelu_back(act_grad)[0]
    inner_low = inner_grad.astype(jnp.bfloat16)
    up_bias_grad = jnp.sum(inner_low.astype(jnp.float32), 0)
    up_grad = left_dot(first_low, inner_low)
    first_grad = grad_two + right_dot(inner_low, wup_full)
    unused_one, norm_one_back = jax.vjp(norm_rows, summed_one, vec_wide[4], vec_wide[5])
    grad_one, gain_one_grad, shift_one_grad = norm_one_back(first_grad)
    branch_low = grad_one.astype(jnp.bfloat16)
    out_bias_grad = jnp.sum(branch_low.astype(jnp.float32), 0)
    out_grad = left_dot(mixed_low, branch_low)
    mixed_grad = (
        right_dot(branch_low, wout_full).astype(jnp.bfloat16).reshape(pairs, slots, HEADS, HEAD_DIM)
    )
    scores = (
        jnp.einsum("pqhd,pkhd->phqk", queries, keys_all, preferred_element_type=jnp.float32) * scale
    )
    scores = jnp.where(valid, scores, NEG)
    attend = jnp.exp(scores - log_total)
    attend_grad = jnp.einsum(
        "pqhd,pkhd->phqk", mixed_grad, values_all, preferred_element_type=jnp.float32
    )
    score_grad = attend * (attend_grad - jnp.sum(attend * attend_grad, -1, keepdims=True))
    score_low = score_grad.astype(jnp.bfloat16)
    query_grad = (
        jnp.einsum("phqk,pkhd->pqhd", score_low, keys_all, preferred_element_type=jnp.float32)
        * scale
    )
    key_grad = (
        jnp.einsum("phqk,pqhd->pkhd", score_low, queries, preferred_element_type=jnp.float32)
        * scale
    )
    value_grad = jnp.einsum(
        "phqk,pqhd->pkhd",
        attend.astype(jnp.bfloat16),
        mixed_grad,
        preferred_element_type=jnp.float32,
    )
    key_grad = key_grad.reshape(pairs, 2 * slots, width)
    value_grad = value_grad.reshape(pairs, 2 * slots, width)
    back_key, back_value = (
        shifted(key_grad[:, slots:].astype(jnp.bfloat16), "mod", half).astype(jnp.float32),
        shifted(value_grad[:, slots:].astype(jnp.bfloat16), "mod", half).astype(jnp.float32),
    )
    key_total = (key_grad[:, :slots] + back_key).reshape(rows_count, width)
    value_total = (value_grad[:, :slots] + back_value).reshape(rows_count, width)
    qkv_low = jnp.concatenate(
        [query_grad.reshape(rows_count, width), key_total, value_total], 1
    ).astype(jnp.bfloat16)
    qkv_wide = qkv_low.astype(jnp.float32)
    query_bias_grad = jnp.sum(qkv_wide[:, :width], 0)
    value_bias_grad = jnp.sum(qkv_wide[:, 2 * width :], 0)
    qkv_weight_grad = left_dot(rows_in, qkv_low)
    input_grad = grad_one + right_dot(qkv_low, wqkv_full)
    vector_grad = jnp.stack(
        [
            query_bias_grad,
            value_bias_grad,
            out_bias_grad,
            down_bias_grad,
            gain_one_grad,
            shift_one_grad,
            gain_two_grad,
            shift_two_grad,
        ]
    )
    terms = (
        qkv_weight_grad,
        out_grad,
        up_grad,
        down_grad,
        vector_grad,
        up_bias_grad.reshape(8, -1),
    )
    return (terms, input_grad)


def per_device(rows_input, grad_out, w_qkv, w_out, w_up, w_down, vectors, b_up, live_rows):
    half = lax.axis_size("mod") // 2
    rows_step = PAIRS_DEV * SLOTS
    totals = tuple(
        (
            jnp.zeros(shard.shape, jnp.float32)
            for shard in (w_qkv, w_out, w_up, w_down, vectors, b_up)
        )
    )
    outputs = []
    input_grads = []
    for micro_step in range(MICRO):
        rows_in = rows_input[micro_step * rows_step : (micro_step + 1) * rows_step]
        grad_rows = grad_out[micro_step * rows_step : (micro_step + 1) * rows_step].astype(
            jnp.float32
        )
        live = live_rows[micro_step * PAIRS_DEV : (micro_step + 1) * PAIRS_DEV]
        fetched = fetch(w_qkv, w_out, w_up, w_down, vectors, b_up)
        result, kept = forward(rows_in, live, fetched, half)
        fetched = fetch(w_qkv, w_out, w_up, w_down, vectors, b_up)
        terms, input_grad = backward(kept, grad_rows, fetched, half)
        outputs.append(result)
        input_grads.append(input_grad)
        shares = reduce_grads(terms)
        totals = tuple((running + share for running, share in zip(totals, shares)))
    return (
        jnp.concatenate(outputs, 0),
        jnp.concatenate(input_grads, 0),
        totals[0],
        totals[1],
        totals[2],
        totals[3],
        totals[4],
        totals[5],
    )


def solution(mesh):
    placed = (
        P(("mod", "pair"), None),
        P(("mod", "pair"), None),
        P("pair", "mod"),
        P("pair", "mod"),
        P("pair", "mod"),
        P("pair", "mod"),
        P("pair", "mod"),
        P("pair", "mod"),
        P(("mod", "pair")),
    )
    return jax.shard_map(
        per_device,
        mesh=mesh,
        in_specs=placed,
        out_specs=(
            P(("mod", "pair"), None),
            P(("mod", "pair"), None),
            P("pair", "mod"),
            P("pair", "mod"),
            P("pair", "mod"),
            P("pair", "mod"),
            P("pair", "mod"),
            P("pair", "mod"),
        ),
        check_vma=False,
    )
```

profile of v0, /device:TPU:0, one launch (start us, length us, event | category | flops | bytes accessed | tf_op | source)
XLA Modules:
  0.0 2423.6 jit_solution(2118831239353846040)
XLA Ops:
  50.1 21.8 all-gather.3
  71.9 17.6 all-gather.1
  204.8 78.0 %collective-permute-done.2 = bf16[8,64,768]{2,1,0:T(8,128)(2,1)} collective-permute-done((bf16[8,64,768]{2,1,0:T(8,128)(2,1)}, bf16[8,64,768]{2,1,0:T(8,128)(2,1)}, u32[]{:S(2)}, u32[]{:S(2)}) %collective-permute-start.2) | collective-permute-done | bytes 786464 | tf_op jit(solution)/shard_map/ppermute | solution.py:19
  291.6 34.8 %collective-permute-done = bf16[8,64,768]{2,1,0:T(8,128)(2,1)} collective-permute-done((bf16[8,64,768]{2,1,0:T(8,128)(2,1)}, bf16[8,64,768]{2,1,0:T(8,128)(2,1)}, u32[]{:S(2)}, u32[]{:S(2)}) %collective-permute-start) | collective-permute-done | bytes 786464 | tf_op jit(solution)/shard_map/ppermute | solution.py:19
  338.9 39.7 %collective-permute-done.5 = bf16[8,64,768]{2,1,0:T(8,128)(2,1)} collective-permute-done((bf16[8,64,768]{2,1,0:T(8,128)(2,1)}, bf16[8,64,768]{2,1,0:T(8,128)(2,1)}, u32[]{:S(2)}, u32[]{:S(2)}) %collective-permute-start.5) | collective-permute-done | bytes 786464 | tf_op jit(solution)/shard_map/ppermute | solution.py:19
  387.3 25.0 %collective-permute-done.3 = bf16[8,64,768]{2,1,0:T(8,128)(2,1)} collective-permute-done((bf16[8,64,768]{2,1,0:T(8,128)(2,1)}, bf16[8,64,768]{2,1,0:T(8,128)(2,1)}, u32[]{:S(2)}, u32[]{:S(2)}) %collective-permute-start.3) | collective-permute-done | bytes 786464 | tf_op jit(solution)/shard_map/ppermute | solution.py:19
  491.0 66.6 %multiply_convert_fusion.3 = (bf16[512,3072]{1,0:T(8,128)(2,1)}, f32[512,3072]{1,0:T(8,128)}, bf16[512,3072]{1,0:T(8,128)(2,1)}, f32[512,3072]{1,0:T(8,128)}, bf...) fusion(f32[3072]{0:T(1024)S(1)} %copy-done.144, ...), kind=kOutput, calls=%fused_computation.52 | convolution fusion | flops 2833121280 | bytes 69228544 | tf_op jit(solution)/shard_map/dot_general | solution.py:33
  599.9 34.6 %fusion.167 = (bf16[3072]{0:T(1024)(128)(2,1)}, bf16[512,3072]{1,0:T(8,128)(2,1)}, bf16[3072]{0:T(1024)(128)(2,1)}, bf16[512,3072]{1,0:T(8,128)(2,1)}, bf16[3072...) fusion(f32[512,3072]{1,0:T(8,128)} %get-tuple-element.105, ...), kind=kOutput, calls=%fused_computation.430 | convolution fusion | flops 2516570112 | bytes 87330816 | tf_op jit(solution)/shard_map/dot_general | solution.py:43
  745.9 22.8 collective-permute-done.14
  830.0 30.2 %collective-permute-done.12 = bf16[8,64,768]{2,1,0:T(8,128)(2,1)} collective-permute-done((bf16[8,64,768]{2,1,0:T(8,128)(2,1)}, bf16[8,64,768]{2,1,0:T(8,128)(2,1)}, u32[]{:S(2)}, u32[]{:S(2)}) %collective-permute-start.12) | collective-permute-done | bytes 786464 | tf_op jit(solution)/shard_map/ppermute | solution.py:19
  955.1 30.4 %collective-permute-done.18 = bf16[8,64,768]{2,1,0:T(8,128)(2,1)} collective-permute-done((bf16[8,64,768]{2,1,0:T(8,128)(2,1)}, bf16[8,64,768]{2,1,0:T(8,128)(2,1)}, u32[]{:S(2)}, u32[]{:S(2)}) %collective-permute-start.18) | collective-permute-done | bytes 786464 | tf_op jit(solution)/shard_map/ppermute | solution.py:19
  1046.7 42.9 %collective-permute-done.16 = bf16[8,64,768]{2,1,0:T(8,128)(2,1)} collective-permute-done((bf16[8,64,768]{2,1,0:T(8,128)(2,1)}, bf16[8,64,768]{2,1,0:T(8,128)(2,1)}, u32[]{:S(2)}, u32[]{:S(2)}) %collective-permute-start.16) | collective-permute-done | bytes 786464 | tf_op jit(solution)/shard_map/ppermute | solution.py:19
  1093.8 19.3 collective-permute-done.17
  1219.7 34.5 %reduce-scatter.79.cloned.1.call-done = bf16[768,144]{0,1:T(8,128)(2,1)} async-done(((bf16[768,2304]{0,1:T(8,128)(2,1)}), bf16[768,144]{0,1:T(8,128)(2,1)}) %reduce-scatter.79.cloned.1.call-update) | async-done | bytes 221200 | tf_op jit(solution)/shard_map/reduce_scatter | solution.py:69
  1256.1 68.7 %reduce-scatter.77.cloned.1.call-done = bf16[768,144]{0,1:T(8,128)(2,1)} async-done(((bf16[768,2304]{0,1:T(8,128)(2,1)}), bf16[768,144]{0,1:T(8,128)(2,1)}) %reduce-scatter.77.cloned.1.call-update) | async-done | bytes 221200 | tf_op jit(solution)/shard_map/reduce_scatter | solution.py:69
  1326.8 76.9 %reduce-scatter.95.cloned.1.call-done = bf16[768,192]{0,1:T(8,128)(2,1)} async-done(((bf16[768,3072]{0,1:T(8,128)(2,1)}), bf16[768,192]{0,1:T(8,128)(2,1)}) %reduce-scatter.95.cloned.1.call-update) | async-done | bytes 294928 | tf_op jit(solution)/shard_map/reduce_scatter | solution.py:75
  1405.7 76.9 %reduce-scatter.91.cloned.1.call-done = bf16[768,192]{0,1:T(8,128)(2,1)} async-done(((bf16[768,3072]{0,1:T(8,128)(2,1)}), bf16[768,192]{0,1:T(8,128)(2,1)}) %reduce-scatter.91.cloned.1.call-update) | async-done | bytes 294928 | tf_op jit(solution)/shard_map/reduce_scatter | solution.py:75
  1487.1 59.0 %all-reduce.12 = (bf16[8,384]{1,0:T(8,128)(2,1)S(1)}, bf16[8,384]{1,0:T(8,128)(2,1)S(1)}, bf16[8,384]{1,0:T(8,128)(2,1)S(1)}, bf16[8,384]{1,0:T(8,128)(2,1)S(1)}) all-reduce(bf16[8,384]{1,0:T(8,128)(2,1)S(1)} %convert_element_type.639, ...), channel_id=42, replica_groups=mesh['mod'=16,'pair'=2] {'mod'}, use_global_device_ids=true, to_apply=%region_117.118.clone | all-reduce | flops 12288 | bytes 49152
  1568.8 71.4 %reduce-scatter.89.cloned.1.call-done = bf16[768,192]{0,1:T(8,128)(2,1)} async-done(((bf16[768,3072]{0,1:T(8,128)(2,1)}), bf16[768,192]{0,1:T(8,128)(2,1)}) %reduce-scatter.89.cloned.1.call-update) | async-done | bytes 294928 | tf_op jit(solution)/shard_map/reduce_scatter | solution.py:75
  1648.9 69.6 %reduce-scatter.109.cloned.1.call-done = bf16[3072,48]{0,1:T(8,128)(2,1)} async-done(((bf16[3072,768]{0,1:T(8,128)(2,1)}), bf16[3072,48]{0,1:T(8,128)(2,1)}) %reduce-scatter.109.cloned.1.call-update) | async-done | bytes 294928 | tf_op jit(solution)/shard_map/reduce_scatter | solution.py:78
  1724.7 72.7 %reduce-scatter.97.cloned.1.call-done = bf16[3072,48]{0,1:T(8,128)(2,1)} async-done(((bf16[3072,768]{0,1:T(8,128)(2,1)}), bf16[3072,48]{0,1:T(8,128)(2,1)}) %reduce-scatter.97.cloned.1.call-update) | async-done | bytes 294928 | tf_op jit(solution)/shard_map/reduce_scatter | solution.py:78
  1803.5 72.4 %reduce-scatter.101.cloned.1.call-done = bf16[3072,48]{0,1:T(8,128)(2,1)} async-done(((bf16[3072,768]{0,1:T(8,128)(2,1)}), bf16[3072,48]{0,1:T(8,128)(2,1)}) %reduce-scatter.101.cloned.1.call-update) | async-done | bytes 294928 | tf_op jit(solution)/shard_map/reduce_scatter | solution.py:78
  1880.5 51.8 %reduce-scatter.139.cloned.1.call-done = bf16[48,8]{1,0:T(8,128)(2,1)} async-done(((bf16[768,8]{1,0:T(8,128)(2,1)}), bf16[48,8]{1,0:T(8,128)(2,1)}) %reduce-scatter.139.cloned.1.call-update) | async-done | bytes 784
  1933.1 55.8 %reduce-scatter.137.cloned.1.call-done = bf16[48,8]{1,0:T(8,128)(2,1)} async-done(((bf16[768,8]{1,0:T(8,128)(2,1)}), bf16[48,8]{1,0:T(8,128)(2,1)}) %reduce-scatter.137.cloned.1.call-update) | async-done | bytes 784
  1989.7 55.8 %reduce-scatter.143.cloned.1.call-done = bf16[48,8]{1,0:T(8,128)(2,1)} async-done(((bf16[768,8]{1,0:T(8,128)(2,1)}), bf16[48,8]{1,0:T(8,128)(2,1)}) %reduce-scatter.143.cloned.1.call-update) | async-done | bytes 784
  2046.2 55.8 %reduce-scatter.141.cloned.1.call-done = bf16[48,8]{1,0:T(8,128)(2,1)} async-done(((bf16[768,8]{1,0:T(8,128)(2,1)}), bf16[48,8]{1,0:T(8,128)(2,1)}) %reduce-scatter.141.cloned.1.call-update) | async-done | bytes 784
  2156.5 79.0 %reduce-scatter.105.cloned.1.call-done = bf16[3072,48]{0,1:T(8,128)(2,1)} async-done(((bf16[3072,768]{0,1:T(8,128)(2,1)}), bf16[3072,48]{0,1:T(8,128)(2,1)}) %reduce-scatter.105.cloned.1.call-update) | async-done | bytes 294928 | tf_op jit(solution)/shard_map/reduce_scatter | solution.py:78
  2266.3 14.4 reduce-scatter.119.cloned.1.call-done
  2281.7 14.5 reduce-scatter.117.cloned.1.call-done
  2312.5 14.4 reduce-scatter.131.cloned.1.call-done
  2328.0 14.3 reduce-scatter.133.cloned.1.call-done
  2400.3 14.3 reduce-scatter.107.cloned.1.call-done
  (894 shorter events, 968.3 us)
Async XLA Ops:
  20.8 457.0 %all-gather.13.cloned.1.call-start = ((), (), s32[]{:S(2)}) async-start(), calls=%async_computation.38 | async-start | bytes 5013504 | tf_op jit(solution)/shard_map/all_gather | solution.py:60
  28.0 529.7 %all-gather.15.cloned.1.call-start = ((), (), s32[]{:S(2)}) async-start(), calls=%async_computation.39 | async-start | bytes 5013504 | tf_op jit(solution)/shard_map/all_gather | solution.py:61
  41.1 1161.2 %reduce-scatter.87.cloned.1.call-start = ((), (), s32[]{:S(2)}) async-start(), calls=%async_computation.47 | async-start | bytes 1253376 | tf_op jit(solution)/shard_map/reduce_scatter | solution.py:72
  663.4 540.7 %reduce-scatter.85.cloned.1.call-start = ((), (), s32[]{:S(2)}) async-start(), calls=%async_computation.46 | async-start | bytes 1253376 | tf_op jit(solution)/shard_map/reduce_scatter | solution.py:72
  673.3 532.6 %reduce-scatter.83.cloned.1.call-start = ((), (), s32[]{:S(2)}) async-start(), calls=%async_computation.45 | async-start | bytes 1253376 | tf_op jit(solution)/shard_map/reduce_scatter | solution.py:72
  694.5 513.1 %reduce-scatter.81.cloned.1.call-start = ((), (), s32[]{:S(2)}) async-start(), calls=%async_computation.44 | async-start | bytes 1253376 | tf_op jit(solution)/shard_map/reduce_scatter | solution.py:72
  717.8 498.0 %reduce-scatter.75.cloned.1.call-start = ((), (), s32[]{:S(2)}) async-start(), calls=%async_computation.41 | async-start | bytes 3760128 | tf_op jit(solution)/shard_map/reduce_scatter | solution.py:69
  1147.3 492.9 %reduce-scatter.89.cloned.1.call-start = ((), (), s32[]{:S(2)}) async-start(), calls=%async_computation.48 | async-start | bytes 5013504 | tf_op jit(solution)/shard_map/reduce_scatter | solution.py:75
  1155.5 563.0 %reduce-scatter.109.cloned.1.call-start = ((), (), s32[]{:S(2)}) async-start(), calls=%async_computation.58 | async-start | bytes 5013504 | tf_op jit(solution)/shard_map/reduce_scatter | solution.py:78
  1163.0 634.4 %reduce-scatter.97.cloned.1.call-start = ((), (), s32[]{:S(2)}) async-start(), calls=%async_computation.52 | async-start | bytes 5013504 | tf_op jit(solution)/shard_map/reduce_scatter | solution.py:78
  1170.5 705.4 %reduce-scatter.101.cloned.1.call-start = ((), (), s32[]{:S(2)}) async-start(), calls=%async_computation.54 | async-start | bytes 5013504 | tf_op jit(solution)/shard_map/reduce_scatter | solution.py:78
  1178.0 754.3 %reduce-scatter.139.cloned.1.call-start = ((), (), s32[]{:S(2)}) async-start(), calls=%async_computation.73 | async-start | bytes 208896
  1192.3 796.6 %reduce-scatter.137.cloned.1.call-start = ((), (), s32[]{:S(2)}) async-start(), calls=%async_computation.72 | async-start | bytes 208896
  1195.6 849.9 %reduce-scatter.143.cloned.1.call-start = ((), (), s32[]{:S(2)}) async-start(), calls=%async_computation.75 | async-start | bytes 208896
  1198.9 903.1 %reduce-scatter.141.cloned.1.call-start = ((), (), s32[]{:S(2)}) async-start(), calls=%async_computation.74 | async-start | bytes 208896
  1202.2 912.6 %reduce-scatter.127.cloned.1.call-start = ((), (), s32[]{:S(2)}) async-start(), calls=%async_computation.67 | async-start | bytes 294912
  1204.0 924.7 %reduce-scatter.125.cloned.1.call-start = ((), (), s32[]{:S(2)}) async-start(), calls=%async_computation.66 | async-start | bytes 294912
  1205.8 936.6 %reduce-scatter.123.cloned.1.call-start = ((), (), s32[]{:S(2)}) async-start(), calls=%async_computation.65 | async-start | bytes 294912
  1207.6 947.9 %reduce-scatter.121.cloned.1.call-start = ((), (), s32[]{:S(2)}) async-start(), calls=%async_computation.64 | async-start | bytes 294912
  1209.4 1026.0 %reduce-scatter.105.cloned.1.call-start = ((), (), s32[]{:S(2)}) async-start(), calls=%async_computation.56 | async-start | bytes 5013504 | tf_op jit(solution)/shard_map/reduce_scatter | solution.py:78
  1215.8 1034.2 %reduce-scatter.115.cloned.1.call-start = ((), (), s32[]{:S(2)}) async-start(), calls=%async_computation.61 | async-start | bytes 589824
  1217.7 1047.6 %reduce-scatter.113.cloned.1.call-start = ((), (), s32[]{:S(2)}) async-start(), calls=%async_computation.60 | async-start | bytes 589824
  1219.7 1061.0 %reduce-scatter.119.cloned.1.call-start = ((), (), s32[]{:S(2)}) async-start(), calls=%async_computation.63 | async-start | bytes 589824
  1256.1 1040.1 %reduce-scatter.117.cloned.1.call-start = ((), (), s32[]{:S(2)}) async-start(), calls=%async_computation.62 | async-start | bytes 589824
  1326.7 984.7 %reduce-scatter.135.cloned.1.call-start = ((), (), s32[]{:S(2)}) async-start(), calls=%async_computation.71 | async-start | bytes 589824
  1405.7 921.3 %reduce-scatter.131.cloned.1.call-start = ((), (), s32[]{:S(2)}) async-start(), calls=%async_computation.69 | async-start | bytes 589824
  1484.5 857.8 %reduce-scatter.133.cloned.1.call-start = ((), (), s32[]{:S(2)}) async-start(), calls=%async_computation.70 | async-start | bytes 589824
  1563.3 794.4 %reduce-scatter.129.cloned.1.call-start = ((), (), s32[]{:S(2)}) async-start(), calls=%async_computation.68 | async-start | bytes 589824
  1642.2 729.6 %reduce-scatter.111.cloned.1.call-start = ((), (), s32[]{:S(2)}) async-start(), calls=%async_computation.59 | async-start | bytes 442368 | tf_op jit(solution)/shard_map/reduce_scatter | solution.py:98
  1718.6 667.5 %reduce-scatter.99.cloned.1.call-start = ((), (), s32[]{:S(2)}) async-start(), calls=%async_computation.53 | async-start | bytes 442368 | tf_op jit(solution)/shard_map/reduce_scatter | solution.py:98
  1797.4 602.8 %reduce-scatter.103.cloned.1.call-start = ((), (), s32[]{:S(2)}) async-start(), calls=%async_computation.55 | async-start | bytes 442368 | tf_op jit(solution)/shard_map/reduce_scatter | solution.py:98
  1875.9 538.7 %reduce-scatter.107.cloned.1.call-start = ((), (), s32[]{:S(2)}) async-start(), calls=%async_computation.57 | async-start | bytes 442368 | tf_op jit(solution)/shard_map/reduce_scatter | solution.py:98
  (234 other events, 9962.0 us)
Sparse Core Ops, SparseCore 0:
  15.9 47.6 all-gather.8
  65.8 37.3 all-gather.10
  105.5 135.1 all-gather.12
  242.8 129.5 all-gather.14
  663.5 90.0 reduce-scatter.86
  757.1 88.5 reduce-scatter.84
  849.3 59.2 reduce-scatter.82
  912.2 109.3 reduce-scatter.80
  1025.4 76.1 reduce-scatter.74
  1105.3 77.9 reduce-scatter.72
  1187.2 66.9 reduce-scatter.78
  1257.9 66.9 reduce-scatter.76
  1329.3 74.4 reduce-scatter.94
  1407.9 74.5 reduce-scatter.90
  1486.3 75.0 reduce-scatter.92
  1565.6 74.5 reduce-scatter.88
  1643.9 74.5 reduce-scatter.108
  1722.8 74.5 reduce-scatter.96
  1801.2 74.5 reduce-scatter.100
  1879.6 52.6 reduce-scatter.138
  1936.2 52.6 reduce-scatter.136
  1992.8 52.6 reduce-scatter.142
  2049.4 52.6 reduce-scatter.140
  2159.9 75.5 reduce-scatter.104
  2237.7 12.1 reduce-scatter.114
  2252.1 13.1 reduce-scatter.112
  2267.5 13.1 reduce-scatter.118
  2283.0 13.1 reduce-scatter.116
  2298.3 13.0 reduce-scatter.134
  2313.7 13.1 reduce-scatter.130
  2329.2 13.0 reduce-scatter.132
  2344.5 13.1 reduce-scatter.128
  (8 shorter events, 90.5 us)
where the time goes:
time: 2430 us; the launch traced here: 2420 us
  waiting for transfers between devices  1420 us (58%)
  matrix products  390 us (16%)
  local copies, waits for them, and re-layouts  327 us (13%)
  blocking collectives  142 us (6%)
  other arithmetic  95.7 us (4%)
  starting transfers between devices  26.8 us (1%)
    unnamed x56, waiting for transfers between devices  374 us
    ppermute x20, waiting for transfers between devices, shifted(): lax.ppermute(shard, axis, [(i, (i + by) % count) for i in range(count)])  359 us
    reduce_scatter x4, waiting for transfers between devices, reduce_grads(): lax.psum_scatter(terms[3].astype(jnp.bfloat16), 'mod', scatter_dimension=...  294 us
    reduce_scatter x4, waiting for transfers between devices, reduce_grads(): lax.psum_scatter(terms[2].astype(jnp.bfloat16), 'mod', scatter_dimension=...  237 us
    unnamed x464, local copies, waits for them, and re-layouts  121 us
    dot_general x16, matrix products, plain_dot(): return jnp.dot(left, right, preferred_element_type=jnp.float32)  121 us
    dot_general x16, matrix products, right_dot(): lax.dot_general(left, right, (((1,), (1,)), ((), ())), preferred_element_...  106 us
    reduce_scatter x4, waiting for transfers between devices, reduce_grads(): lax.psum_scatter(terms[0].astype(jnp.bfloat16), 'mod', scatter_dimension=...  103 us
  transfers between devices with their start and end apart: 60, of which 42 were waited for; matrix products, arithmetic and copies ran while one was open for 28% of the time, Pallas kernels for 0%

commit v1 on v0

v1 whole, which is shorter than its diff:
```python
import jax
import jax.numpy as jnp
from jax import lax
from jax.experimental import pallas as pl
from jax.experimental.pallas import tpu as pltpu
from jax.sharding import PartitionSpec as P

HEADS = 12
HEAD_DIM = 64
SLOTS = 64
CHUNKS = 4
EPS = 1e-05
NEG = -1000000000.0
FB = 512
LIMIT = 60 * 2**20
F32 = jnp.float32
BF = jnp.bfloat16
ANY = pl.BlockSpec(memory_space=pl.ANY)


def nt(a,b): return lax.dot_general(a,b,(((1,),(1,)),((),())),preferred_element_type=F32)
def nn(a,b): return lax.dot_general(a,b,(((1,),(0,)),((),())),preferred_element_type=F32)
def tn(a,b): return lax.dot_general(a,b,(((0,),(0,)),((),())),preferred_element_type=F32)
def colsum(v): return jnp.sum(v,0,keepdims=True)
VM=pl.BlockSpec(memory_space=pltpu.VMEM)
SM=pl.BlockSpec(memory_space=pltpu.SMEM)

def pulls(pieces, core, first_row, rows, into, sem):
    copies = []
    for which, ref in enumerate(pieces):
        place = core if which == 0 else 1 - core
        for group in range(ref.shape[0]):
            start = pl.multiple_of((2 * group + place) * rows, 8)
            copies.append(
                pltpu.make_async_copy(
                    ref.at[group, pl.ds(first_row, rows), :], into.at[pl.ds(start, rows), :], sem
                )
            )
    return copies


def start_all(copies):
    for copy in copies:
        copy.start()


def wait_whole(into, sem):
    pltpu.make_async_copy(into, into, sem).wait()


def attend_kernel(core_ref, live_ref, own_ref, far_ref, wa_ref, wb_ref, vec_ref, qkv_ref, prob_ref, mixed_ref, sum1_ref, wqkv_ref, wout_ref, sems):
    core = core_ref[0]
    per = 2 * wa_ref.shape[0]
    rq, ro = wqkv_ref.shape[0] // per, wout_ref.shape[0] // per
    start_all(pulls((wa_ref, wb_ref), core, 0, rq, wqkv_ref, sems.at[0]))
    start_all(pulls((wa_ref, wb_ref), core, rq, ro, wout_ref, sems.at[1]))
    wait_whole(wqkv_ref, sems.at[0])
    h,width=own_ref.shape
    seqs=prob_ref.shape[0]; slots=h//seqs
    x=jnp.concatenate([own_ref[...],far_ref[...]],0)
    for part in range(3):
        cols=slice(part*width,(part+1)*width)
        acc=nt(x,wqkv_ref[cols,:])
        if part==0: acc=(acc+vec_ref[0:1,:])
        if part==2: acc=acc+vec_ref[1:2,:]
        qkv_ref[:,cols]=acc.astype(BF)
    lane=lax.broadcasted_iota(jnp.int32,(2*slots,2*HEAD_DIM),1)
    low_half=lane<HEAD_DIM
    key=lax.broadcasted_iota(jnp.int32,(2*slots,4*slots),1)%(2*slots)
    def seq(s,_):
        a=pl.multiple_of(s*slots,slots); b=pl.multiple_of(h+s*slots,slots)
        live_own=live_ref[0,s]; live_far=live_ref[1,s]
        valid=key<jnp.where(key<slots,live_own,live_far+slots)
        for p in range(HEADS//2):
            def take(part):
                c=slice(part*width+p*128,part*width+(p+1)*128)
                return jnp.concatenate([qkv_ref[pl.ds(a,slots),c],qkv_ref[pl.ds(b,slots),c]],0)
            q,k,v=take(0),take(1),take(2)
            zero=jnp.zeros_like(k)
            k2=jnp.concatenate([jnp.where(low_half,k,zero),jnp.where(low_half,zero,k)],0)
            v2=jnp.concatenate([jnp.where(low_half,v,zero),jnp.where(low_half,zero,v)],0)
            sc=jnp.where(valid,nt(q,k2)*(HEAD_DIM**-0.5),NEG)
            halves=[]
            for half in (sc[:,:2*slots],sc[:,2*slots:]):
                e=jnp.exp(half-jnp.max(half,-1,keepdims=True))
                halves.append((e/jnp.sum(e,-1,keepdims=True)).astype(BF))
            prob=jnp.concatenate(halves,1)
            prob_ref[s,p]=prob
            o=nn(prob,v2).astype(BF)
            c=slice(p*128,(p+1)*128)
            mixed_ref[pl.ds(a,slots),c]=o[:slots]
            mixed_ref[pl.ds(b,slots),c]=o[slots:]
        return 0
    lax.fori_loop(0,seqs,seq,0)
    wait_whole(wout_ref, sems.at[1])
    branch=nt(mixed_ref[...],wout_ref[...])
    sum1_ref[...]=x.astype(F32)+branch+vec_ref[2:3,:]

def attend(core,live,own,far,wa,wb,vec):
    h,width=own.shape; seqs=live.shape[1]
    return pl.pallas_call(attend_kernel,
        out_shape=(jax.ShapeDtypeStruct((2*h,3*width),BF),jax.ShapeDtypeStruct((seqs,HEADS//2,128,256),BF),
                   jax.ShapeDtypeStruct((2*h,width),BF),jax.ShapeDtypeStruct((2*h,width),F32)),
        in_specs=[SM,SM,VM,VM,ANY,ANY,VM],out_specs=(VM,)*4,
        scratch_shapes=[pltpu.VMEM((3*width,width),BF),pltpu.VMEM((width,width),BF),pltpu.SemaphoreType.DMA((2,))],
        compiler_params=pltpu.CompilerParams(vmem_limit_bytes=LIMIT),name="attend")(core,live,own,far,wa,wb,vec)

def normed(v):
    c=v-jnp.mean(v,-1,keepdims=True)
    r=lax.rsqrt(jnp.mean(c*c,-1,keepdims=True)+EPS)
    return c*r,r
def norm_back(g,n,r):
    return r*(g-jnp.mean(g,-1,keepdims=True)-n*jnp.mean(g*n,-1,keepdims=True))

def feed_kernel(core_ref,sum1_ref,gown_ref,gfar_ref,ua_ref,ub_ref,da_ref,db_ref,vec_ref,bup_ref,
                yown_ref,yfar_ref,act_ref,dinner_ref,first_ref,dout_ref,dbranch_ref,vsum_ref,bsum_ref,
                wup_ref,wdown_ref,sems,slope_ref,acc_ref,n1_ref):
    h,width=gown_ref.shape; ff=wup_ref.shape[0]
    core = core_ref[0]
    per = 2 * ua_ref.shape[0]
    start_all(pulls((ua_ref, ub_ref), core, 0, ff // per, wup_ref, sems.at[0]))
    start_all(pulls((da_ref, db_ref), core, 0, width // per, wdown_ref, sems.at[1]))
    n1,r1=normed(sum1_ref[...])
    n1_ref[...]=n1
    first=n1*vec_ref[4:5,:]+vec_ref[5:6,:]
    first_ref[...]=first.astype(BF)
    acc_ref[...]=first+vec_ref[3:4,:]
    def up(j,_):
        o=pl.multiple_of(j*FB,FB)
        inner=nt(first_ref[...],wup_ref[pl.ds(o,FB),:])+bup_ref[0:1,pl.ds(o,FB)]
        phi=0.5+0.5*lax.erf(inner*(2**-0.5))
        act=(inner*phi).astype(BF)
        act_ref[:,pl.ds(o,FB)]=act
        slope_ref[:,pl.ds(o,FB)]=(phi+inner*(jnp.exp(-0.5*inner*inner)*0.3989422804014327)).astype(slope_ref.dtype)
        acc_ref[...]+=nt(act,wdown_ref[:,pl.ds(o,FB)])
        return 0
    wait_whole(wup_ref, sems.at[0])
    wait_whole(wdown_ref, sems.at[1])
    lax.fori_loop(0,ff//FB,up,0)
    n2,r2=normed(acc_ref[...])
    y=(n2*vec_ref[6:7,:]+vec_ref[7:8,:]).astype(BF)
    yown_ref[...]=y[:h]; yfar_ref[...]=y[h:]
    g=jnp.concatenate([gown_ref[...],gfar_ref[...]],0).astype(F32)
    vsum_ref[4:5,:]=colsum(g*n2); vsum_ref[5:6,:]=colsum(g)
    dz2=norm_back(g*vec_ref[6:7,:],n2,r2)
    dout=dz2.astype(BF)
    dout_ref[...]=dout
    vsum_ref[1:2,:]=colsum(dz2)
    acc_ref[...]=dz2
    def down(j,_):
        o=pl.multiple_of(j*FB,FB)
        dinner=nn(dout_ref[...],wdown_ref[:,pl.ds(o,FB)])*slope_ref[:,pl.ds(o,FB)].astype(F32)
        bsum_ref[0:1,pl.ds(o,FB)]=colsum(dinner)
        dlow=dinner.astype(BF)
        dinner_ref[:,pl.ds(o,FB)]=dlow
        acc_ref[...]+=nn(dlow,wup_ref[pl.ds(o,FB),:])
        return 0
    lax.fori_loop(0,ff//FB,down,0)
    d=acc_ref[...]; n1=n1_ref[...]
    _,r1=normed(sum1_ref[...])
    vsum_ref[2:3,:]=colsum(d*n1); vsum_ref[3:4,:]=colsum(d)
    dz1=norm_back(d*vec_ref[4:5,:],n1,r1)
    dbranch_ref[...]=dz1.astype(BF)
    vsum_ref[0:1,:]=colsum(dz1)

def feed(core,sum1,gown,gfar,ua,ub,da,db,vec,bup):
    h,width=gown.shape; ff=bup.shape[1]; r=2*h
    S=jax.ShapeDtypeStruct
    return pl.pallas_call(feed_kernel,
        out_shape=(S((h,width),BF),S((h,width),BF),S((r,ff),BF),S((r,ff),BF),S((r,width),BF),S((r,width),BF),S((r,width),BF),S((8,width),F32),S((1,ff),F32)),
        in_specs=[SM,VM,VM,VM,ANY,ANY,ANY,ANY,VM,VM],out_specs=(VM,)*9,
        scratch_shapes=[pltpu.VMEM((ff,width),BF),pltpu.VMEM((width,ff),BF),pltpu.SemaphoreType.DMA((2,)),pltpu.VMEM((r,ff),BF),pltpu.VMEM((r,width),F32),pltpu.VMEM((r,width),F32)],
        compiler_params=pltpu.CompilerParams(vmem_limit_bytes=LIMIT),name="feed")(core,sum1,gown,gfar,ua,ub,da,db,vec,bup)

def back_kernel(core_ref,dbranch_ref,qkv_ref,prob_ref,wa_ref,wb_ref,dqkv_ref,dxown_ref,dxfar_ref,vsum_ref,wqkv_ref,wout_ref,sems,dmix_ref):
    r,width=dbranch_ref.shape; h=r//2
    core = core_ref[0]
    per = 2 * wa_ref.shape[0]
    rq, ro = wqkv_ref.shape[0] // per, wout_ref.shape[0] // per
    start_all(pulls((wa_ref, wb_ref), core, rq, ro, wout_ref, sems.at[1]))
    start_all(pulls((wa_ref, wb_ref), core, 0, rq, wqkv_ref, sems.at[0]))
    wait_whole(wout_ref, sems.at[1])
    seqs=prob_ref.shape[0]; slots=h//seqs
    dmix_ref[...]=nn(dbranch_ref[...],wout_ref[...]).astype(BF)
    lane=lax.broadcasted_iota(jnp.int32,(2*slots,2*HEAD_DIM),1)
    low_half=lane<HEAD_DIM
    def seq(s,_):
        a=pl.multiple_of(s*slots,slots); b=pl.multiple_of(h+s*slots,slots)
        for p in range(HEADS//2):
            def rows(ref,part):
                c=slice(part*width+p*128,part*width+(p+1)*128)
                return jnp.concatenate([ref[pl.ds(a,slots),c],ref[pl.ds(b,slots),c]],0)
            q,k,v=rows(qkv_ref,0),rows(qkv_ref,1),rows(qkv_ref,2)
            do=rows(dmix_ref,0)
            zero=jnp.zeros_like(k)
            k2=jnp.concatenate([jnp.where(low_half,k,zero),jnp.where(low_half,zero,k)],0)
            v2=jnp.concatenate([jnp.where(low_half,v,zero),jnp.where(low_half,zero,v)],0)
            prob=prob_ref[s,p]
            dp=nt(do,v2)
            pf=prob.astype(F32)
            halves=[]
            for u in range(2):
                c=slice(u*2*slots,(u+1)*2*slots)
                w=pf[:,c]*dp[:,c]
                halves.append((w-pf[:,c]*jnp.sum(w,-1,keepdims=True)).astype(BF))
            ds=jnp.concatenate(halves,1)
            sc=HEAD_DIM**-0.5
            dq=nn(ds,k2)*sc
            dk=tn(ds,q)*sc
            dv=tn(prob,do)
            dk=jnp.where(low_half,dk[:2*slots],dk[2*slots:])
            dv=jnp.where(low_half,dv[:2*slots],dv[2*slots:])
            for part,val in enumerate((dq,dk,dv)):
                c=slice(part*width+p*128,part*width+(p+1)*128)
                dqkv_ref[pl.ds(a,slots),c]=val[:slots].astype(BF)
                dqkv_ref[pl.ds(b,slots),c]=val[slots:].astype(BF)
        return 0
    lax.fori_loop(0,seqs,seq,0)
    wait_whole(wqkv_ref, sems.at[0])
    dx=dbranch_ref[...].astype(F32)+nn(dqkv_ref[...],wqkv_ref[...])
    dxown_ref[...]=dx[:h]; dxfar_ref[...]=dx[h:].astype(BF)
    vsum_ref[...]=jnp.zeros_like(vsum_ref)
    vsum_ref[0:1,:]=colsum(dqkv_ref[:,:width].astype(F32))
    vsum_ref[1:2,:]=colsum(dqkv_ref[:,2*width:].astype(F32))

def back(core,dbranch,qkv,prob,wa,wb):
    r,width=dbranch.shape; h=r//2
    S=jax.ShapeDtypeStruct
    return pl.pallas_call(back_kernel,
        out_shape=(S((r,3*width),BF),S((h,width),F32),S((h,width),BF),S((8,width),F32)),
        in_specs=[SM,VM,VM,VM,ANY,ANY],out_specs=(VM,)*4,
        scratch_shapes=[pltpu.VMEM((3*width,width),BF),pltpu.VMEM((width,width),BF),pltpu.SemaphoreType.DMA((2,)),pltpu.VMEM((r,width),BF)],
        compiler_params=pltpu.CompilerParams(vmem_limit_bytes=LIMIT),name="back")(core,dbranch,qkv,prob,wa,wb)

def bits_of(axis):
    return (lax.axis_size(axis) - 1).bit_length()


def swapped(values, axis, mask):
    count = lax.axis_size(axis)
    return lax.ppermute(values, axis, [(i, i ^ mask) for i in range(count)])


def bit_at(axis, bit):
    return (lax.axis_index(axis) >> bit) & 1


def stages(pair_first):
    mod_bits = bits_of("mod")
    top = [("mod", bit) for bit in range(mod_bits - 1, 1, -1)]
    low = [("mod", 1)]
    pairs = [("pair", bit) for bit in range(bits_of("pair"))]
    return top + (pairs + low if pair_first else low + pairs)


def gather(slab, pair_first):
    held = slab
    depth = 0
    for axis, bit in stages(pair_first):
        other = swapped(held, axis, 1 << bit)
        upper = bit_at(axis, bit) == 1
        first, second = jnp.where(upper, other, held), jnp.where(upper, held, other)
        if axis == "mod":
            held = jnp.stack([first, second], depth)
            depth += 1
        else:
            held = jnp.concatenate([first, second], -1)
    held = held.reshape((-1,) + held.shape[depth:])
    return held, swapped(held, "mod", 1)


def scatter_sum(keep, send, pair_first):
    steps = stages(pair_first)
    depth = sum(axis == "mod" for axis, bit in steps)
    lead = (2,) * depth
    held = keep.reshape(lead + keep.shape[1:])
    came = swapped(send, "mod", 1).reshape(held.shape)
    for axis, bit in reversed(steps):
        mine = bit_at(axis, bit)
        if axis == "mod":
            depth -= 1
            dim, size = depth, 1
        else:
            dim = held.ndim - 1
            size = held.shape[-1] // 2

        def part(values, which):
            return lax.dynamic_slice_in_dim(values, which * size, size, dim)

        away = (part(held, 1 - mine).astype(F32) + part(came, 1 - mine).astype(F32)).astype(BF)
        held = part(held, mine).astype(F32) + part(came, mine).astype(F32)
        came = swapped(away, axis, 1 << bit)
    return (held + came.astype(F32)).reshape(held.shape[-2:])


def split_cores(full, core, groups):
    view = full.reshape(groups, 2, -1, full.shape[-1])
    keep = lax.dynamic_index_in_dim(view, core, 1, keepdims=False)
    send = lax.dynamic_index_in_dim(view, 1 - core, 1, keepdims=False)
    return keep, send


def per_device(rows_input, grad_out, w_qkv, w_out, w_up, w_down, vectors, b_up, live_rows):
    mod_size = lax.axis_size("mod")
    pair_size = lax.axis_size("pair")
    groups = mod_size // 2
    half = mod_size // 2
    rows, width = rows_input.shape
    moved = rows // 2
    step = moved // CHUNKS
    seqs = step // SLOTS
    place = lax.axis_index("mod")
    upper = place >= half
    core = place & 1
    core_ref = core.reshape(1)
    own_start = jnp.where(upper, moved, 0)
    away_start = jnp.where(upper, 0, moved)

    def over(values):
        return swapped(values, "mod", half)

    own_rows, far_rows = [], []
    live_own = lax.dynamic_slice_in_dim(live_rows, own_start // SLOTS, moved // SLOTS)
    live_far = over(lax.dynamic_slice_in_dim(live_rows, away_start // SLOTS, moved // SLOTS))
    live = jnp.stack([live_own, live_far])
    for c in range(CHUNKS):
        own_rows.append(lax.dynamic_slice_in_dim(rows_input, own_start + c * step, step))
        far_rows.append(over(lax.dynamic_slice_in_dim(rows_input, away_start + c * step, step)))

    small = jnp.concatenate([vectors.reshape(-1), b_up.reshape(-1)])
    line = w_qkv.shape[0]
    small_rows = -(-small.shape[0] // line)
    small = jnp.pad(small, (0, 16 * line - small.shape[0])).reshape(16, line)
    proj_slab = jnp.concatenate([w_qkv.T, w_out.T, small], 0)
    wa, wb = gather(proj_slab, True)
    tiny_at = w_qkv.shape[1] + w_out.shape[1]
    tiny_a = wa[:, tiny_at : tiny_at + small_rows].reshape(groups, small_rows, pair_size, line)
    tiny_b = wb[:, tiny_at : tiny_at + small_rows].reshape(groups, small_rows, pair_size, line)
    flip = core == 1
    tiny = jnp.stack([jnp.where(flip, tiny_b, tiny_a), jnp.where(flip, tiny_a, tiny_b)], 1)
    tiny = tiny.reshape(mod_size, small_rows, pair_size, line).transpose(2, 0, 1, 3).reshape(pair_size, mod_size, -1)
    count = vectors.size
    vec = tiny[:, :, :count].reshape((pair_size, mod_size) + vectors.shape).transpose(0, 2, 1, 3)
    vec = vec.reshape(8, width).astype(F32)
    bup = tiny[:, :, count : count + b_up.size].reshape((pair_size, mod_size) + b_up.shape).transpose(0, 2, 1, 3)
    bup = bup.reshape(1, -1).astype(F32)

    ua, ub = gather(w_up.T, False)
    da, db = gather(w_down.T, True)

    own_grads, far_grads = [], []
    for c in range(CHUNKS):
        own_grads.append(lax.dynamic_slice_in_dim(grad_out, own_start + c * step, step))
        far_grads.append(over(lax.dynamic_slice_in_dim(grad_out, away_start + c * step, step)))

    result = jnp.zeros((rows, width), BF)
    input_grad = jnp.zeros((rows, width), F32)
    kept = []
    for c in range(CHUNKS):
        kept.append(attend(core_ref, live[:, c * seqs : (c + 1) * seqs], own_rows[c], far_rows[c], wa, wb, vec))
    fed, backed = [], []
    for c in range(CHUNKS):
        qkv, prob, mixed, sum1 = kept[c]
        out = feed(core_ref, sum1, own_grads[c], far_grads[c], ua, ub, da, db, vec, bup)
        fed.append(out)
        result = lax.dynamic_update_slice_in_dim(result, out[0], own_start + c * step, 0)
        result = lax.dynamic_update_slice_in_dim(result, over(out[1]), away_start + c * step, 0)
        dqkv, dx_own, dx_far, vsum = back(core_ref, out[6], qkv, prob, wa, wb)
        backed.append((dqkv, vsum))
        input_grad = lax.dynamic_update_slice_in_dim(input_grad, dx_own, own_start + c * step, 0)
        input_grad = lax.dynamic_update_slice_in_dim(input_grad, over(dx_far).astype(F32), away_start + c * step, 0)

    def joined(parts):
        return jnp.concatenate(parts, 0)

    def weight(left, right, pair_first):
        full = tn(joined(left), joined(right)).astype(BF)
        keep, send = split_cores(full, core, groups)
        return scatter_sum(keep, send, pair_first).T

    both = [jnp.concatenate([a, b], 0) for a, b in zip(own_rows, far_rows)]
    g_up = weight([f[3] for f in fed], [f[4] for f in fed], False)
    g_down = weight([f[5] for f in fed], [f[2] for f in fed], True)
    g_out = weight([f[6] for f in fed], [k[2] for k in kept], False)
    g_qkv = weight([b[0] for b in backed], both, True)

    vec_sum = sum(f[7] for f in fed)
    qv_sum = sum(b[1] for b in backed)
    bup_sum = sum(f[8] for f in fed)
    vec_grad = jnp.concatenate([qv_sum[:2], vec_sum[:6]], 0).reshape(pair_size, -1, mod_size, vectors.shape[1])
    bup_grad = bup_sum.reshape(pair_size, -1, mod_size, b_up.shape[1])
    tiny_grad = jnp.concatenate(
        [vec_grad.transpose(2, 0, 1, 3).reshape(mod_size, pair_size, -1), bup_grad.transpose(2, 0, 1, 3).reshape(mod_size, pair_size, -1)], -1
    )
    tiny_sum = lax.psum(tiny_grad.astype(BF), ("mod", "pair"))
    tiny_mine = tiny_sum[place, lax.axis_index("pair")].astype(F32)
    g_vec = tiny_mine[: vectors.size].reshape(vectors.shape)
    g_bup = tiny_mine[vectors.size :].reshape(b_up.shape)
    return (result, input_grad, g_qkv, g_out, g_up, g_down, g_vec, g_bup)


def solution(mesh):
    sharded = P("pair", "mod")
    spread = P(("mod", "pair"), None)
    weights = (sharded,) * 6
    return jax.shard_map(
        per_device,
        mesh=mesh,
        in_specs=(spread, spread) + weights + (P(("mod", "pair")),),
        out_specs=(spread, spread) + weights,
        check_vma=False,
    )
```

time: 2430 us -> 733 us (0.30)
  waiting for transfers between devices: 1420 us -> 315 us
  matrix products: 390 us -> 43.3 us
  local copies, waits for them, and re-layouts: 327 us -> 35.4 us
  Pallas kernels: 0 us -> 209 us
  blocking collectives: 142 us -> 40.4 us
  other arithmetic: 95.7 us -> 24.2 us
  starting transfers between devices: 26.8 us -> 56.3 us
    reduce_scatter x20 -> x0, waiting for transfers between devices: 689 us -> none  [the longest x4 294 us: reduce_grads(): lax.psum_scatter(terms[3].astype(jnp.bfloat16), 'mod', scatter_dimension=...]
    unnamed x56 -> x0, waiting for transfers between devices: 374 us -> none
    dot_general x72 -> x4, matrix products: 390 us -> 43.3 us  [tn(): lax.dot_general(a, b, (((0,), (0,)), ((), ())), preferred_element_type=F32)]
    pallas_call x0 -> x12, Pallas kernels: none -> 209 us  [the longest x4 95.4 us: feed(): pl.pallas_call(feed_kernel, out_shape=(S((h, width), BF), S((h, width), B...]
    unnamed x464 -> x98, local copies, waits for them, and re-layouts: 121 us -> 10.9 us
    reshape x44 -> x8, local copies, waits for them, and re-layouts: 79 us -> 1.94 us  [the longest x2 1.52 us: per_device(): small = jnp.concatenate([vectors.reshape(-1), b_up.reshape(-1)])]
    all_gather x8 -> x0, blocking collectives: 75.2 us -> none  [the longest x1 21.8 us: fetch(): lax.all_gather(sectioned[5], 'mod', axis=1, tiled=True)]
    unnamed x2 -> x0, blocking collectives: 67.1 us -> none
  transfers between devices with their start and end apart: 60 -> 52, of which waited for: 42 -> 28; matrix products, arithmetic and copies ran while one was open for 28% -> 11% of each run, Pallas kernels for 0% -> 23%
where the time goes in v1:
time: 733 us; the launch traced here: 725 us
  waiting for transfers between devices  315 us (43%)
  Pallas kernels  209 us (29%)
  starting transfers between devices  56.3 us (8%)
  matrix products  43.3 us (6%)
  blocking collectives  40.4 us (6%)
  local copies, waits for them, and re-layouts  35.4 us (5%)
  other arithmetic  24.2 us (3%)
    ppermute x52, waiting for transfers between devices, swapped(): return lax.ppermute(values, axis, [(i, i ^ mask) for i in range(count)])  315 us
    pallas_call x4, Pallas kernels, feed(): pl.pallas_call(feed_kernel, out_shape=(S((h, width), BF), S((h, width), B...  95.4 us
    pallas_call x4, Pallas kernels, back(): pl.pallas_call(back_kernel, out_shape=(S((r, 3 * width), BF), S((h, width...  65.4 us
    ppermute x52, starting transfers between devices, swapped(): return lax.ppermute(values, axis, [(i, i ^ mask) for i in range(count)])  56.3 us
    pallas_call x4, Pallas kernels, attend(): pl.pallas_call(attend_kernel, out_shape=(jax.ShapeDtypeStruct((2 * h, 3 *...  48.1 us
    dot_general x4, matrix products, tn(): lax.dot_general(a, b, (((0,), (0,)), ((), ())), preferred_element_type=F32)  43.3 us
    psum x1, blocking collectives, per_device(): tiny_sum = lax.psum(tiny_grad.astype(BF), ('mod', 'pair'))  40.4 us
  transfers between devices with their start and end apart: 52, of which 28 were waited for; matrix products, arithmetic and copies ran while one was open for 11% of the time, Pallas kernels for 23%

profile of v1, /device:TPU:0, one launch (start us, length us, event | category | flops | bytes accessed | tf_op | source)
XLA Modules:
  0.0 725.4 jit_solution(1016226824471211718)
XLA Ops:
  10.3 9.1 %collective-permute-done.13 = bf16[48,1536]{1,0:T(8,128)(2,1)S(1)} collective-permute-done((bf16[48,1536]{1,0:T(8,128)(2,1)}, bf16[48,1536]{1,0:T(8,128)(2,1)S(1)}, u32[]{:S(2)}, u32[]{:S(2)}) %collective-permute-start.13) | collective-permute-done | bytes 147488 | tf_op jit(solution)/shard_map/ppermute | solution.py:241
  74.0 16.1 %collective-permute-done.10 = bf16[2,2,192,384]{3,2,0,1:T(8,128)(2,1)S(1)} collective-permute-done((bf16[2,2,192,384]{3,2,0,1:T(8,128)(2,1)}, bf16[2,2,192,384]{3,2,0,1:T(8,128)(2,1)S(1)}, u32[]{:S(2)}, u32[]{:S(2)}) %collective-permute-start.10) | collective-permute-done | bytes 589856 | tf_op jit(solution)/shard_map/ppermute | solution.py:241
  93.6 22.6 %collective-permute-done.5 = bf16[2,2,208,768]{3,2,0,1:T(8,128)(2,1)S(1)} collective-permute-done((bf16[2,2,208,768]{3,2,0,1:T(8,128)(2,1)S(1)}, bf16[2,2,208,768]{3,2,0,1:T(8,128)(2,1)S(1)}, u32[]{:S(2)}, u32[]{:S(2)}) %collective-permute-start.5) | collective-permute-done | bytes 1277984 | tf_op jit(solution)/shard_map/ppermute | solution.py:241
  127.1 17.4 %collective-permute-done.19.far_ref = bf16[256,768]{1,0:T(8,128)(2,1)S(1)} collective-permute-done((bf16[256,768]{1,0:T(8,128)(2,1)S(1)}, bf16[256,768]{1,0:T(8,128)(2,1)S(1)}, u32[]{:S(2)}, u32[]{:S(2)}) %collective-permute-start.19) | collective-permute-done | bytes 393248 | tf_op jit(solution)/shard_map/ppermute | solution.py:241
  153.1 23.6 %collective-permute-done.22.far_ref = bf16[256,768]{1,0:T(8,128)(2,1)S(1)} collective-permute-done((bf16[256,768]{1,0:T(8,128)(2,1)}, bf16[256,768]{1,0:T(8,128)(2,1)S(1)}, u32[]{:S(2)}, u32[]{:S(2)}) %collective-permute-start.22) | collective-permute-done | bytes 393248 | tf_op jit(solution)/shard_map/ppermute | solution.py:241
  179.5 14.1 %collective-permute-done.25.far_ref = bf16[256,768]{1,0:T(8,128)(2,1)S(1)} collective-permute-done((bf16[256,768]{1,0:T(8,128)(2,1)}, bf16[256,768]{1,0:T(8,128)(2,1)S(1)}, u32[]{:S(2)}, u32[]{:S(2)}) %collective-permute-start.25) | collective-permute-done | bytes 393248 | tf_op jit(solution)/shard_map/ppermute | solution.py:241
  198.4 20.6 %collective-permute-done.26.gfar_ref = bf16[256,768]{1,0:T(8,128)(2,1)} collective-permute-done((bf16[256,768]{1,0:T(8,128)(2,1)}, bf16[256,768]{1,0:T(8,128)(2,1)}, u32[]{:S(2)}, u32[]{:S(2)}) %collective-permute-start.26) | collective-permute-done | bytes 393248 | tf_op jit(solution)/shard_map/ppermute | solution.py:241
  220.7 12.2 %attend.7 = (bf16[512,2304]{1,0:T(8,128)(2,1)}, bf16[4,6,128,256]{3,2,1,0:T(8,128)(2,1)}, bf16[512,768]{1,0:T(8,128)(2,1)}, f32[512,768]{1,0:T(8,128)}) custom-call(s32[1]{0:T(128)} %bitcast.core_ref, s32[2,4]{1,0:T(2,128)} %get-tuple-element.224.live_ref, bf16[256,768]{1,0:T(8,128)(2,1)} %get-tuple-element.147.own_ref, bf16[256,768]{1,0:T(8,128)(2,1)} %copy-done.7, ...), custom_call_target="tpu_custom_call" | custom-call | tf_op jit(solution)/shard_map/attend/pallas_call | solution.py:101
  232.9 12.0 %attend.6 = (bf16[512,2304]{1,0:T(8,128)(2,1)}, bf16[4,6,128,256]{3,2,1,0:T(8,128)(2,1)}, bf16[512,768]{1,0:T(8,128)(2,1)}, f32[512,768]{1,0:T(8,128)}) custom-call(s32[1]{0:T(128)} %bitcast.core_ref, s32[2,4]{1,0:T(2,128)} %get-tuple-element.225.live_ref, bf16[256,768]{1,0:T(8,128)(2,1)} %get-tuple-element.181.own_ref, bf16[256,768]{1,0:T(8,128)(2,1)} %copy-done.6, ...), custom_call_target="tpu_custom_call" | custom-call | tf_op jit(solution)/shard_map/attend/pallas_call | solution.py:101
  244.9 12.0 %attend.5 = (bf16[512,2304]{1,0:T(8,128)(2,1)}, bf16[4,6,128,256]{3,2,1,0:T(8,128)(2,1)}, bf16[512,768]{1,0:T(8,128)(2,1)}, f32[512,768]{1,0:T(8,128)}) custom-call(s32[1]{0:T(128)} %bitcast.core_ref, s32[2,4]{1,0:T(2,128)} %get-tuple-element.226.live_ref, bf16[256,768]{1,0:T(8,128)(2,1)} %get-tuple-element.151.own_ref, bf16[256,768]{1,0:T(8,128)(2,1)} %copy-done.5, ...), custom_call_target="tpu_custom_call" | custom-call | tf_op jit(solution)/shard_map/attend/pallas_call | solution.py:101
  256.8 12.0 %attend.4 = (bf16[512,2304]{1,0:T(8,128)(2,1)}, bf16[4,6,128,256]{3,2,1,0:T(8,128)(2,1)}, bf16[512,768]{1,0:T(8,128)(2,1)}, f32[512,768]{1,0:T(8,128)}) custom-call(s32[1]{0:T(128)} %bitcast.core_ref, s32[2,4]{1,0:T(2,128)} %get-tuple-element.227.live_ref, bf16[256,768]{1,0:T(8,128)(2,1)} %get-tuple-element.153.own_ref, bf16[256,768]{1,0:T(8,128)(2,1)} %copy-done.4, ...), custom_call_target="tpu_custom_call" | custom-call | tf_op jit(solution)/shard_map/attend/pallas_call | solution.py:101
  268.9 24.0 %feed.7 = (bf16[256,768]{1,0:T(8,128)(2,1)}, bf16[256,768]{1,0:T(8,128)(2,1)}, bf16[512,3072]{1,0:T(8,128)(2,1)}, bf16[512,3072]{1,0:T(8,128)(2,1)}, bf16[512,76...) custom-call(s32[1]{0:T(128)} %bitcast.core_ref, ...), custom_call_target="tpu_custom_call" | custom-call | tf_op jit(solution)/shard_map/feed/pallas_call | solution.py:169
  292.9 16.2 %back.7 = (bf16[512,2304]{1,0:T(8,128)(2,1)}, f32[256,768]{1,0:T(8,128)}, bf16[256,768]{1,0:T(8,128)(2,1)}, f32[8,768]{1,0:T(8,128)}) custom-call(s32[1]{0:T(128)} %bitcast.core_ref, bf16[512,768]{1,0:T(8,128)(2,1)} %get-tuple-element.103.dbranch_ref, bf16[512,2304]{1,0:T(8,128)(2,1)} %get-tuple-element.104.qkv_ref, ...), custom_call_target="tpu_custom_call" | custom-call | tf_op jit(solution)/shard_map/back/pallas_call | solution.py:229
  309.2 23.7 %feed.6 = (bf16[256,768]{1,0:T(8,128)(2,1)}, bf16[256,768]{1,0:T(8,128)(2,1)}, bf16[512,3072]{1,0:T(8,128)(2,1)}, bf16[512,3072]{1,0:T(8,128)(2,1)}, bf16[512,76...) custom-call(s32[1]{0:T(128)} %bitcast.core_ref, ...), custom_call_target="tpu_custom_call" | custom-call | tf_op jit(solution)/shard_map/feed/pallas_call | solution.py:169
  332.9 16.3 %back.6 = (bf16[512,2304]{1,0:T(8,128)(2,1)}, f32[256,768]{1,0:T(8,128)}, bf16[256,768]{1,0:T(8,128)(2,1)}, f32[8,768]{1,0:T(8,128)}) custom-call(s32[1]{0:T(128)} %bitcast.core_ref, bf16[512,768]{1,0:T(8,128)(2,1)} %get-tuple-element.98.dbranch_ref, bf16[512,2304]{1,0:T(8,128)(2,1)} %get-tuple-element.99.qkv_ref, ...), custom_call_target="tpu_custom_call" | custom-call | tf_op jit(solution)/shard_map/back/pallas_call | solution.py:229
  349.2 23.9 %feed.5 = (bf16[256,768]{1,0:T(8,128)(2,1)}, bf16[256,768]{1,0:T(8,128)(2,1)}, bf16[512,3072]{1,0:T(8,128)(2,1)}, bf16[512,3072]{1,0:T(8,128)(2,1)}, bf16[512,76...) custom-call(s32[1]{0:T(128)} %bitcast.core_ref, ...), custom_call_target="tpu_custom_call" | custom-call | tf_op jit(solution)/shard_map/feed/pallas_call | solution.py:169
  373.0 16.5 %back.5 = (bf16[512,2304]{1,0:T(8,128)(2,1)}, f32[256,768]{1,0:T(8,128)}, bf16[256,768]{1,0:T(8,128)(2,1)}, f32[8,768]{1,0:T(8,128)}) custom-call(s32[1]{0:T(128)} %bitcast.core_ref, bf16[512,768]{1,0:T(8,128)(2,1)} %get-tuple-element.93.dbranch_ref, bf16[512,2304]{1,0:T(8,128)(2,1)} %get-tuple-element.94.qkv_ref, ...), custom_call_target="tpu_custom_call" | custom-call | tf_op jit(solution)/shard_map/back/pallas_call | solution.py:229
  390.3 23.7 %feed.4 = (bf16[256,768]{1,0:T(8,128)(2,1)}, bf16[256,768]{1,0:T(8,128)(2,1)}, bf16[512,3072]{1,0:T(8,128)(2,1)}, bf16[512,3072]{1,0:T(8,128)(2,1)}, bf16[512,76...) custom-call(s32[1]{0:T(128)} %bitcast.core_ref, ...), custom_call_target="tpu_custom_call" | custom-call | tf_op jit(solution)/shard_map/feed/pallas_call | solution.py:169
  414.1 16.4 %back.4 = (bf16[512,2304]{1,0:T(8,128)(2,1)}, f32[256,768]{1,0:T(8,128)}, bf16[256,768]{1,0:T(8,128)(2,1)}, f32[8,768]{1,0:T(8,128)}) custom-call(s32[1]{0:T(128)} %bitcast.core_ref, bf16[512,768]{1,0:T(8,128)(2,1)} %get-tuple-element.88.dbranch_ref, bf16[512,2304]{1,0:T(8,128)(2,1)} %get-tuple-element.89.qkv_ref, ...), custom_call_target="tpu_custom_call" | custom-call | tf_op jit(solution)/shard_map/back/pallas_call | solution.py:229
  432.1 40.4 %psum.7 = bf16[16,2,288]{2,1,0:T(2,128)(2,1)S(1)} all-reduce(bf16[16,2,288]{2,1,0:T(2,128)(2,1)S(1)} %pad_maximum_fusion.14), channel_id=1, replica_groups=mesh['mod'=16,'pair'=2] {'mod','pair'}, use_global_device_ids=true, to_apply=%region_0.1 | all-reduce | flops 9216 | bytes 36864 | tf_op jit(solution)/shard_map/psum | solution.py:395
  473.9 14.9 %fusion.24 = bf16[768,3072]{1,0:T(8,128)(2,1)} fusion(bf16[512,3072]{1,0:T(8,128)(2,1)S(1)} %copy-done.31, bf16[512,3072]{1,0:T(8,128)(2,1)} %get-tuple-element.130, bf16[512,3072]{1,0:T(8,128)(2,1)} %get-tuple-element.129, bf16[512,3072]{1,0:T(8,128)(2,1)} %get-tuple-element.128, bf16[512,768]{1,0:T(8,128)(2,1)} %get-tuple-element.127, ...), kind=kOutput, calls=%fused_computation.24 | convolution fusion | flops 9728950272 | bytes 20447232 | tf_op jit(solution)/shard_map/dot_general | solution.py:23
  493.2 15.4 %fusion.30 = bf16[3072,768]{1,0:T(8,128)(2,1)} fusion(bf16[512,3072]{1,0:T(8,128)(2,1)} %get-tuple-element.119, bf16[512,3072]{1,0:T(8,128)(2,1)} %get-tuple-element.118, bf16[512,3072]{1,0:T(8,128)(2,1)} %get-tuple-element.117, bf16[512,3072]{1,0:T(8,128)(2,1)} %get-tuple-element.116, bf16[512,768]{1,0:T(8,128)(2,1)S(1)} %copy-done.37, ...), kind=kOutput, calls=%fused_computation.26 | convolution fusion | flops 9728950272 | bytes 20447232 | tf_op jit(solution)/shard_map/dot_general | solution.py:23
  517.2 10.3 %fusion.27 = bf16[2304,768]{1,0:T(8,128)(2,1)S(1)} fusion(bf16[2048,768]{1,0:T(8,128)(2,1)S(1)} %copy-done.21, bf16[512,2304]{1,0:T(8,128)(2,1)S(1)} %copy-done.32, bf16[512,2304]{1,0:T(8,128)(2,1)} %get-tuple-element.110, bf16[512,2304]{1,0:T(8,128)(2,1)} %get-tuple-element.109, bf16[512,2304]{1,0:T(8,128)(2,1)} %get-tuple-element.108), kind=kOutput, calls=%fused_computation.25 | convolution fusion | flops 7287275520 | bytes 16121856 | tf_op jit(solution)/shard_map/dot_general | solution.py:23
  532.2 9.9 %collective-permute-done.28 = bf16[256,768]{1,0:T(8,128)(2,1)S(1)} collective-permute-done((bf16[256,768]{1,0:T(8,128)(2,1)S(1)}, bf16[256,768]{1,0:T(8,128)(2,1)S(1)}, u32[]{:S(2)}, u32[]{:S(2)}) %collective-permute-start.28) | collective-permute-done | bytes 393248 | tf_op jit(solution)/shard_map/ppermute | solution.py:241
  542.3 16.7 %collective-permute-done.29 = bf16[256,768]{1,0:T(8,128)(2,1)S(1)} collective-permute-done((bf16[256,768]{1,0:T(8,128)(2,1)S(1)}, bf16[256,768]{1,0:T(8,128)(2,1)S(1)}, u32[]{:S(2)}, u32[]{:S(2)}) %collective-permute-start.29) | collective-permute-done | bytes 393248 | tf_op jit(solution)/shard_map/ppermute | solution.py:241
  559.1 16.8 %collective-permute-done.18 = bf16[256,768]{1,0:T(8,128)(2,1)S(1)} collective-permute-done((bf16[256,768]{1,0:T(8,128)(2,1)S(1)}, bf16[256,768]{1,0:T(8,128)(2,1)S(1)}, u32[]{:S(2)}, u32[]{:S(2)}) %collective-permute-start.18) | collective-permute-done | bytes 393248 | tf_op jit(solution)/shard_map/ppermute | solution.py:241
  576.0 16.7 %collective-permute-done.30 = bf16[256,768]{1,0:T(8,128)(2,1)S(1)} collective-permute-done((bf16[256,768]{1,0:T(8,128)(2,1)S(1)}, bf16[256,768]{1,0:T(8,128)(2,1)S(1)}, u32[]{:S(2)}, u32[]{:S(2)}) %collective-permute-start.30) | collective-permute-done | bytes 393248 | tf_op jit(solution)/shard_map/ppermute | solution.py:241
  592.8 8.2 %collective-permute-done.31 = bf16[256,768]{1,0:T(8,128)(2,1)S(1)} collective-permute-done((bf16[256,768]{1,0:T(8,128)(2,1)S(1)}, bf16[256,768]{1,0:T(8,128)(2,1)S(1)}, u32[]{:S(2)}, u32[]{:S(2)}) %collective-permute-start.31) | collective-permute-done | bytes 393248 | tf_op jit(solution)/shard_map/ppermute | solution.py:241
  609.3 19.9 %collective-permute-done.21 = bf16[256,768]{1,0:T(8,128)(2,1)S(1)} collective-permute-done((bf16[256,768]{1,0:T(8,128)(2,1)S(1)}, bf16[256,768]{1,0:T(8,128)(2,1)S(1)}, u32[]{:S(2)}, u32[]{:S(2)}) %collective-permute-start.21) | collective-permute-done | bytes 393248 | tf_op jit(solution)/shard_map/ppermute | solution.py:241
  635.7 10.4 %collective-permute-done.24 = bf16[256,768]{1,0:T(8,128)(2,1)S(1)} collective-permute-done((bf16[256,768]{1,0:T(8,128)(2,1)S(1)}, bf16[256,768]{1,0:T(8,128)(2,1)S(1)}, u32[]{:S(2)}, u32[]{:S(2)}) %collective-permute-start.24) | collective-permute-done | bytes 393248 | tf_op jit(solution)/shard_map/ppermute | solution.py:241
  663.7 20.9 %collective-permute-done.34 = bf16[2,2,1,144,384]{4,3,2,1,0:T(8,128)(2,1)S(1)} collective-permute-done((bf16[2,2,1,144,384]{4,3,2,1,0:T(8,128)(2,1)S(1)}, bf16[2,2,1,144,384]{4,3,2,1,0:T(8,128)(2,1)S(1)}, u32[]{:S(2)}, u32[]{:S(2)}) %collective-permute-start.34) | collective-permute-done | bytes 442400 | tf_op jit(solution)/shard_map/ppermute | solution.py:241
  687.3 9.3 %collective-permute-done.49 = bf16[2,2,1,48,1536]{4,3,2,1,0:T(8,128)(2,1)S(1)} collective-permute-done((bf16[2,2,1,48,1536]{4,3,2,1,0:T(8,128)(2,1)S(1)}, bf16[2,2,1,48,1536]{4,3,2,1,0:T(8,128)(2,1)S(1)}, u32[]{:S(2)}, u32[]{:S(2)}) %collective-permute-start.49) | collective-permute-done | bytes 589856 | tf_op jit(solution)/shard_map/ppermute | solution.py:241
  (296 shorter events, 180.9 us)
Async XLA Ops:
  48.4 43.4 %collective-permute-start.16 = (bf16[2,2,48,3072]{3,2,0,1:T(8,128)(2,1)}, bf16[2,2,48,3072]{3,2,0,1:T(8,128)(2,1)}, u32[]{:S(2)}, u32[]{:S(2)}) collective-permute-start(bf16[2,2,48,3072]{3,2,0,1:T(8,128)(2,1)} %pad_maximum_fusion.5), channel_id=1, source_target_pairs={{0,4},{2,6},{4,0},{6,2},{8,12},{10,14},{12,8},{14,10},{16,20},{18,... | collective-permute-start | bytes 3538952 | tf_op jit(solution)/shard_map/ppermute | solution.py:241
  50.8 39.3 %collective-permute-start.10 = (bf16[2,2,192,384]{3,2,0,1:T(8,128)(2,1)}, bf16[2,2,192,384]{3,2,0,1:T(8,128)(2,1)S(1)}, u32[]{:S(2)}, u32[]{:S(2)}) collective-permute-start(bf16[2,2,192,384]{3,2,0,1:T(8,128)(2,1)} %pad_maximum_fusion.7), channel_id=1, source_target_pairs={{0,4},{2,6},{4,0},{6,2},{8,12},{10,14},{12,8},{14,10},{16,20},{18,... | collective-permute-start | bytes 1769480 | tf_op jit(solution)/shard_map/ppermute | solution.py:241
  63.6 52.7 %collective-permute-start.5 = (bf16[2,2,208,768]{3,2,0,1:T(8,128)(2,1)S(1)}, bf16[2,2,208,768]{3,2,0,1:T(8,128)(2,1)S(1)}, u32[]{:S(2)}, u32[]{:S(2)}) collective-permute-start(bf16[2,2,208,768]{3,2,0,1:T(8,128)(2,1)S(1)} %pad_maximum_fusion.3), channel_id=1, source_target_pairs={{0,4},{2,6},{4,0},{6,2},{8,12},{10,14},{12,8},{14,10},{16,20},{18,... | collective-permute-start | bytes 3833864 | tf_op jit(solution)/shard_map/ppermute | solution.py:241
  90.4 29.2 %collective-permute-start.11 = (bf16[2,2,2,192,384]{4,3,0,1,2:T(8,128)(2,1)S(1)}, bf16[2,2,2,192,384]{4,3,0,1,2:T(8,128)(2,1)S(1)}, u32[]{:S(2)}, u32[]{:S(2)}) collective-permute-start(bf16[2,2,2,192,384]{4,3,0,1,2:T(8,128)(2,1)S(1)} %pad_maximum_fusion.4), channel_id=1, source_target_pairs={{0,1},{1,0},{2,3},{3,2},{4,5},{5,4},{6,7},{7,6},{8,9},{9,8},{10,11... | collective-permute-start | bytes 3538952 | tf_op jit(solution)/shard_map/ppermute | solution.py:241
  117.2 77.3 %collective-permute-start.6 = (bf16[8,208,768]{2,1,0:T(8,128)(2,1)S(1)}, bf16[8,208,768]{2,1,0:T(8,128)(2,1)}, u32[]{:S(2)}, u32[]{:S(2)}) collective-permute-start(bf16[8,208,768]{2,1,0:T(8,128)(2,1)S(1)} %bitcast.102), channel_id=1, source_target_pairs={{0,2},{2,0},{4,6},{6,4},{8,10},{10,8},{12,14},{14,12},{16,18},{18,... | collective-permute-start | bytes 7667720 | tf_op jit(solution)/shard_map/ppermute | solution.py:241
  119.5 149.4 %collective-permute-start.17 = (bf16[8,48,3072]{2,1,0:T(8,128)(2,1)}, bf16[8,48,3072]{2,1,0:T(8,128)(2,1)}, u32[]{:S(2)}, u32[]{:S(2)}) collective-permute-start(bf16[8,48,3072]{2,1,0:T(8,128)(2,1)} %bitcast.31.da_ref), channel_id=1, source_target_pairs={{0,2},{2,0},{4,6},{6,4},{8,10},{10,8},{12,14},{14,12},{16,18},{18,... | collective-permute-start | bytes 7077896 | tf_op jit(solution)/shard_map/ppermute | solution.py:241
  121.6 147.2 %collective-permute-start.12 = (bf16[8,192,768]{2,1,0:T(8,128)(2,1)}, bf16[8,192,768]{2,1,0:T(8,128)(2,1)}, u32[]{:S(2)}, u32[]{:S(2)}) collective-permute-start(bf16[8,192,768]{2,1,0:T(8,128)(2,1)} %bitcast.23.ua_ref), channel_id=1, source_target_pairs={{0,2},{2,0},{4,6},{6,4},{8,10},{10,8},{12,14},{14,12},{16,18},{18,... | collective-permute-start | bytes 7077896 | tf_op jit(solution)/shard_map/ppermute | solution.py:241
  125.8 23.7 %collective-permute-start = (s32[16]{0:T(128)S(1)}, s32[16]{0:T(128)S(1)}, u32[]{:S(2)}, u32[]{:S(2)}) collective-permute-start(s32[16]{0:T(128)S(1)} %get-tuple-element.229), channel_id=1, source_target_pairs={{0,16},{2,18},{4,20},{6,22},{8,24},{10,26},{12,28},{14,30},{16,0},... | collective-permute-start | bytes 200 | tf_op jit(solution)/shard_map/ppermute | solution.py:241
  147.8 29.0 %collective-permute-start.22 = (bf16[256,768]{1,0:T(8,128)(2,1)}, bf16[256,768]{1,0:T(8,128)(2,1)S(1)}, u32[]{:S(2)}, u32[]{:S(2)}) collective-permute-start(bf16[256,768]{1,0:T(8,128)(2,1)} %get-tuple-element.179), channel_id=1, source_target_pairs={{0,16},{2,18},{4,20},{6,22},{8,24},{10,26},{12,28},{14,30},{16,0},... | collective-permute-start | bytes 1179656 | tf_op jit(solution)/shard_map/ppermute | solution.py:241
  149.5 44.1 %collective-permute-start.25 = (bf16[256,768]{1,0:T(8,128)(2,1)}, bf16[256,768]{1,0:T(8,128)(2,1)S(1)}, u32[]{:S(2)}, u32[]{:S(2)}) collective-permute-start(bf16[256,768]{1,0:T(8,128)(2,1)} %get-tuple-element.178), channel_id=1, source_target_pairs={{0,16},{2,18},{4,20},{6,22},{8,24},{10,26},{12,28},{14,30},{16,0},... | collective-permute-start | bytes 1179656 | tf_op jit(solution)/shard_map/ppermute | solution.py:241
  176.8 42.2 %collective-permute-start.26 = (bf16[256,768]{1,0:T(8,128)(2,1)}, bf16[256,768]{1,0:T(8,128)(2,1)}, u32[]{:S(2)}, u32[]{:S(2)}) collective-permute-start(bf16[256,768]{1,0:T(8,128)(2,1)} %get-tuple-element.170), channel_id=1, source_target_pairs={{0,16},{2,18},{4,20},{6,22},{8,24},{10,26},{12,28},{14,30},{16,0},... | collective-permute-start | bytes 1179656 | tf_op jit(solution)/shard_map/ppermute | solution.py:241
  193.6 115.5 %collective-permute-start.23 = (bf16[256,768]{1,0:T(8,128)(2,1)}, bf16[256,768]{1,0:T(8,128)(2,1)}, u32[]{:S(2)}, u32[]{:S(2)}) collective-permute-start(bf16[256,768]{1,0:T(8,128)(2,1)} %get-tuple-element.171), channel_id=1, source_target_pairs={{0,16},{2,18},{4,20},{6,22},{8,24},{10,26},{12,28},{14,30},{16,0},... | collective-permute-start | bytes 1179656 | tf_op jit(solution)/shard_map/ppermute | solution.py:241
  194.5 154.7 %collective-permute-start.20 = (bf16[256,768]{1,0:T(8,128)(2,1)}, bf16[256,768]{1,0:T(8,128)(2,1)}, u32[]{:S(2)}, u32[]{:S(2)}) collective-permute-start(bf16[256,768]{1,0:T(8,128)(2,1)} %get-tuple-element.173), channel_id=1, source_target_pairs={{0,16},{2,18},{4,20},{6,22},{8,24},{10,26},{12,28},{14,30},{16,0},... | collective-permute-start | bytes 1179656 | tf_op jit(solution)/shard_map/ppermute | solution.py:241
  219.0 170.5 %collective-permute-start.7 = (bf16[256,768]{1,0:T(8,128)(2,1)}, bf16[256,768]{1,0:T(8,128)(2,1)S(1)}, u32[]{:S(2)}, u32[]{:S(2)}) collective-permute-start(bf16[256,768]{1,0:T(8,128)(2,1)} %get-tuple-element.175), channel_id=1, source_target_pairs={{0,16},{2,18},{4,20},{6,22},{8,24},{10,26},{12,28},{14,30},{16,0},... | collective-permute-start | bytes 1179656 | tf_op jit(solution)/shard_map/ppermute | solution.py:241
  493.2 107.9 %collective-permute-start.47 = (bf16[8,48,3072]{2,1,0:T(8,128)(2,1)}, bf16[8,48,3072]{2,1,0:T(8,128)(2,1)}, u32[]{:S(2)}, u32[]{:S(2)}) collective-permute-start(bf16[8,48,3072]{2,1,0:T(8,128)(2,1)} %get-tuple-element.157), channel_id=1, source_target_pairs={{0,2},{2,0},{4,6},{6,4},{8,10},{10,8},{12,14},{14,12},{16,18},{18,... | collective-permute-start | bytes 7077896 | tf_op jit(solution)/shard_map/ppermute | solution.py:241
  513.1 118.8 %collective-permute-start.42 = (bf16[8,192,768]{2,1,0:T(8,128)(2,1)}, bf16[8,192,768]{2,1,0:T(8,128)(2,1)}, u32[]{:S(2)}, u32[]{:S(2)}) collective-permute-start(bf16[8,192,768]{2,1,0:T(8,128)(2,1)} %get-tuple-element.161), channel_id=1, source_target_pairs={{0,2},{2,0},{4,6},{6,4},{8,10},{10,8},{12,14},{14,12},{16,18},{18,... | collective-permute-start | bytes 7077896 | tf_op jit(solution)/shard_map/ppermute | solution.py:241
  513.6 28.5 %collective-permute-start.28 = (bf16[256,768]{1,0:T(8,128)(2,1)S(1)}, bf16[256,768]{1,0:T(8,128)(2,1)S(1)}, u32[]{:S(2)}, u32[]{:S(2)}) collective-permute-start(bf16[256,768]{1,0:T(8,128)(2,1)S(1)} %copy-done.45), channel_id=1, source_target_pairs={{0,16},{2,18},{4,20},{6,22},{8,24},{10,26},{12,28},{14,30},{16,0},... | collective-permute-start | bytes 1179656 | tf_op jit(solution)/shard_map/ppermute | solution.py:241
  527.7 78.8 %collective-permute-start.32 = (bf16[8,144,768]{2,1,0:T(8,128)(2,1)S(1)}, bf16[8,144,768]{2,1,0:T(8,128)(2,1)S(1)}, u32[]{:S(2)}, u32[]{:S(2)}) collective-permute-start(bf16[8,144,768]{2,1,0:T(8,128)(2,1)S(1)} %get-tuple-element.169), channel_id=1, source_target_pairs={{0,2},{2,0},{4,6},{6,4},{8,10},{10,8},{12,14},{14,12},{16,18},{18,... | collective-permute-start | bytes 5308424 | tf_op jit(solution)/shard_map/ppermute | solution.py:241
  528.4 30.5 %collective-permute-start.29 = (bf16[256,768]{1,0:T(8,128)(2,1)S(1)}, bf16[256,768]{1,0:T(8,128)(2,1)S(1)}, u32[]{:S(2)}, u32[]{:S(2)}) collective-permute-start(bf16[256,768]{1,0:T(8,128)(2,1)S(1)} %copy-done.43), channel_id=1, source_target_pairs={{0,16},{2,18},{4,20},{6,22},{8,24},{10,26},{12,28},{14,30},{16,0},... | collective-permute-start | bytes 1179656 | tf_op jit(solution)/shard_map/ppermute | solution.py:241
  542.1 33.7 %collective-permute-start.18 = (bf16[256,768]{1,0:T(8,128)(2,1)S(1)}, bf16[256,768]{1,0:T(8,128)(2,1)S(1)}, u32[]{:S(2)}, u32[]{:S(2)}) collective-permute-start(bf16[256,768]{1,0:T(8,128)(2,1)S(1)} %copy-done.44), channel_id=1, source_target_pairs={{0,16},{2,18},{4,20},{6,22},{8,24},{10,26},{12,28},{14,30},{16,0},... | collective-permute-start | bytes 1179656 | tf_op jit(solution)/shard_map/ppermute | solution.py:241
  559.0 33.7 %collective-permute-start.30 = (bf16[256,768]{1,0:T(8,128)(2,1)S(1)}, bf16[256,768]{1,0:T(8,128)(2,1)S(1)}, u32[]{:S(2)}, u32[]{:S(2)}) collective-permute-start(bf16[256,768]{1,0:T(8,128)(2,1)S(1)} %copy-done.42), channel_id=1, source_target_pairs={{0,16},{2,18},{4,20},{6,22},{8,24},{10,26},{12,28},{14,30},{16,0},... | collective-permute-start | bytes 1179656 | tf_op jit(solution)/shard_map/ppermute | solution.py:241
  575.8 25.2 %collective-permute-start.31 = (bf16[256,768]{1,0:T(8,128)(2,1)S(1)}, bf16[256,768]{1,0:T(8,128)(2,1)S(1)}, u32[]{:S(2)}, u32[]{:S(2)}) collective-permute-start(bf16[256,768]{1,0:T(8,128)(2,1)S(1)} %copy-done.40), channel_id=1, source_target_pairs={{0,16},{2,18},{4,20},{6,22},{8,24},{10,26},{12,28},{14,30},{16,0},... | collective-permute-start | bytes 1179656 | tf_op jit(solution)/shard_map/ppermute | solution.py:241
  592.7 39.0 %collective-permute-start.37 = (bf16[8,48,768]{2,1,0:T(8,128)(2,1)S(1)}, bf16[8,48,768]{2,1,0:T(8,128)(2,1)S(1)}, u32[]{:S(2)}, u32[]{:S(2)}) collective-permute-start(bf16[8,48,768]{2,1,0:T(8,128)(2,1)S(1)} %get-tuple-element.203), channel_id=1, source_target_pairs={{0,2},{2,0},{4,6},{6,4},{8,10},{10,8},{12,14},{14,12},{16,18},{18,... | collective-permute-start | bytes 1769480 | tf_op jit(solution)/shard_map/ppermute | solution.py:241
  601.0 28.2 %collective-permute-start.21 = (bf16[256,768]{1,0:T(8,128)(2,1)S(1)}, bf16[256,768]{1,0:T(8,128)(2,1)S(1)}, u32[]{:S(2)}, u32[]{:S(2)}) collective-permute-start(bf16[256,768]{1,0:T(8,128)(2,1)S(1)} %copy-done.41), channel_id=1, source_target_pairs={{0,16},{2,18},{4,20},{6,22},{8,24},{10,26},{12,28},{14,30},{16,0},... | collective-permute-start | bytes 1179656 | tf_op jit(solution)/shard_map/ppermute | solution.py:241
  601.1 45.0 %collective-permute-start.24 = (bf16[256,768]{1,0:T(8,128)(2,1)S(1)}, bf16[256,768]{1,0:T(8,128)(2,1)S(1)}, u32[]{:S(2)}, u32[]{:S(2)}) collective-permute-start(bf16[256,768]{1,0:T(8,128)(2,1)S(1)} %copy-done.39), channel_id=1, source_target_pairs={{0,16},{2,18},{4,20},{6,22},{8,24},{10,26},{12,28},{14,30},{16,0},... | collective-permute-start | bytes 1179656 | tf_op jit(solution)/shard_map/ppermute | solution.py:241
  606.5 50.5 %collective-permute-start.48 = (bf16[2,2,1,48,3072]{4,3,2,1,0:T(8,128)(2,1)S(1)}, bf16[2,2,1,48,3072]{4,3,2,1,0:T(8,128)(2,1)S(1)}, u32[]{:S(2)}, u32[]{:S(2)}) collective-permute-start(bf16[2,2,1,48,3072]{4,3,2,1,0:T(8,128)(2,1)S(1)} %get-tuple-element.154), channel_id=1, source_target_pairs={{0,4},{2,6},{4,0},{6,2},{8,12},{10,14},{12,8},{14,10},{16,20},{18,... | collective-permute-start | bytes 3538952 | tf_op jit(solution)/shard_map/ppermute | solution.py:241
  629.3 25.4 %collective-permute-start.33 = (bf16[2,2,1,144,768]{4,3,2,1,0:T(8,128)(2,1)S(1)}, bf16[2,2,1,144,768]{4,3,2,1,0:T(8,128)(2,1)S(1)}, u32[]{:S(2)}, u32[]{:S(2)}) collective-permute-start(bf16[2,2,1,144,768]{4,3,2,1,0:T(8,128)(2,1)S(1)} %get-tuple-element.166), channel_id=1, source_target_pairs={{0,4},{2,6},{4,0},{6,2},{8,12},{10,14},{12,8},{14,10},{16,20},{18,... | collective-permute-start | bytes 2654216 | tf_op jit(solution)/shard_map/ppermute | solution.py:241
  631.7 27.3 %collective-permute-start.27 = (bf16[256,768]{1,0:T(8,128)(2,1)S(1)}, bf16[256,768]{1,0:T(8,128)(2,1)S(1)}, u32[]{:S(2)}, u32[]{:S(2)}) collective-permute-start(bf16[256,768]{1,0:T(8,128)(2,1)S(1)} %copy-done.38), channel_id=1, source_target_pairs={{0,16},{2,18},{4,20},{6,22},{8,24},{10,26},{12,28},{14,30},{16,0},... | collective-permute-start | bytes 1179656 | tf_op jit(solution)/shard_map/ppermute | solution.py:241
  646.1 38.7 %collective-permute-start.43 = (bf16[2,2,2,192,384]{4,3,2,1,0:T(8,128)(2,1)S(1)}, bf16[2,2,2,192,384]{4,3,2,1,0:T(8,128)(2,1)S(1)}, u32[]{:S(2)}, u32[]{:S(2)}) collective-permute-start(bf16[2,2,2,192,384]{4,3,2,1,0:T(8,128)(2,1)S(1)} %get-tuple-element.158), channel_id=1, source_target_pairs={{0,1},{1,0},{2,3},{3,2},{4,5},{5,4},{6,7},{7,6},{8,9},{9,8},{10,11... | collective-permute-start | bytes 3538952 | tf_op jit(solution)/shard_map/ppermute | solution.py:241
  654.9 29.8 %collective-permute-start.34 = (bf16[2,2,1,144,384]{4,3,2,1,0:T(8,128)(2,1)S(1)}, bf16[2,2,1,144,384]{4,3,2,1,0:T(8,128)(2,1)S(1)}, u32[]{:S(2)}, u32[]{:S(2)}) collective-permute-start(bf16[2,2,1,144,384]{4,3,2,1,0:T(8,128)(2,1)S(1)} %get-tuple-element.184), channel_id=1, source_target_pairs={{0,1},{1,0},{2,3},{3,2},{4,5},{5,4},{6,7},{7,6},{8,9},{9,8},{10,11... | collective-permute-start | bytes 1327112 | tf_op jit(solution)/shard_map/ppermute | solution.py:241
  657.4 39.2 %collective-permute-start.49 = (bf16[2,2,1,48,1536]{4,3,2,1,0:T(8,128)(2,1)S(1)}, bf16[2,2,1,48,1536]{4,3,2,1,0:T(8,128)(2,1)S(1)}, u32[]{:S(2)}, u32[]{:S(2)}) collective-permute-start(bf16[2,2,1,48,1536]{4,3,2,1,0:T(8,128)(2,1)S(1)} %get-tuple-element.162), channel_id=1, source_target_pairs={{0,1},{1,0},{2,3},{3,2},{4,5},{5,4},{6,7},{7,6},{8,9},{9,8},{10,11... | collective-permute-start | bytes 1769480 | tf_op jit(solution)/shard_map/ppermute | solution.py:241
  661.9 34.9 %collective-permute-start.41 = (bf16[1,1,1,48,384]{4,3,2,1,0:T(8,128)(2,1)S(1)}, bf16[1,1,1,48,384]{4,3,2,1,0:T(8,128)(2,1)S(1)}, u32[]{:S(2)}, u32[]{:S(2)}) collective-permute-start(bf16[1,1,1,48,384]{4,3,2,1,0:T(8,128)(2,1)S(1)} %add_convert_fusion.15), channel_id=1, source_target_pairs={{0,16},{2,18},{4,20},{6,22},{8,24},{10,26},{12,28},{14,30},{16,0},... | collective-permute-start | bytes 110600 | tf_op jit(solution)/shard_map/ppermute | solution.py:241
  (66 other events, 1147.2 us)

commit v2 on v1

v2 whole, which is shorter than its diff:
```python
import functools

import jax
import jax.numpy as jnp
from jax import lax
from jax.experimental import pallas as pl
from jax.experimental.pallas import tpu as pltpu
from jax.sharding import PartitionSpec as P

HEADS = 12
HEAD_DIM = 64
SLOTS = 64
CHUNKS = 4
X_UNITS = (1, 1, 1, 1)
ATTENDS_BEFORE = (0, 2)
FEED_UNITS = (1, 1, 2)
Y_UNITS = (2, 2)
BACK_UNITS = (1, 1, 1, 1)
DX_UNITS = (1, 1, 1, 1)
BLOCKS = 4
EPS = 1e-05
NEG = -1000000000.0
LIMIT = 60 * 2**20
F32 = jnp.float32
BF = jnp.bfloat16
ANY = pl.BlockSpec(memory_space=pl.ANY)
VM = pl.BlockSpec(memory_space=pltpu.VMEM)
SM = pl.BlockSpec(memory_space=pltpu.SMEM)
S = jax.ShapeDtypeStruct
QUICK = pl.CostEstimate(flops=1, bytes_accessed=1, transcendentals=0)
SLOW = pl.CostEstimate(flops=10**10, bytes_accessed=30 * 10**6, transcendentals=0)
DMA = pltpu.SemaphoreType.DMA


def nt(a, b):
    return lax.dot_general(a, b, (((1,), (1,)), ((), ())), preferred_element_type=F32)


def nn(a, b):
    return lax.dot_general(a, b, (((1,), (0,)), ((), ())), preferred_element_type=F32)


def tn(a, b):
    return lax.dot_general(a, b, (((0,), (0,)), ((), ())), preferred_element_type=F32)


def colsum(v):
    return jnp.sum(v, 0, keepdims=True)


def copy(src, dst, sem):
    pltpu.make_async_copy(src, dst, sem).start()


def wait_for(ref, sem):
    pltpu.make_async_copy(ref, ref, sem).wait()


def pull(where, views, part, into, sem):
    core, low, side = where[0], where[1], where[2]
    for piece, (dc, dy, dx) in views:
        slab = (low ^ dy) * 2 + (core ^ dc)
        cols = piece.shape[-1]
        lane = pl.multiple_of((side ^ dx) * cols, cols)
        mid = (slice(None),) * (len(into.shape) - 3)
        copy(piece.at[:, part], into.at[(slice(None), slab) + mid + (pl.ds(lane, cols),)], sem)


def proj_views(refs):
    return [(ref.at[2 * dy + dx], (dc, dy, dx)) for dc, ref in enumerate(refs) for dy in (0, 1) for dx in (0, 1)]


def wide_views(refs):
    first, second = [], []
    for dc in (0, 1):
        for later in (0, 1):
            for early in (0, 1):
                first.append((refs[4 * dc + later].at[early], (dc, later, early)))
                second.append((refs[4 * dc + 2 + later].at[early], (dc, early, later)))
    return first, second


def attend_kernel(c, skip, where, live, rows, far, vec, *refs):
    views, refs = proj_views(refs[:2]), refs[-11:]
    qkv_all, prob_all, mixed_all, x_all, done, wqkv, xs, qkv, prob, mixed, sems = refs
    r, width = xs.shape
    h = r // 2
    seqs = prob.shape[0]
    done[...] = jnp.zeros_like(done)
    start = pl.multiple_of(where[3] + c * h, h)
    copy(rows.at[pl.ds(start, h)], xs.at[pl.ds(0, h)], sems.at[0])
    copy(far.at[pl.ds(skip * h, h)], xs.at[pl.ds(h, h)], sems.at[0])
    pull(where, views, pl.ds(0, wqkv.shape[2]), wqkv, sems.at[1])
    wait_for(xs, sems.at[0])
    span = pl.ds(c * r, r)
    copy(xs, x_all.at[span], sems.at[2])
    wait_for(wqkv, sems.at[1])
    flat = wqkv.reshape(3 * width, width)
    x = xs[...]
    for part in range(3):
        cols = slice(part * width, (part + 1) * width)
        acc = nt(x, flat[cols, :])
        if part == 0:
            acc = acc + vec[0:1, :]
        if part == 2:
            acc = acc + vec[1:2, :]
        qkv[:, cols] = acc.astype(BF)
    copy(qkv, qkv_all.at[span], sems.at[3])
    lane = lax.broadcasted_iota(jnp.int32, (2 * SLOTS, 2 * HEAD_DIM), 1)
    low_half = lane < HEAD_DIM
    key = lax.broadcasted_iota(jnp.int32, (2 * SLOTS, 4 * SLOTS), 1) % (2 * SLOTS)

    def seq(s, carry):
        a = pl.multiple_of(s * SLOTS, SLOTS)
        b = pl.multiple_of(h + s * SLOTS, SLOTS)
        at = c * seqs + s
        valid = key < jnp.where(key < SLOTS, live[0, at], live[1, at] + SLOTS)
        for p in range(HEADS // 2):

            def take(part):
                cols = slice(part * width + p * 128, part * width + (p + 1) * 128)
                return jnp.concatenate([qkv[pl.ds(a, SLOTS), cols], qkv[pl.ds(b, SLOTS), cols]], 0)

            q, k, v = take(0), take(1), take(2)
            zero = jnp.zeros_like(k)
            k2 = jnp.concatenate([jnp.where(low_half, k, zero), jnp.where(low_half, zero, k)], 0)
            v2 = jnp.concatenate([jnp.where(low_half, v, zero), jnp.where(low_half, zero, v)], 0)
            score = jnp.where(valid, nt(q, k2) * (HEAD_DIM**-0.5), NEG)
            halves = []
            for one in (score[:, : 2 * SLOTS], score[:, 2 * SLOTS :]):
                e = jnp.exp(one - jnp.max(one, -1, keepdims=True))
                halves.append((e / jnp.sum(e, -1, keepdims=True)).astype(BF))
            both = jnp.concatenate(halves, 1)
            prob[s, p] = both
            o = nn(both, v2).astype(BF)
            cols = slice(p * 128, (p + 1) * 128)
            mixed[pl.ds(a, SLOTS), cols] = o[:SLOTS]
            mixed[pl.ds(b, SLOTS), cols] = o[SLOTS:]
        copy(prob.at[s], prob_all.at[at], sems.at[4])
        return carry

    lax.fori_loop(0, seqs, seq, 0)
    copy(mixed, mixed_all.at[span], sems.at[5])
    wait_for(xs, sems.at[2])
    wait_for(qkv, sems.at[3])
    wait_for(prob, sems.at[4])
    wait_for(mixed, sems.at[5])


def attend(c, skip, where, live, rows, far, vec, pieces, before, tokens):
    width = far.shape[1]
    total = rows.shape[0]
    r = total // CHUNKS
    seqs = r // 2 // SLOTS
    groups = pieces[0].shape[1]
    per = 3 * width // (4 * groups)
    shapes = (
        S((total, 3 * width), BF),
        S((CHUNKS * seqs, HEADS // 2, 2 * SLOTS, 4 * SLOTS), BF),
        S((total, width), BF),
        S((total, width), BF),
    )
    return pl.pallas_call(
        functools.partial(attend_kernel, c, skip),
        out_shape=shapes + (S((8, 128), F32),),
        in_specs=[SM, SM, ANY, ANY, VM] + [ANY] * (2 + len(before) + len(tokens)),
        out_specs=(ANY,) * 4 + (VM,),
        input_output_aliases={7 + i: i for i in range(len(before))},
        scratch_shapes=[
            pltpu.VMEM((groups, 4, per, width), BF),
            pltpu.VMEM((r, width), BF),
            pltpu.VMEM((r, 3 * width), BF),
            pltpu.VMEM((seqs,) + shapes[1].shape[1:], BF),
            pltpu.VMEM((r, width), BF),
            DMA((6,)),
        ],
        compiler_params=pltpu.CompilerParams(vmem_limit_bytes=LIMIT),
        cost_estimate=SLOW,
        name="attend",
    )(where, live, rows, far, vec, *pieces, *before, *tokens)


def normed(v):
    c = v - jnp.mean(v, -1, keepdims=True)
    r = lax.rsqrt(jnp.mean(c * c, -1, keepdims=True) + EPS)
    return c * r, r


def norm_back(g, n, r):
    return r * (g - jnp.mean(g, -1, keepdims=True) - n * jnp.mean(g * n, -1, keepdims=True))


def feed_kernel(c0, subs, skip, sides, where, grads, far, x_all, mixed_all, vec, bup, *refs):
    first_views, second_views = wide_views(refs[:8])
    refs = refs[-27:]
    outs, sums, refs = refs[:8], refs[8:10], refs[10:]
    y_all, act_all, dinner_all, first_all, dout_all, dbranch_all, dmix_all, y_far = outs
    vsum, bsum = sums
    wout, wup, wdown, xs, mixed, gs, ys, act, slope, dinner, first, dout, dbranch, dmix, acc, n1, sems = refs
    r, width = xs.shape
    h = r // 2
    pull(where, first_views, pl.ds(0, 1), wout, sems.at[0])
    pull(where, first_views, pl.ds(1, BLOCKS), wup, sems.at[1])
    pull(where, second_views, pl.ds(0, BLOCKS), wdown, sems.at[2])
    out_flat = wout.reshape(width, width)
    ff = BLOCKS * width
    up_flat = wup.reshape(ff, width)
    step = width // sides

    def up_block(b):
        parts = [up_flat[pl.ds(side * BLOCKS * step + b * step, step), :] for side in range(sides)]
        return jnp.concatenate(parts, 0)

    def down_block(b):
        return wdown[:, :, b].reshape(width, width)

    for t in range(subs):
        c = c0 + t
        span = pl.ds(c * r, r)
        start = pl.multiple_of(where[3] + c * h, h)
        ins = (
            pltpu.make_async_copy(x_all.at[span], xs, sems.at[3]),
            pltpu.make_async_copy(mixed_all.at[span], mixed, sems.at[3]),
            pltpu.make_async_copy(grads.at[pl.ds(start, h)], gs.at[pl.ds(0, h)], sems.at[4]),
            pltpu.make_async_copy(far.at[pl.ds(t * h, h)], gs.at[pl.ds(h, h)], sems.at[4]),
        )
        for one in ins:
            one.start()
        wait_for(xs, sems.at[3])
        wait_for(mixed, sems.at[3])
        if t == 0:
            wait_for(wout, sems.at[0])
        sum1 = xs[...].astype(F32) + nt(mixed[...], out_flat[...]) + vec[2:3, :]
        hat, r1 = normed(sum1)
        n1[...] = hat
        top = hat * vec[4:5, :] + vec[5:6, :]
        if t:
            for ref in (act, dinner, first, dout, dbranch, dmix, ys):
                wait_for(ref, sems.at[5])
        first[...] = top.astype(BF)
        copy(first, first_all.at[span], sems.at[5])
        acc[...] = top + vec[3:4, :]
        if t == 0:
            wait_for(wup, sems.at[1])
            wait_for(wdown, sems.at[2])
        for b in range(BLOCKS):
            cols = slice(b * width, (b + 1) * width)
            inner = nt(first[...], up_block(b)) + bup[b : b + 1, :]
            phi = 0.5 + 0.5 * lax.erf(inner * (2**-0.5))
            low = (inner * phi).astype(BF)
            act[:, cols] = low
            copy(act.at[:, cols], act_all.at[span, cols], sems.at[5])
            slope[:, cols] = (phi + inner * (jnp.exp(-0.5 * inner * inner) * 0.3989422804014327)).astype(BF)
            acc[...] += nt(low, down_block(b))
        n2, r2 = normed(acc[...])
        ys[...] = (n2 * vec[6:7, :] + vec[7:8, :]).astype(BF)
        copy(ys.at[pl.ds(0, h)], y_all.at[pl.ds(start, h)], sems.at[5])
        copy(ys.at[pl.ds(h, h)], y_far.at[pl.ds((skip + t) * h, h)], sems.at[5])
        wait_for(gs, sems.at[4])
        g = gs[...].astype(F32)
        sums_of = [None] * 6
        sums_of[4] = colsum(g * n2)
        sums_of[5] = colsum(g)
        dz2 = norm_back(g * vec[6:7, :], n2, r2)
        dout[...] = dz2.astype(BF)
        copy(dout, dout_all.at[span], sems.at[5])
        sums_of[1] = colsum(dz2)
        acc[...] = dz2
        for b in range(BLOCKS):
            cols = slice(b * width, (b + 1) * width)
            grad = nn(dout[...], down_block(b)) * slope[:, cols].astype(F32)
            part = colsum(grad)
            bsum[0:1, cols] = part if t == 0 else bsum[0:1, cols] + part
            low = grad.astype(BF)
            dinner[:, cols] = low
            copy(dinner.at[:, cols], dinner_all.at[span, cols], sems.at[5])
            acc[...] += nn(low, up_block(b))
        d = acc[...]
        hat = n1[...]
        sums_of[2] = colsum(d * hat)
        sums_of[3] = colsum(d)
        dz1 = norm_back(d * vec[4:5, :], hat, r1)
        sums_of[0] = colsum(dz1)
        low = dz1.astype(BF)
        dbranch[...] = low
        copy(dbranch, dbranch_all.at[span], sems.at[5])
        dmix[...] = nn(low, out_flat[...]).astype(BF)
        copy(dmix, dmix_all.at[span], sems.at[5])
        for i, part in enumerate(sums_of):
            vsum[i : i + 1, :] = part if t == 0 else vsum[i : i + 1, :] + part
    for ref in (act, dinner, first, dout, dbranch, dmix, ys):
        wait_for(ref, sems.at[5])


def feed(c0, subs, skip, y_rows, sides, where, grads, far, x_all, mixed_all, vec, bup, pieces, before, tokens):
    total, width = x_all.shape
    r = total // CHUNKS
    ff = BLOCKS * width
    groups, thin = pieces[0].shape[1], pieces[0].shape[3]
    shapes = (
        S(grads.shape, BF),
        S((total, ff), BF),
        S((total, ff), BF),
        S((total, width), BF),
        S((total, width), BF),
        S((total, width), BF),
        S((total, width), BF),
    )
    return pl.pallas_call(
        functools.partial(feed_kernel, c0, subs, skip, sides),
        out_shape=shapes + (S((y_rows, width), BF), S((8, width), F32), S((1, ff), F32)),
        in_specs=[SM, ANY, ANY, ANY, ANY, VM, VM] + [ANY] * (8 + len(before) + len(tokens)),
        out_specs=(ANY,) * 8 + (VM,) * 2,
        input_output_aliases={15 + i: i for i in range(len(before))},
        scratch_shapes=[
            pltpu.VMEM((groups, 4, 1, thin, width), BF),
            pltpu.VMEM((groups, 4, BLOCKS, thin, width), BF),
            pltpu.VMEM((groups, 4, BLOCKS, thin, width), BF),
            pltpu.VMEM((r, width), BF),
            pltpu.VMEM((r, width), BF),
            pltpu.VMEM((r, width), BF),
            pltpu.VMEM((r, width), BF),
            pltpu.VMEM((r, ff), BF),
            pltpu.VMEM((r, ff), BF),
            pltpu.VMEM((r, ff), BF),
            pltpu.VMEM((r, width), BF),
            pltpu.VMEM((r, width), BF),
            pltpu.VMEM((r, width), BF),
            pltpu.VMEM((r, width), BF),
            pltpu.VMEM((r, width), F32),
            pltpu.VMEM((r, width), F32),
            DMA((6,)),
        ],
        compiler_params=pltpu.CompilerParams(vmem_limit_bytes=LIMIT),
        cost_estimate=QUICK,
        name="feed",
    )(where, grads, far, x_all, mixed_all, vec, bup, *pieces, *before, *tokens)


def back_kernel(c0, skip, where, qkv_all, prob_all, dbranch_all, dmix_all, *refs):
    views, refs = proj_views(refs[:2]), refs[-13:]
    dx_all, dqkv_all, dx_far, vsum, wqkv, qkv, prob, dbranch, dmix, dqkv, dxs, dxf, sems = refs
    r, width = dbranch.shape
    h = dx_all.shape[0] // (2 * CHUNKS)
    subs = r // (2 * h)
    seqs = h // SLOTS
    span = pl.ds(c0 * 2 * h, r)
    copy(qkv_all.at[span], qkv, sems.at[0])
    copy(dmix_all.at[span], dmix, sems.at[1])
    copy(prob_all.at[pl.ds(c0 * seqs, subs * seqs)], prob, sems.at[2])
    pull(where, views, pl.ds(0, wqkv.shape[2]), wqkv, sems.at[3])
    copy(dbranch_all.at[span], dbranch, sems.at[4])
    wait_for(qkv, sems.at[0])
    wait_for(dmix, sems.at[1])
    wait_for(prob, sems.at[2])
    lane = lax.broadcasted_iota(jnp.int32, (2 * SLOTS, 2 * HEAD_DIM), 1)
    low_half = lane < HEAD_DIM

    def seq(t, s):
        a = pl.multiple_of(2 * h * t + s * SLOTS, SLOTS)
        b = pl.multiple_of(2 * h * t + h + s * SLOTS, SLOTS)
        for p in range(HEADS // 2):

            def take(ref, part):
                cols = slice(part * width + p * 128, part * width + (p + 1) * 128)
                return jnp.concatenate([ref[pl.ds(a, SLOTS), cols], ref[pl.ds(b, SLOTS), cols]], 0)

            q, k, v = take(qkv, 0), take(qkv, 1), take(qkv, 2)
            do = take(dmix, 0)
            zero = jnp.zeros_like(k)
            k2 = jnp.concatenate([jnp.where(low_half, k, zero), jnp.where(low_half, zero, k)], 0)
            v2 = jnp.concatenate([jnp.where(low_half, v, zero), jnp.where(low_half, zero, v)], 0)
            both = prob[t * seqs + s, p]
            dp = nt(do, v2)
            wide = both.astype(F32)
            halves = []
            for u in range(2):
                cols = slice(u * 2 * SLOTS, (u + 1) * 2 * SLOTS)
                w = wide[:, cols] * dp[:, cols]
                halves.append((w - wide[:, cols] * jnp.sum(w, -1, keepdims=True)).astype(BF))
            ds = jnp.concatenate(halves, 1)
            scale = HEAD_DIM**-0.5
            dq = nn(ds, k2) * scale
            dk = tn(ds, q) * scale
            dv = tn(both, do)
            dk = jnp.where(low_half, dk[: 2 * SLOTS], dk[2 * SLOTS :])
            dv = jnp.where(low_half, dv[: 2 * SLOTS], dv[2 * SLOTS :])
            for part, val in enumerate((dq, dk, dv)):
                cols = slice(part * width + p * 128, part * width + (p + 1) * 128)
                dqkv[pl.ds(a, SLOTS), cols] = val[:SLOTS].astype(BF)
                dqkv[pl.ds(b, SLOTS), cols] = val[SLOTS:].astype(BF)

    vsum[...] = jnp.zeros_like(vsum)
    for t in range(subs):
        chunk = pl.ds(t * 2 * h, 2 * h)

        def step(s, carry, t=t):
            seq(t, s)
            return carry

        lax.fori_loop(0, seqs, step, 0)
        copy(dqkv.at[chunk], dqkv_all.at[pl.ds((c0 + t) * 2 * h, 2 * h)], sems.at[5])
        if t == 0:
            wait_for(wqkv, sems.at[3])
            wait_for(dbranch, sems.at[4])
        mine = dqkv[chunk]
        dx = dbranch[chunk].astype(F32) + nn(mine, wqkv.reshape(3 * width, width)[...])
        dxs[t * h : (t + 1) * h, :] = dx[:h]
        start = pl.multiple_of(where[3] + (c0 + t) * h, h)
        copy(dxs.at[pl.ds(t * h, h)], dx_all.at[pl.ds(start, h)], sems.at[6])
        dxf[t * h : (t + 1) * h, :] = dx[h:].astype(BF)
        copy(dxf.at[pl.ds(t * h, h)], dx_far.at[pl.ds((skip + t) * h, h)], sems.at[7])
        vsum[0:1, :] += colsum(mine[:, :width].astype(F32))
        vsum[1:2, :] += colsum(mine[:, 2 * width :].astype(F32))
    wait_for(dqkv, sems.at[5])
    wait_for(dxs, sems.at[6])
    wait_for(dxf, sems.at[7])


def back(c0, subs, skip, dx_rows, where, rows, qkv_all, prob_all, dbranch_all, dmix_all, pieces, before, tokens):
    total, width = dbranch_all.shape
    r = subs * total // CHUNKS
    h = r // 2
    seqs = h // SLOTS
    groups = pieces[0].shape[1]
    per = 3 * width // (4 * groups)
    return pl.pallas_call(
        functools.partial(back_kernel, c0, skip),
        out_shape=(S((rows, width), F32), S((total, 3 * width), BF), S((dx_rows, width), BF), S((8, width), F32)),
        in_specs=[SM] + [ANY] * (6 + len(before) + len(tokens)),
        out_specs=(ANY, ANY, ANY, VM),
        input_output_aliases={7 + i: i for i in range(len(before))},
        scratch_shapes=[
            pltpu.VMEM((groups, 4, per, width), BF),
            pltpu.VMEM((r, 3 * width), BF),
            pltpu.VMEM((seqs,) + prob_all.shape[1:], BF),
            pltpu.VMEM((r, width), BF),
            pltpu.VMEM((r, width), BF),
            pltpu.VMEM((r, 3 * width), BF),
            pltpu.VMEM((h, width), F32),
            pltpu.VMEM((h, width), BF),
            DMA((8,)),
        ],
        compiler_params=pltpu.CompilerParams(vmem_limit_bytes=LIMIT),
        cost_estimate=QUICK,
        name="back",
    )(where, qkv_all, prob_all, dbranch_all, dmix_all, *pieces, *before, *tokens)


def put(buf, where, mod, value, dims, by_pair=False):
    core, low, side = where[0], where[1], where[2]
    cols = buf.shape[-1]
    dc = core ^ (mod & 1)
    dy = low ^ ((mod >> 1) & 1)
    for half in range(2):
        dx = side ^ half
        at = dx * 2 + dy if by_pair else dy * 2 + dx
        buf[(dc, at, mod >> 2) + dims] = value[..., half * cols : (half + 1) * cols]


def hand_over(bufs, outs, sems):
    copies = []
    for i, buf in enumerate(bufs):
        for dc in (1, 0):
            at = 2 * i + dc
            copies.append(pltpu.make_async_copy(buf.at[dc], outs[at], sems.at[at]))
    for one in copies:
        one.start()
    for one in copies:
        one.wait()


def wide_grads_kernel(sides, where, dinner, act, first, dout, dbranch, mixed, *refs):
    outs, (one, two, sems) = refs[-7:-3], refs[-3:]
    b = pl.program_id(0)
    width = first.shape[1]
    thin = one.shape[4]
    mods = 4 * one.shape[2]

    @pl.when(b == 0)
    def _():
        whole = tn(dbranch[...], mixed[...]).astype(BF)
        for mod in range(mods):
            put(one, where, mod, whole[mod * thin : (mod + 1) * thin], (0,))

    up = tn(dinner[...], first[...]).astype(BF)
    step = width // sides
    tall = BLOCKS * thin
    for side in range(sides):
        for i in range(step // tall):
            mod = side * BLOCKS * step // tall + b * (step // tall) + i
            rows = slice(side * step + i * tall, side * step + (i + 1) * tall)
            put(one, where, mod, up[rows].reshape(BLOCKS, thin, width), (pl.ds(1, BLOCKS),))
    down = tn(dout[...], act[...]).astype(BF)
    for mod in range(mods):
        put(two, where, mod, down[mod * thin : (mod + 1) * thin], (b,), True)

    @pl.when(b == BLOCKS - 1)
    def _():
        hand_over((one, two), outs, sems)


def wide_grads(sides, where, dinner, act, first, dout, dbranch, mixed, groups, tokens):
    total, width = first.shape
    thin = width // (4 * groups)
    shapes = [(4, groups, 1 + BLOCKS, thin, width // 2), (4, groups, BLOCKS, thin, width // 2)]

    def whole(array):
        return pl.BlockSpec(array.shape, lambda b: (0, 0), pipeline_mode=pl.Buffered(1))

    block = pl.BlockSpec((total, width), lambda b: (0, b))
    return pl.pallas_call(
        functools.partial(wide_grads_kernel, sides),
        grid=(BLOCKS,),
        out_shape=(S(shapes[0], BF),) * 2 + (S(shapes[1], BF),) * 2,
        in_specs=[SM, block, block, whole(first), whole(dout), whole(dbranch), whole(mixed)] + [ANY] * len(tokens),
        out_specs=(ANY,) * 4,
        scratch_shapes=[pltpu.VMEM((2,) + shapes[0], BF), pltpu.VMEM((2,) + shapes[1], BF), DMA((4,))],
        compiler_params=pltpu.CompilerParams(vmem_limit_bytes=LIMIT),
        cost_estimate=QUICK,
        name="wide_grads",
    )(where, dinner, act, first, dout, dbranch, mixed, *tokens)


def proj_grads_kernel(where, dqkv, x, tiny, *refs):
    keep, send, buf, sems = refs[-4:]
    b = pl.program_id(0)
    mods = 4 * buf.shape[2]
    per = buf.shape[3] - tiny.shape[1]
    part = tn(dqkv[...], x[...]).astype(BF)
    for i in range(mods // 2):
        put(buf, where, b * (mods // 2) + i, part[i * per : (i + 1) * per], (pl.ds(0, per),))

    @pl.when(b == 1)
    def _():
        for mod in range(mods):
            put(buf, where, mod, tiny[mod], (pl.ds(per, tiny.shape[1]),))
        hand_over((buf,), (keep, send), sems)


def proj_grads(where, dqkv, x, tiny, groups, tokens):
    total, width = x.shape
    per = 3 * width // (4 * groups)
    shape = (4, groups, per + tiny.shape[1], width // 2)
    half = dqkv.shape[1] // 2
    return pl.pallas_call(
        proj_grads_kernel,
        grid=(2,),
        out_shape=(S(shape, BF),) * 2,
        in_specs=[
            SM,
            pl.BlockSpec((total, half), lambda b: (0, b)),
            pl.BlockSpec(x.shape, lambda b: (0, 0), pipeline_mode=pl.Buffered(1)),
            pl.BlockSpec(tiny.shape, lambda b: (0, 0, 0), pipeline_mode=pl.Buffered(1)),
        ]
        + [ANY] * len(tokens),
        out_specs=(ANY, ANY),
        scratch_shapes=[pltpu.VMEM((2,) + shape, BF), DMA((2,))],
        compiler_params=pltpu.CompilerParams(vmem_limit_bytes=LIMIT),
        cost_estimate=QUICK,
        name="proj_grads",
    )(where, dqkv, x, tiny, *tokens)


def bits_of(axis):
    return (lax.axis_size(axis) - 1).bit_length()


def swapped(values, axis, mask):
    return lax.ppermute(values, axis, [(i, i ^ mask) for i in range(lax.axis_size(axis))])


def across(values, dc, dy, dx):
    pairs = lax.axis_size("pair")
    mask = (2 * dy + dc) * pairs + dx * (pairs // 2)
    count = lax.axis_size("mod") * pairs
    return lax.ppermute(values, ("mod", "pair"), [(i, i ^ mask) for i in range(count)])


def bit_at(axis, bit):
    return (lax.axis_index(axis) >> bit) & 1


def gather_far(slab, came=None):
    held = slab
    depth = 0
    for bit in range(bits_of("mod") - 1, 1, -1):
        other = swapped(held, "mod", 1 << bit) if depth or came is None else came
        upper = bit_at("mod", bit) == 1
        held = jnp.stack([jnp.where(upper, other, held), jnp.where(upper, held, other)], depth)
        depth += 1
    held = held.reshape((-1,) + slab.shape)
    for bit in range(bits_of("pair") - 1):
        other = swapped(held, "pair", 1 << bit)
        upper = bit_at("pair", bit) == 1
        held = jnp.concatenate([jnp.where(upper, other, held), jnp.where(upper, held, other)], -1)
    return held


def after(values, tokens):
    return lax.optimization_barrier((values, tokens))[0]


def gather_proj(slab):
    held = gather_far(slab)
    near = jnp.stack([held] + [across(held, 0, dy, dx) for dy, dx in ((0, 1), (1, 0), (1, 1))])
    return [near, across(near, 1, 0, 0)]


def gather_wide(slab, came, first):
    held = gather_far(slab, came)
    one, two = held[:, :first], held[:, first:]
    one = jnp.stack([one, across(one, 0, 0, 1)])
    two = jnp.stack([two, across(two, 0, 1, 0)])
    (one, two), early = lax.optimization_barrier(((one, two), (yield)))
    near = [one, across(one, 0, 1, 0), two, across(two, 0, 0, 1)]
    near, late = lax.optimization_barrier((near, (yield)))
    yield near + [across(piece, 1, 0, 0) for piece in near], early[:1] + late[:1]


def low(values):
    return values.astype(BF)


def wide(values):
    return values.astype(F32)


def reduce_proj(keep, send, gate_one, gate_two):
    came = across(send, 1, 0, 0)
    held = wide(keep[0]) + wide(came[0])
    ready = after([low(wide(keep[i]) + wide(came[i])) for i in (1, 2, 3)], gate_one)
    for part, (dy, dx) in zip(ready, ((0, 1), (1, 0), (1, 1))):
        held = held + wide(across(part, 0, dy, dx))
    *_, (held,) = reduce_far(after(held, gate_two))
    return held


def reduce_wide(keep_one, send_one, keep_two, send_two):
    came = across(send_one, 1, 0, 0), across(send_two, 1, 0, 0)
    gate = yield
    came_one, came_two = after(came, gate)
    go_one = low(wide(keep_one[2:]) + wide(came_one[2:]))
    go_two = low(wide(keep_two[2:]) + wide(came_two[2:]))
    back = across(go_one, 0, 1, 0), across(go_two, 0, 0, 1)
    gate = yield [go_one, go_two]
    back_one, back_two = after(back, gate)
    next_one = low(wide(keep_one[1]) + wide(came_one[1]) + wide(back_one[1]))
    next_two = low(wide(keep_two[1]) + wide(came_two[1]) + wide(back_two[1]))
    last = across(next_one, 0, 0, 1), across(next_two, 0, 1, 0)
    gate = yield [next_one, next_two]
    last_one, last_two = after(last, gate)
    held_one = wide(keep_one[0]) + wide(came_one[0]) + wide(back_one[0]) + wide(last_one)
    held_two = wide(keep_two[0]) + wide(came_two[0]) + wide(back_two[0]) + wide(last_two)
    held = jnp.concatenate([held_one, held_two], 1)
    yield [held]
    yield from reduce_far(held)


def reduce_far(held):
    def halved(held, axis, bit, dim):
        size = held.shape[dim] // 2
        mine = bit_at(axis, bit)
        away = low(lax.dynamic_slice_in_dim(held, (1 - mine) * size, size, dim))
        stay = lax.dynamic_slice_in_dim(held, mine * size, size, dim)
        return stay + wide(swapped(away, axis, 1 << bit))

    for bit in range(bits_of("pair") - 2, -1, -1):
        held = halved(held, "pair", bit, held.ndim - 1)
    depth = bits_of("mod") - 2
    rest = held.shape[1:]
    held = held.reshape((2,) * depth + rest)
    for bit in range(2, bits_of("mod")):
        held = halved(held, "mod", bit, depth - 1 - (bit - 2))
        yield [held.reshape((-1,) + rest)]


def settle(pieces, row, rows):
    part = jnp.stack([piece[:, :, row : row + rows] for piece in pieces])
    groups, rows, cols = part.shape[2:]
    part = part.reshape((2, 2, 2) + part.shape[2:])
    bits = (bit_at("mod", 0), bit_at("mod", 1), bit_at("pair", bits_of("pair") - 1))
    for dim, bit in enumerate(bits):
        part = jnp.where(bit == 1, jnp.flip(part, dim), part)
    return part.transpose(3, 1, 0, 4, 2, 5).reshape(4 * groups, rows, 2 * cols)


def per_device(rows_input, grad_out, w_qkv, w_out, w_up, w_down, vectors, b_up, live_rows):
    mods, pairs = lax.axis_size("mod"), lax.axis_size("pair")
    groups = mods // 4
    rows, width = rows_input.shape
    moved = rows // 2
    place = lax.axis_index("mod")
    upper = place >= mods // 2
    own_start = jnp.where(upper, moved, 0)
    away_start = jnp.where(upper, 0, moved)
    where = jnp.stack([place & 1, (place >> 1) & 1, bit_at("pair", bits_of("pair") - 1), own_start])

    def over(values):
        return swapped(values, "mod", mods // 2)

    chunk = moved // CHUNKS

    def units(sizes):
        return [(sum(sizes[:i]), size) for i, size in enumerate(sizes)]

    def over_units(array, sizes):
        return [
            over(lax.dynamic_slice_in_dim(array, away_start + c * chunk, n * chunk)) for c, n in units(sizes)
        ]

    line = w_qkv.shape[0]
    per, thin = w_qkv.shape[1], w_out.shape[1]
    small = jnp.concatenate([vectors.reshape(-1), b_up.reshape(-1)])
    small_rows = -(-small.shape[0] // line)
    small = jnp.pad(small, (0, 16 * line - small.shape[0])).reshape(16, line)
    proj_slab = jnp.concatenate([w_qkv.T, small], 0)
    down = w_down.T.reshape(thin, BLOCKS, line).transpose(1, 0, 2)
    slab = [w_out.T.reshape(1, thin, line), w_up.T.reshape(BLOCKS, thin, line), down]
    slab = jnp.concatenate(slab, 0)

    live_own = lax.dynamic_slice_in_dim(live_rows, own_start // SLOTS, moved // SLOTS)
    live_away = lax.dynamic_slice_in_dim(live_rows, away_start // SLOTS, moved // SLOTS)
    head = jnp.pad(live_away.astype(BF)[None], ((0, 15), (0, width - moved // SLOTS)))
    folded = jnp.concatenate(jnp.split(slab.reshape(-1, line), width // line, 0), 1)
    first_rows = lax.dynamic_slice_in_dim(rows_input, away_start, X_UNITS[0] * chunk)
    parcel = over(jnp.concatenate([first_rows, folded, head], 0))
    tall = folded.shape[0]
    came = parcel[first_rows.shape[0] : first_rows.shape[0] + tall]
    came = jnp.concatenate(jnp.split(came, width // line, 1), 0).reshape(slab.shape)
    live = jnp.stack([live_own, parcel[first_rows.shape[0] + tall, : moved // SLOTS].astype(jnp.int32)])

    proj = gather_proj(proj_slab)
    far_rows = [parcel] + over_units(rows_input, X_UNITS)[1:]
    wide_steps = gather_wide(slab, came, 1 + BLOCKS)
    next(wide_steps)
    far_grads = over_units(grad_out, FEED_UNITS)

    tiny = settle(proj, per, small_rows).reshape(mods, small_rows, pairs, line)
    tiny = tiny.transpose(2, 0, 1, 3).reshape(pairs, mods, -1)
    count = vectors.size
    vec = tiny[:, :, :count].reshape((pairs, mods) + vectors.shape).transpose(0, 2, 1, 3)
    vec = vec.reshape(8, width).astype(F32)
    bup = tiny[:, :, count : count + b_up.size].reshape((pairs, mods) + b_up.shape).transpose(0, 2, 1, 3)
    bup = bup.reshape(pairs, BLOCKS, line).transpose(1, 0, 2).reshape(BLOCKS, width).astype(F32)

    kept = ()
    for (c0, n), far in zip(units(X_UNITS), far_rows):
        for i in range(n):
            *kept, done = attend(c0 + i, i, where, live, rows_input, far, vec, proj, kept, [])
            if c0 + i in ATTENDS_BEFORE:
                arrived = far_rows[3:] + far_grads[:1] if c0 + i else []
                gathered = wide_steps.send([done] + arrived)
    wide_pieces, gates = gathered
    qkv_all, prob_all, mixed_all, x_all = kept
    fed, back_rows = (), []
    vec_sum, bup_sum = 0.0, 0.0
    for (c0, n), far in zip(units(FEED_UNITS), far_grads):
        (y0, size), = [unit for unit in units(Y_UNITS) if unit[0] <= c0 < unit[0] + unit[1]]
        fed = fed[: 7 if c0 == y0 else 8]
        out = feed(
            c0, n, c0 - y0, size * chunk, pairs, where, grad_out, far, x_all, mixed_all, vec, bup, wide_pieces, fed, gates
        )
        gates = []
        fed = out[:8]
        if c0 + n == y0 + size:
            back_rows.append(over(out[7]))
        vec_sum, bup_sum = vec_sum + out[8], bup_sum + out[9]
    result, act_all, dinner_all, first_all, dout_all, dbranch_all, dmix_all = fed[:7]
    wide_pair = wide_grads(
        pairs, where, dinner_all, act_all, first_all, dout_all, dbranch_all, mixed_all, groups, back_rows[:1]
    )
    wide_steps = reduce_wide(*after(wide_pair, back_rows[1:]))
    next(wide_steps)
    backed, back_grads = (), []
    qv_sum, done = 0.0, None
    for c0, n in units(BACK_UNITS):
        (d0, size), = [unit for unit in units(DX_UNITS) if unit[0] <= c0 < unit[0] + unit[1]]
        backed = backed[: 2 if c0 == d0 else 3]
        tokens = []
        if c0 in (1, 3):
            tokens = wide_steps.send(done)
        if c0 == 3:
            tokens = tokens + back_grads[:1]
        out = back(
            c0, n, c0 - d0, size * chunk, where, rows, qkv_all, prob_all, dbranch_all, dmix_all, proj, backed, tokens
        )
        backed, done = out[:3], out[3]
        if c0 + n == d0 + size:
            back_grads.append(over(out[2]))
        qv_sum = qv_sum + out[3]
    input_grad, dqkv_all = backed[:2]

    vec_grad = jnp.concatenate([qv_sum[:2], vec_sum[:6]], 0).reshape(pairs, -1, mods, vectors.shape[1])
    bup_grad = bup_sum.reshape(BLOCKS, pairs, line).transpose(1, 0, 2).reshape(pairs, -1, mods, b_up.shape[1])
    tiny_grad = [g.transpose(2, 0, 1, 3).reshape(mods, pairs, -1) for g in (vec_grad, bup_grad)]
    tiny_grad = jnp.concatenate(tiny_grad, -1)
    tiny_grad = jnp.pad(tiny_grad, ((0, 0), (0, 0), (0, 16 * line - small_size(vectors, b_up))))
    tiny_grad = tiny_grad.reshape(mods, pairs, 16, line).transpose(0, 2, 1, 3).reshape(mods, 16, width).astype(BF)
    tokens = wide_steps.send(done) + back_grads[1:2]
    proj_pair = proj_grads(where, dqkv_all, x_all, tiny_grad, groups, tokens)
    *gates, g_wide = wide_steps
    g_proj = reduce_proj(*after(proj_pair, back_grads[2:3] + gates[0]), [], g_wide)[0]
    g_wide = g_wide[0][0]

    for (c0, n), part in zip(units(Y_UNITS), back_rows):
        result = lax.dynamic_update_slice_in_dim(result, part, away_start + c0 * chunk, 0)
    for (c0, n), part in zip(units(DX_UNITS), back_grads):
        input_grad = lax.dynamic_update_slice_in_dim(input_grad, wide(part), away_start + c0 * chunk, 0)
    g_small = g_proj[per:].reshape(-1)
    return (
        result,
        input_grad,
        g_proj[:per].T,
        g_wide[0].T,
        g_wide[1 : 1 + BLOCKS].reshape(-1, line).T,
        g_wide[1 + BLOCKS :].transpose(1, 0, 2).reshape(thin, -1).T,
        g_small[:count].reshape(vectors.shape),
        g_small[count : count + b_up.size].reshape(b_up.shape),
    )


def small_size(vectors, b_up):
    return vectors.size + b_up.size


def solution(mesh):
    sharded = P("pair", "mod")
    spread = P(("mod", "pair"), None)
    weights = (sharded,) * 6
    return jax.shard_map(
        per_device,
        mesh=mesh,
        in_specs=(spread, spread) + weights + (P(("mod", "pair")),),
        out_specs=(spread, spread) + weights,
        check_vma=False,
    )
```

time: 733 us -> 450 us (0.61)
  waiting for transfers between devices: 315 us -> 104 us
  matrix products: 43.3 us -> 0 us
  blocking collectives: 40.4 us -> 0 us
  Pallas kernels: 209 us -> 234 us
  starting transfers between devices: 56.3 us -> 45.2 us
    ppermute x52 -> x42, waiting for transfers between devices: 315 us -> 104 us  [the longest x20 83.8 us: swapped(): lax.ppermute(values, axis, [(i, i ^ mask) for i in range(lax.axis_size(ax...]
    dot_general x4 -> x0, matrix products: 43.3 us -> none  [tn(): lax.dot_general(a, b, (((0,), (0,)), ((), ())), preferred_element_type=F32)]
    psum x1 -> x0, blocking collectives: 40.4 us -> none  [per_device(): tiny_sum = lax.psum(tiny_grad.astype(BF), ('mod', 'pair'))]
    pallas_call x12 -> x13, Pallas kernels: 209 us -> 234 us  [the longest x3 83.8 us: feed(): pl.pallas_call(functools.partial(feed_kernel, c0, subs, skip, sides), out...]
    ppermute x52 -> x42, starting transfers between devices: 56.3 us -> 45.2 us  [the longest x20 26.9 us: swapped(): lax.ppermute(values, axis, [(i, i ^ mask) for i in range(lax.axis_size(ax...]
    dynamic_slice x6 -> x3, local copies, waits for them, and re-layouts: 13.2 us -> 5.65 us  [over_units(): lax.dynamic_slice_in_dim(array, away_start + c * chunk, n * chunk)]
  transfers between devices with their start and end apart: 52 -> 42, of which waited for: 28 -> 17; matrix products, arithmetic and copies ran while one was open for 11% -> 10% of each run, Pallas kernels for 23% -> 53%
where the time goes in v2:
time: 450 us; the launch traced here: 444 us
  Pallas kernels  234 us (52%)
  waiting for transfers between devices  104 us (23%)
  starting transfers between devices  45.2 us (10%)
  local copies, waits for them, and re-layouts  29.8 us (7%)
  other arithmetic  29.2 us (6%)
    ppermute x20, waiting for transfers between devices, swapped(): lax.ppermute(values, axis, [(i, i ^ mask) for i in range(lax.axis_size(ax...  83.8 us
    pallas_call x3, Pallas kernels, feed(): pl.pallas_call(functools.partial(feed_kernel, c0, subs, skip, sides), out...  83.8 us
    pallas_call x4, Pallas kernels, back(): pl.pallas_call(functools.partial(back_kernel, c0, skip), out_shape=(S((ro...  59.3 us
    pallas_call x4, Pallas kernels, attend(): pl.pallas_call(functools.partial(attend_kernel, c, skip), out_shape=shape...  44.2 us
    pallas_call x1, Pallas kernels, wide_grads(): pl.pallas_call(functools.partial(wide_grads_kernel, sides), grid=(BLOCKS,...  33.6 us
    ppermute x20, starting transfers between devices, swapped(): lax.ppermute(values, axis, [(i, i ^ mask) for i in range(lax.axis_size(ax...  26.9 us
    ppermute x22, waiting for transfers between devices, across(): lax.ppermute(values, ('mod', 'pair'), [(i, i ^ mask) for i in range(count)])  20 us
    ppermute x22, starting transfers between devices, across(): lax.ppermute(values, ('mod', 'pair'), [(i, i ^ mask) for i in range(count)])  18.2 us
  transfers between devices with their start and end apart: 42, of which 17 were waited for; matrix products, arithmetic and copies ran while one was open for 10% of the time, Pallas kernels for 53%

profile of v2, /device:TPU:0, one launch (start us, length us, event | category | flops | bytes accessed | tf_op | source)
XLA Modules:
  0.0 444.2 jit_solution(4019540825257324161)
XLA Ops:
  3.2 4.1 collective-permute-start.3
  10.0 2.4 constant_dynamic-slice_fusion.2
  14.7 19.3 %collective-permute-done.4 = bf16[2,160,384]{2,1,0:T(8,128)(2,1)S(1)} collective-permute-done((bf16[2,160,384]{2,1,0:T(8,128)(2,1)S(1)}, bf16[2,160,384]{2,1,0:T(8,128)(2,1)S(1)}, u32[]{:S(2)}, u32[]{:S(2)}) %collective-permute-start.4) | collective-permute-done | bytes 245792 | tf_op jit(solution)/shard_map/ppermute | solution.py:570
  37.7 10.1 %collective-permute-done.1.far = bf16[488,768]{1,0:T(8,128)(2,1)S(1)} collective-permute-done((bf16[488,768]{1,0:T(8,128)(2,1)S(1)}, bf16[488,768]{1,0:T(8,128)(2,1)S(1)}, u32[]{:S(2)}, u32[]{:S(2)}) %collective-permute-start.1) | collective-permute-done | bytes 749600 | tf_op jit(solution)/shard_map/ppermute | solution.py:570
  48.4 9.4 %collective-permute-done.6 = bf16[4,160,384]{2,1,0:T(8,128)(2,1)S(1)} collective-permute-done((bf16[4,160,384]{2,1,0:T(8,128)(2,1)S(1)}, bf16[4,160,384]{2,1,0:T(8,128)(2,1)S(1)}, u32[]{:S(2)}, u32[]{:S(2)}) %collective-permute-start.6) | collective-permute-done | bytes 491552 | tf_op jit(solution)/shard_map/ppermute | solution.py:577
  58.1 5.8 %collective-permute-done.11 = bf16[2,9,48,384]{3,2,1,0:T(8,128)(2,1)S(1)} collective-permute-done((bf16[2,9,48,384]{3,2,1,0:T(8,128)(2,1)S(1)}, bf16[2,9,48,384]{3,2,1,0:T(8,128)(2,1)S(1)}, u32[]{:S(2)}, u32[]{:S(2)}) %collective-permute-start.11) | collective-permute-done | bytes 663584 | tf_op jit(solution)/shard_map/ppermute | solution.py:570
  76.4 4.9 %collective-permute-done.13 = bf16[4,4,48,384]{3,2,1,0:T(8,128)(2,1)} collective-permute-done((bf16[4,4,48,384]{3,2,1,0:T(8,128)(2,1)}, bf16[4,4,48,384]{3,2,1,0:T(8,128)(2,1)}, u32[]{:S(2)}, u32[]{:S(2)}) %collective-permute-start.13) | collective-permute-done | bytes 589856 | tf_op jit(solution)/shard_map/ppermute | solution.py:577
  81.3 2.5 collective-permute-start.2
  83.7 2.2 pad_maximum_fusion.4.refs_2_
  90.5 11.2 %attend.4 = (bf16[2048,2304]{1,0:T(8,128)(2,1)}, bf16[16,6,128,256]{3,2,1,0:T(8,128)(2,1)}, bf16[2048,768]{1,0:T(8,128)(2,1)}, bf16[2048,768]{1,0:T(8,128)(2,1)}, f32[8,128]{1,0:T(8,128)}) custom-call(s32[4]{0:T(128)} %pad_add_fusion.1.where, s32[2,16]{1,0:T(2,128)} %pad_add_fusion.live, bf16[2048,768]{1,0:T(8,128)(2,1)} %rows.7, ...), custom_call_target="tpu_custom_call" | custom-call | flops 10000000000 | bytes 30000000 | tf_op jit(solution)/shard_map/attend/pallas_call | solution.py:163
  103.2 10.5 %collective-permute-done.10.far = bf16[256,768]{1,0:T(8,128)(2,1)} collective-permute-done((bf16[256,768]{1,0:T(8,128)(2,1)}, bf16[256,768]{1,0:T(8,128)(2,1)}, u32[]{:S(2)}, u32[]{:S(2)}) %collective-permute-start.10) | collective-permute-done | bytes 393248 | tf_op jit(solution)/shard_map/ppermute | solution.py:570
  114.3 10.9 %attend.5 = (bf16[2048,2304]{1,0:T(8,128)(2,1)}, bf16[16,6,128,256]{3,2,1,0:T(8,128)(2,1)}, bf16[2048,768]{1,0:T(8,128)(2,1)}, bf16[2048,768]{1,0:T(8,128)(2,1)}, f32[8,128]{1,0:T(8,128)}) custom-call(s32[4]{0:T(128)} %pad_add_fusion.1.where, s32[2,16]{1,0:T(2,128)} %pad_add_fusion.live, ...), custom_call_target="tpu_custom_call", output_to_operand_aliasing={{0}: (7, {}), {1}: (8, {}), {2}: (9, {}), {3}: (10, {})} | custom-call | flops 10000000000 | bytes 30000000 | tf_op jit(solution)/shard_map/attend/pallas_call | solution.py:163
  125.2 10.9 %attend.6 = (bf16[2048,2304]{1,0:T(8,128)(2,1)}, bf16[16,6,128,256]{3,2,1,0:T(8,128)(2,1)}, bf16[2048,768]{1,0:T(8,128)(2,1)}, bf16[2048,768]{1,0:T(8,128)(2,1)}, f32[8,128]{1,0:T(8,128)}) custom-call(s32[4]{0:T(128)} %pad_add_fusion.1.where, s32[2,16]{1,0:T(2,128)} %pad_add_fusion.live, ...), custom_call_target="tpu_custom_call", output_to_operand_aliasing={{0}: (7, {}), {1}: (8, {}), {2}: (9, {}), {3}: (10, {})} | custom-call | flops 10000000000 | bytes 30000000 | tf_op jit(solution)/shard_map/attend/pallas_call | solution.py:163
  146.0 11.3 %attend.7 = (bf16[2048,2304]{1,0:T(8,128)(2,1)}, bf16[16,6,128,256]{3,2,1,0:T(8,128)(2,1)}, bf16[2048,768]{1,0:T(8,128)(2,1)}, bf16[2048,768]{1,0:T(8,128)(2,1)}, f32[8,128]{1,0:T(8,128)}) custom-call(s32[4]{0:T(128)} %pad_add_fusion.1.where, s32[2,16]{1,0:T(2,128)} %pad_add_fusion.live, ...), custom_call_target="tpu_custom_call", output_to_operand_aliasing={{0}: (7, {}), {1}: (8, {}), {2}: (9, {}), {3}: (10, {})} | custom-call | flops 10000000000 | bytes 30000000 | tf_op jit(solution)/shard_map/attend/pallas_call | solution.py:163
  158.2 22.2 %feed.3 = (bf16[2048,768]{1,0:T(8,128)(2,1)}, bf16[2048,3072]{1,0:T(8,128)(2,1)}, bf16[2048,3072]{1,0:T(8,128)(2,1)}, bf16[2048,768]{1,0:T(8,128)(2,1)}, bf16[20...) custom-call(s32[4]{0:T(128)} %pad_add_fusion.1.where, ...), custom_call_target="tpu_custom_call" | custom-call | flops 1 | bytes 1 | tf_op jit(solution)/shard_map/feed/pallas_call | solution.py:309
  180.4 22.3 %feed.4 = (bf16[2048,768]{1,0:T(8,128)(2,1)}, bf16[2048,3072]{1,0:T(8,128)(2,1)}, bf16[2048,3072]{1,0:T(8,128)(2,1)}, bf16[2048,768]{1,0:T(8,128)(2,1)}, bf16[20...) custom-call(s32[4]{0:T(128)} %pad_add_fusion.1.where, ...), custom_call_target="tpu_custom_call", output_to_operand_aliasing={{0}: (15, {}), {1}: (16, {}), {2}: (17, {}), {3}: (18, {}),... | custom-call | flops 1 | bytes 1 | tf_op jit(solution)/shard_map/feed/pallas_call | solution.py:309
  205.6 39.3 %feed.5 = (bf16[2048,768]{1,0:T(8,128)(2,1)}, bf16[2048,3072]{1,0:T(8,128)(2,1)}, bf16[2048,3072]{1,0:T(8,128)(2,1)}, bf16[2048,768]{1,0:T(8,128)(2,1)}, bf16[20...) custom-call(s32[4]{0:T(128)} %pad_add_fusion.1.where, ...), custom_call_target="tpu_custom_call", output_to_operand_aliasing={{0}: (15, {}), {1}: (16, {}), {2}: (17, {}), {3}: (18, {}),... | custom-call | flops 1 | bytes 1 | tf_op jit(solution)/shard_map/feed/pallas_call | solution.py:309
  246.9 33.6 %wide_grads.1 = (bf16[4,4,5,48,384]{4,3,2,1,0:T(8,128)(2,1)}, bf16[4,4,5,48,384]{4,3,2,1,0:T(8,128)(2,1)}, bf16[4,4,4,48,384]{4,3,2,1,0:T(8,128)(2,1)}, bf16[4,4,4,48,384]{4,3,2,1,0:T(8,128)(2,1)}) custom-call(s32[4]{0:T(128)} %pad_add_fusion.1.where, bf16[2048,3072]{1,0:T(8,128)(2,1)} %get-tuple-element.149.dinner, ...), custom_call_target="tpu_custom_call" | custom-call | flops 1 | bytes 1 | tf_op jit(solution)/shard_map/wide_grads/pallas_call | solution.py:512
  283.3 14.9 %back.4 = (f32[2048,768]{1,0:T(8,128)}, bf16[2048,2304]{1,0:T(8,128)(2,1)}, bf16[256,768]{1,0:T(8,128)(2,1)}, f32[8,768]{1,0:T(8,128)}) custom-call(s32[4]{0:T(128)} %pad_add_fusion.1.where, bf16[2048,2304]{1,0:T(8,128)(2,1)} %get-tuple-element.143.qkv_all, bf16[16,6,128,256]{3,2,1,0:T(8,128)(2,1)} %get-tuple-element.144.prob_all, ...), custom_call_target="tpu_custom_call" | custom-call | flops 1 | bytes 1 | tf_op jit(solution)/shard_map/back/pallas_call | solution.py:427
  299.9 2.3 add_convert_fusion.refs_4_
  305.9 14.7 %back.5 = (f32[2048,768]{1,0:T(8,128)}, bf16[2048,2304]{1,0:T(8,128)(2,1)}, bf16[256,768]{1,0:T(8,128)(2,1)}, f32[8,768]{1,0:T(8,128)}) custom-call(s32[4]{0:T(128)} %pad_add_fusion.1.where, bf16[2048,2304]{1,0:T(8,128)(2,1)} %get-tuple-element.143.qkv_all, ...), custom_call_target="tpu_custom_call", output_to_operand_aliasing={{0}: (7, {}), {1}: (8, {})} | custom-call | flops 1 | bytes 1 | tf_op jit(solution)/shard_map/back/pallas_call | solution.py:427
  320.6 2.5 collective-permute-start.29
  323.1 14.7 %back.6 = (f32[2048,768]{1,0:T(8,128)}, bf16[2048,2304]{1,0:T(8,128)(2,1)}, bf16[256,768]{1,0:T(8,128)(2,1)}, f32[8,768]{1,0:T(8,128)}) custom-call(s32[4]{0:T(128)} %pad_add_fusion.1.where, bf16[2048,2304]{1,0:T(8,128)(2,1)} %get-tuple-element.143.qkv_all, ...), custom_call_target="tpu_custom_call", output_to_operand_aliasing={{0}: (7, {}), {1}: (8, {})} | custom-call | flops 1 | bytes 1 | tf_op jit(solution)/shard_map/back/pallas_call | solution.py:427
  345.8 15.0 %back.7 = (f32[2048,768]{1,0:T(8,128)}, bf16[2048,2304]{1,0:T(8,128)(2,1)}, bf16[256,768]{1,0:T(8,128)(2,1)}, f32[8,768]{1,0:T(8,128)}) custom-call(s32[4]{0:T(128)} %pad_add_fusion.1.where, bf16[2048,2304]{1,0:T(8,128)(2,1)} %get-tuple-element.143.qkv_all, ...), custom_call_target="tpu_custom_call", output_to_operand_aliasing={{0}: (7, {}), {1}: (8, {})} | custom-call | flops 1 | bytes 1 | tf_op jit(solution)/shard_map/back/pallas_call | solution.py:427
  369.7 13.3 %proj_grads.1 = (bf16[4,4,160,384]{3,2,1,0:T(8,128)(2,1)}, bf16[4,4,160,384]{3,2,1,0:T(8,128)(2,1)}) custom-call(s32[4]{0:T(128)} %pad_add_fusion.1.where, bf16[2048,2304]{1,0:T(8,128)(2,1)} %get-tuple-element.176.dqkv, bf16[2048,768]{1,0:T(8,128)(2,1)} %get-tuple-element.113.x_all.x, bf16[16,16,768]{2,1,0:T(8,128)(2,1)} %convert_element_type.250.tiny, ...), custom_call_target="tpu_custom_call" | custom-call | flops 1 | bytes 1 | tf_op jit(solution)/shard_map/proj_grads/pallas_call | solution.py:546
  386.3 2.4 collective-permute-start.31
  396.3 2.5 collective-permute-start.37
  398.8 8.5 %collective-permute-done.31 = bf16[256,768]{1,0:T(8,128)(2,1)S(1)} collective-permute-done((bf16[256,768]{1,0:T(8,128)(2,1)S(1)}, bf16[256,768]{1,0:T(8,128)(2,1)S(1)}, u32[]{:S(2)}, u32[]{:S(2)}) %collective-permute-start.31) | collective-permute-done | bytes 393248 | tf_op jit(solution)/shard_map/ppermute | solution.py:570
  408.2 6.2 %collective-permute-done.40 = bf16[2,1,9,48,384]{4,3,2,1,0:T(8,128)(2,1)S(1)} collective-permute-done((bf16[2,1,9,48,384]{4,3,2,1,0:T(8,128)(2,1)S(1)}, bf16[2,1,9,48,384]{4,3,2,1,0:T(8,128)(2,1)S(1)}, u32[]{:S(2)}, u32[]{:S(2)}) %collective-permute-start.40) | collective-permute-done | bytes 663584 | tf_op jit(solution)/shard_map/ppermute | solution.py:570
  414.6 2.5 collective-permute-start.41
  420.0 12.1 %collective-permute-done.41 = bf16[1,1,9,48,384]{4,3,2,1,0:T(8,128)(2,1)S(1)} collective-permute-done((bf16[1,1,9,48,384]{4,3,2,1,0:T(8,128)(2,1)S(1)}, bf16[1,1,9,48,384]{4,3,2,1,0:T(8,128)(2,1)S(1)}, u32[]{:S(2)}, u32[]{:S(2)}) %collective-permute-start.41) | collective-permute-done | bytes 331808 | tf_op jit(solution)/shard_map/ppermute | solution.py:570
  434.4 7.2 %collective-permute-done.39 = bf16[1,1,160,384]{3,2,1,0:T(8,128)(2,1)S(1)} collective-permute-done((bf16[1,1,160,384]{3,2,1,0:T(8,128)(2,1)S(1)}, bf16[1,1,160,384]{3,2,1,0:T(8,128)(2,1)S(1)}, u32[]{:S(2)}, u32[]{:S(2)}) %collective-permute-start.39) | collective-permute-done | bytes 122912 | tf_op jit(solution)/shard_map/ppermute | solution.py:570
  (227 shorter events, 90.6 us)
Async XLA Ops:
  12.5 35.3 %collective-permute-start.1 = (bf16[488,768]{1,0:T(8,128)(2,1)S(1)}, bf16[488,768]{1,0:T(8,128)(2,1)S(1)}, u32[]{:S(2)}, u32[]{:S(2)}) collective-permute-start(bf16[488,768]{1,0:T(8,128)(2,1)S(1)} %fusion.5), channel_id=1, source_target_pairs={{0,16},{2,18},{4,20},{6,22},{8,24},{10,26},{12,28},{14,30},{16,0},... | collective-permute-start | bytes 2248712 | tf_op jit(solution)/shard_map/ppermute | solution.py:570
  13.3 20.6 %collective-permute-start.4 = (bf16[2,160,384]{2,1,0:T(8,128)(2,1)S(1)}, bf16[2,160,384]{2,1,0:T(8,128)(2,1)S(1)}, u32[]{:S(2)}, u32[]{:S(2)}) collective-permute-start(bf16[2,160,384]{2,1,0:T(8,128)(2,1)S(1)} %pad_maximum_fusion.10), channel_id=1, source_target_pairs={{0,8},{2,10},{4,12},{6,14},{8,0},{10,2},{12,4},{14,6},{16,24},{18,... | collective-permute-start | bytes 737288 | tf_op jit(solution)/shard_map/ppermute | solution.py:570
  35.7 22.0 %collective-permute-start.6 = (bf16[4,160,384]{2,1,0:T(8,128)(2,1)S(1)}, bf16[4,160,384]{2,1,0:T(8,128)(2,1)S(1)}, u32[]{:S(2)}, u32[]{:S(2)}) collective-permute-start(bf16[4,160,384]{2,1,0:T(8,128)(2,1)S(1)} %bitcast.150), channel_id=1, source_target_pairs={{0,4},{1,5},{2,6},{3,7},{4,0},{5,1},{6,2},{7,3},{8,12},{9,13},{10,... | collective-permute-start | bytes 1474568 | tf_op jit(solution)/shard_map/ppermute | solution.py:577
  37.2 20.5 %collective-permute-start.7 = (bf16[4,160,384]{2,1,0:T(8,128)(2,1)S(1)}, bf16[4,160,384]{2,1,0:T(8,128)(2,1)S(1)}, u32[]{:S(2)}, u32[]{:S(2)}) collective-permute-start(bf16[4,160,384]{2,1,0:T(8,128)(2,1)S(1)} %bitcast.151), channel_id=1, source_target_pairs={{0,5},{1,4},{2,7},{3,6},{4,1},{5,0},{6,3},{7,2},{8,13},{9,12},{10,... | collective-permute-start | bytes 1474568 | tf_op jit(solution)/shard_map/ppermute | solution.py:577
  58.0 30.4 %collective-permute-start.8 = (bf16[4,4,160,384]{3,2,1,0:T(8,128)(2,1)S(1)}, bf16[4,4,160,384]{3,2,1,0:T(8,128)(2,1)}, u32[]{:S(2)}, u32[]{:S(2)}) collective-permute-start(bf16[4,4,160,384]{3,2,1,0:T(8,128)(2,1)S(1)} %pad_maximum_fusion.1.refs_0_), channel_id=1, source_target_pairs={{0,2},{1,3},{2,0},{3,1},{4,6},{5,7},{6,4},{7,5},{8,10},{9,11},{10,... | collective-permute-start | bytes 5898248 | tf_op jit(solution)/shard_map/ppermute | solution.py:577
  65.5 20.5 %collective-permute-start.12 = (bf16[4,5,48,384]{3,2,1,0:T(8,128)(2,1)}, bf16[4,5,48,384]{3,2,1,0:T(8,128)(2,1)S(1)}, u32[]{:S(2)}, u32[]{:S(2)}) collective-permute-start(bf16[4,5,48,384]{3,2,1,0:T(8,128)(2,1)} %get-tuple-element.206), channel_id=1, source_target_pairs={{0,1},{1,0},{2,3},{3,2},{4,5},{5,4},{6,7},{7,6},{8,9},{9,8},{10,11... | collective-permute-start | bytes 2211848 | tf_op jit(solution)/shard_map/ppermute | solution.py:577
  69.5 44.3 %collective-permute-start.10 = (bf16[256,768]{1,0:T(8,128)(2,1)}, bf16[256,768]{1,0:T(8,128)(2,1)}, u32[]{:S(2)}, u32[]{:S(2)}) collective-permute-start(bf16[256,768]{1,0:T(8,128)(2,1)} %get-tuple-element.199), channel_id=1, source_target_pairs={{0,16},{2,18},{4,20},{6,22},{8,24},{10,26},{12,28},{14,30},{16,0},... | collective-permute-start | bytes 1179656 | tf_op jit(solution)/shard_map/ppermute | solution.py:570
  70.5 54.7 %collective-permute-start.9 = (bf16[256,768]{1,0:T(8,128)(2,1)}, bf16[256,768]{1,0:T(8,128)(2,1)}, u32[]{:S(2)}, u32[]{:S(2)}) collective-permute-start(bf16[256,768]{1,0:T(8,128)(2,1)} %get-tuple-element.200), channel_id=1, source_target_pairs={{0,16},{2,18},{4,20},{6,22},{8,24},{10,26},{12,28},{14,30},{16,0},... | collective-permute-start | bytes 1179656 | tf_op jit(solution)/shard_map/ppermute | solution.py:570
  81.3 54.8 %collective-permute-start.2 = (bf16[256,768]{1,0:T(8,128)(2,1)}, bf16[256,768]{1,0:T(8,128)(2,1)}, u32[]{:S(2)}, u32[]{:S(2)}) collective-permute-start(bf16[256,768]{1,0:T(8,128)(2,1)} %get-tuple-element.201), channel_id=1, source_target_pairs={{0,16},{2,18},{4,20},{6,22},{8,24},{10,26},{12,28},{14,30},{16,0},... | collective-permute-start | bytes 1179656 | tf_op jit(solution)/shard_map/ppermute | solution.py:570
  86.0 52.2 %collective-permute-start.16 = (bf16[256,768]{1,0:T(8,128)(2,1)}, bf16[256,768]{1,0:T(8,128)(2,1)}, u32[]{:S(2)}, u32[]{:S(2)}) collective-permute-start(bf16[256,768]{1,0:T(8,128)(2,1)} %get-tuple-element.198), channel_id=1, source_target_pairs={{0,16},{2,18},{4,20},{6,22},{8,24},{10,26},{12,28},{14,30},{16,0},... | collective-permute-start | bytes 1179656 | tf_op jit(solution)/shard_map/ppermute | solution.py:570
  101.6 38.5 %collective-permute-start.14 = (bf16[2,4,5,48,384]{4,3,2,1,0:T(8,128)(2,1)S(1)}, bf16[2,4,5,48,384]{4,3,2,1,0:T(8,128)(2,1)}, u32[]{:S(2)}, u32[]{:S(2)}) collective-permute-start(bf16[2,4,5,48,384]{4,3,2,1,0:T(8,128)(2,1)S(1)} %pad_maximum_fusion.2.refs_0_), channel_id=1, source_target_pairs={{0,4},{1,5},{2,6},{3,7},{4,0},{5,1},{6,2},{7,3},{8,12},{9,13},{10,... | collective-permute-start | bytes 4423688 | tf_op jit(solution)/shard_map/ppermute | solution.py:577
  113.7 26.4 %collective-permute-start.15 = (bf16[2,4,4,48,384]{4,3,2,1,0:T(8,128)(2,1)S(1)}, bf16[2,4,4,48,384]{4,3,2,1,0:T(8,128)(2,1)}, u32[]{:S(2)}, u32[]{:S(2)}) collective-permute-start(bf16[2,4,4,48,384]{4,3,2,1,0:T(8,128)(2,1)S(1)} %copy-done.3), channel_id=1, source_target_pairs={{0,1},{1,0},{2,3},{3,2},{4,5},{5,4},{6,7},{7,6},{8,9},{9,8},{10,11... | collective-permute-start | bytes 3538952 | tf_op jit(solution)/shard_map/ppermute | solution.py:577
  140.2 18.0 %collective-permute-start.17 = (bf16[2,4,5,48,384]{4,3,2,1,0:T(8,128)(2,1)S(1)}, bf16[2,4,5,48,384]{4,3,2,1,0:T(8,128)(2,1)}, u32[]{:S(2)}, u32[]{:S(2)}) collective-permute-start(bf16[2,4,5,48,384]{4,3,2,1,0:T(8,128)(2,1)S(1)} %pad_maximum_fusion.2.refs_0_), channel_id=1, source_target_pairs={{0,2},{1,3},{2,0},{3,1},{4,6},{5,7},{6,4},{7,5},{8,10},{9,11},{10,... | collective-permute-start | bytes 4423688 | tf_op jit(solution)/shard_map/ppermute | solution.py:577
  140.7 17.5 %collective-permute-start.18 = (bf16[2,4,5,48,384]{4,3,2,1,0:T(8,128)(2,1)}, bf16[2,4,5,48,384]{4,3,2,1,0:T(8,128)(2,1)}, u32[]{:S(2)}, u32[]{:S(2)}) collective-permute-start(bf16[2,4,5,48,384]{4,3,2,1,0:T(8,128)(2,1)} %collective-permute-done.14.refs_1_), channel_id=1, source_target_pairs={{0,2},{1,3},{2,0},{3,1},{4,6},{5,7},{6,4},{7,5},{8,10},{9,11},{10,... | collective-permute-start | bytes 4423688 | tf_op jit(solution)/shard_map/ppermute | solution.py:577
  140.7 39.7 %collective-permute-start.21 = (bf16[256,768]{1,0:T(8,128)(2,1)}, bf16[256,768]{1,0:T(8,128)(2,1)}, u32[]{:S(2)}, u32[]{:S(2)}) collective-permute-start(bf16[256,768]{1,0:T(8,128)(2,1)} %get-tuple-element.197), channel_id=1, source_target_pairs={{0,16},{2,18},{4,20},{6,22},{8,24},{10,26},{12,28},{14,30},{16,0},... | collective-permute-start | bytes 1179656 | tf_op jit(solution)/shard_map/ppermute | solution.py:570
  140.7 17.5 %collective-permute-start.20 = (bf16[2,4,4,48,384]{4,3,2,1,0:T(8,128)(2,1)}, bf16[2,4,4,48,384]{4,3,2,1,0:T(8,128)(2,1)}, u32[]{:S(2)}, u32[]{:S(2)}) collective-permute-start(bf16[2,4,4,48,384]{4,3,2,1,0:T(8,128)(2,1)} %collective-permute-done.15.refs_3_), channel_id=1, source_target_pairs={{0,2},{1,3},{2,0},{3,1},{4,6},{5,7},{6,4},{7,5},{8,10},{9,11},{10,... | collective-permute-start | bytes 3538952 | tf_op jit(solution)/shard_map/ppermute | solution.py:577
  145.0 59.7 %collective-permute-start = (bf16[512,768]{1,0:T(8,128)(2,1)S(1)}, bf16[512,768]{1,0:T(8,128)(2,1)S(1)}, u32[]{:S(2)}, u32[]{:S(2)}) collective-permute-start(bf16[512,768]{1,0:T(8,128)(2,1)S(1)} %constant_dynamic-slice_fusion.6), channel_id=1, source_target_pairs={{0,16},{2,18},{4,20},{6,22},{8,24},{10,26},{12,28},{14,30},{16,0},... | collective-permute-start | bytes 2359304 | tf_op jit(solution)/shard_map/ppermute | solution.py:570
  202.7 43.3 %collective-permute-start.22 = (bf16[512,768]{1,0:T(8,128)(2,1)}, bf16[512,768]{1,0:T(8,128)(2,1)S(1)}, u32[]{:S(2)}, u32[]{:S(2)}) collective-permute-start(bf16[512,768]{1,0:T(8,128)(2,1)} %get-tuple-element.141), channel_id=1, source_target_pairs={{0,16},{2,18},{4,20},{6,22},{8,24},{10,26},{12,28},{14,30},{16,0},... | collective-permute-start | bytes 2359304 | tf_op jit(solution)/shard_map/ppermute | solution.py:570
  244.9 37.0 %collective-permute-start.23 = (bf16[512,768]{1,0:T(8,128)(2,1)}, bf16[512,768]{1,0:T(8,128)(2,1)S(1)}, u32[]{:S(2)}, u32[]{:S(2)}) collective-permute-start(bf16[512,768]{1,0:T(8,128)(2,1)} %get-tuple-element.142), channel_id=1, source_target_pairs={{0,16},{2,18},{4,20},{6,22},{8,24},{10,26},{12,28},{14,30},{16,0},... | collective-permute-start | bytes 2359304 | tf_op jit(solution)/shard_map/ppermute | solution.py:570
  302.3 36.1 %collective-permute-start.26 = (bf16[2,4,5,48,384]{4,3,2,1,0:T(8,128)(2,1)S(1)}, bf16[2,4,5,48,384]{4,3,2,1,0:T(8,128)(2,1)}, u32[]{:S(2)}, u32[]{:S(2)}) collective-permute-start(bf16[2,4,5,48,384]{4,3,2,1,0:T(8,128)(2,1)S(1)} %add_convert_fusion.refs_4_), channel_id=1, source_target_pairs={{0,4},{1,5},{2,6},{3,7},{4,0},{5,1},{6,2},{7,3},{8,12},{9,13},{10,... | collective-permute-start | bytes 4423688 | tf_op jit(solution)/shard_map/ppermute | solution.py:577
  304.4 34.0 %collective-permute-start.27 = (bf16[2,4,4,48,384]{4,3,2,1,0:T(8,128)(2,1)S(1)}, bf16[2,4,4,48,384]{4,3,2,1,0:T(8,128)(2,1)}, u32[]{:S(2)}, u32[]{:S(2)}) collective-permute-start(bf16[2,4,4,48,384]{4,3,2,1,0:T(8,128)(2,1)S(1)} %add_convert_fusion.1.refs_5_), channel_id=1, source_target_pairs={{0,1},{1,0},{2,3},{3,2},{4,5},{5,4},{6,7},{7,6},{8,9},{9,8},{10,11... | collective-permute-start | bytes 3538952 | tf_op jit(solution)/shard_map/ppermute | solution.py:577
  305.0 40.0 %collective-permute-start.28 = (bf16[256,768]{1,0:T(8,128)(2,1)}, bf16[256,768]{1,0:T(8,128)(2,1)S(1)}, u32[]{:S(2)}, u32[]{:S(2)}) collective-permute-start(bf16[256,768]{1,0:T(8,128)(2,1)} %get-tuple-element.171), channel_id=1, source_target_pairs={{0,16},{2,18},{4,20},{6,22},{8,24},{10,26},{12,28},{14,30},{16,0},... | collective-permute-start | bytes 1179656 | tf_op jit(solution)/shard_map/ppermute | solution.py:570
  320.6 48.3 %collective-permute-start.29 = (bf16[256,768]{1,0:T(8,128)(2,1)}, bf16[256,768]{1,0:T(8,128)(2,1)S(1)}, u32[]{:S(2)}, u32[]{:S(2)}) collective-permute-start(bf16[256,768]{1,0:T(8,128)(2,1)} %get-tuple-element.173), channel_id=1, source_target_pairs={{0,16},{2,18},{4,20},{6,22},{8,24},{10,26},{12,28},{14,30},{16,0},... | collective-permute-start | bytes 1179656 | tf_op jit(solution)/shard_map/ppermute | solution.py:570
  337.8 45.2 %collective-permute-start.30 = (bf16[256,768]{1,0:T(8,128)(2,1)}, bf16[256,768]{1,0:T(8,128)(2,1)}, u32[]{:S(2)}, u32[]{:S(2)}) collective-permute-start(bf16[256,768]{1,0:T(8,128)(2,1)} %get-tuple-element.174), channel_id=1, source_target_pairs={{0,16},{2,18},{4,20},{6,22},{8,24},{10,26},{12,28},{14,30},{16,0},... | collective-permute-start | bytes 1179656 | tf_op jit(solution)/shard_map/ppermute | solution.py:570
  340.1 23.3 %collective-permute-start.33 = (bf16[4,4,48,384]{3,2,1,0:T(8,128)(2,1)S(1)}, bf16[4,4,48,384]{3,2,1,0:T(8,128)(2,1)}, u32[]{:S(2)}, u32[]{:S(2)}) collective-permute-start(bf16[4,4,48,384]{3,2,1,0:T(8,128)(2,1)S(1)} %fusion.7.refs_5_), channel_id=1, source_target_pairs={{0,4},{1,5},{2,6},{3,7},{4,0},{5,1},{6,2},{7,3},{8,12},{9,13},{10,... | collective-permute-start | bytes 1769480 | tf_op jit(solution)/shard_map/ppermute | solution.py:577
  343.5 19.9 %collective-permute-start.32 = (bf16[4,5,48,384]{3,2,1,0:T(8,128)(2,1)S(1)}, bf16[4,5,48,384]{3,2,1,0:T(8,128)(2,1)S(1)}, u32[]{:S(2)}, u32[]{:S(2)}) collective-permute-start(bf16[4,5,48,384]{3,2,1,0:T(8,128)(2,1)S(1)} %fusion.6.refs_4_), channel_id=1, source_target_pairs={{0,1},{1,0},{2,3},{3,2},{4,5},{5,4},{6,7},{7,6},{8,9},{9,8},{10,11... | collective-permute-start | bytes 2211848 | tf_op jit(solution)/shard_map/ppermute | solution.py:577
  386.3 20.9 %collective-permute-start.31 = (bf16[256,768]{1,0:T(8,128)(2,1)S(1)}, bf16[256,768]{1,0:T(8,128)(2,1)S(1)}, u32[]{:S(2)}, u32[]{:S(2)}) collective-permute-start(bf16[256,768]{1,0:T(8,128)(2,1)S(1)} %copy-done.31), channel_id=1, source_target_pairs={{0,16},{2,18},{4,20},{6,22},{8,24},{10,26},{12,28},{14,30},{16,0},... | collective-permute-start | bytes 1179656 | tf_op jit(solution)/shard_map/ppermute | solution.py:570
  390.7 23.7 %collective-permute-start.40 = (bf16[2,1,9,48,384]{4,3,2,1,0:T(8,128)(2,1)S(1)}, bf16[2,1,9,48,384]{4,3,2,1,0:T(8,128)(2,1)S(1)}, u32[]{:S(2)}, u32[]{:S(2)}) collective-permute-start(bf16[2,1,9,48,384]{4,3,2,1,0:T(8,128)(2,1)S(1)} %dynamic-slice_convert_fusion), channel_id=1, source_target_pairs={{0,8},{2,10},{4,12},{6,14},{8,0},{10,2},{12,4},{14,6},{16,24},{18,... | collective-permute-start | bytes 1990664 | tf_op jit(solution)/shard_map/ppermute | solution.py:570
  395.2 21.9 %collective-permute-start.35 = (bf16[4,160,384]{2,1,0:T(8,128)(2,1)S(1)}, bf16[4,160,384]{2,1,0:T(8,128)(2,1)S(1)}, u32[]{:S(2)}, u32[]{:S(2)}) collective-permute-start(bf16[4,160,384]{2,1,0:T(8,128)(2,1)S(1)} %get-tuple-element.191), channel_id=1, source_target_pairs={{0,1},{1,0},{2,3},{3,2},{4,5},{5,4},{6,7},{7,6},{8,9},{9,8},{10,11... | collective-permute-start | bytes 1474568 | tf_op jit(solution)/shard_map/ppermute | solution.py:577
  395.8 23.3 %collective-permute-start.36 = (bf16[4,160,384]{2,1,0:T(8,128)(2,1)S(1)}, bf16[4,160,384]{2,1,0:T(8,128)(2,1)S(1)}, u32[]{:S(2)}, u32[]{:S(2)}) collective-permute-start(bf16[4,160,384]{2,1,0:T(8,128)(2,1)S(1)} %get-tuple-element.192), channel_id=1, source_target_pairs={{0,4},{1,5},{2,6},{3,7},{4,0},{5,1},{6,2},{7,3},{8,12},{9,13},{10,... | collective-permute-start | bytes 1474568 | tf_op jit(solution)/shard_map/ppermute | solution.py:577
  396.3 22.8 %collective-permute-start.37 = (bf16[4,160,384]{2,1,0:T(8,128)(2,1)S(1)}, bf16[4,160,384]{2,1,0:T(8,128)(2,1)S(1)}, u32[]{:S(2)}, u32[]{:S(2)}) collective-permute-start(bf16[4,160,384]{2,1,0:T(8,128)(2,1)S(1)} %get-tuple-element.193), channel_id=1, source_target_pairs={{0,5},{1,4},{2,7},{3,6},{4,1},{5,0},{6,3},{7,2},{8,13},{9,12},{10,... | collective-permute-start | bytes 1474568 | tf_op jit(solution)/shard_map/ppermute | solution.py:577
  414.6 17.5 %collective-permute-start.41 = (bf16[1,1,9,48,384]{4,3,2,1,0:T(8,128)(2,1)S(1)}, bf16[1,1,9,48,384]{4,3,2,1,0:T(8,128)(2,1)S(1)}, u32[]{:S(2)}, u32[]{:S(2)}) collective-permute-start(bf16[1,1,9,48,384]{4,3,2,1,0:T(8,128)(2,1)S(1)} %dynamic-slice_convert_fusion.1), channel_id=1, source_target_pairs={{0,16},{2,18},{4,20},{6,22},{8,24},{10,26},{12,28},{14,30},{16,0},... | collective-permute-start | bytes 995336 | tf_op jit(solution)/shard_map/ppermute | solution.py:570
  (42 other events, 385.1 us)

commit v3 on v2

--- a/solution.py
+++ b/solution.py
@@ -12,7 +12,6 @@
 SLOTS = 64
 CHUNKS = 4
 X_UNITS = (1, 1, 1, 1)
-ATTENDS_BEFORE = (0, 2)
 FEED_UNITS = (1, 1, 2)
 Y_UNITS = (2, 2)
 BACK_UNITS = (1, 1, 1, 1)
@@ -20,6 +19,7 @@
 BLOCKS = 4
 EPS = 1e-05
 NEG = -1000000000.0
+SCALE = HEAD_DIM**-0.5
 LIMIT = 60 * 2**20
 F32 = jnp.float32
 BF = jnp.bfloat16
@@ -90,21 +90,25 @@
     start = pl.multiple_of(where[3] + c * h, h)
     copy(rows.at[pl.ds(start, h)], xs.at[pl.ds(0, h)], sems.at[0])
     copy(far.at[pl.ds(skip * h, h)], xs.at[pl.ds(h, h)], sems.at[0])
-    pull(where, views, pl.ds(0, wqkv.shape[2]), wqkv, sems.at[1])
+    halves = wqkv.shape[0] // 2
+    for i in (0, 1):
+        some = [(piece.at[pl.ds(i * halves, halves)], bits) for piece, bits in views]
+        pull(where, some, pl.ds(0, wqkv.shape[2]), wqkv.at[pl.ds(i * halves, halves)], sems.at[(1, 6)[i]])
     wait_for(xs, sems.at[0])
     span = pl.ds(c * r, r)
     copy(xs, x_all.at[span], sems.at[2])
-    wait_for(wqkv, sems.at[1])
     flat = wqkv.reshape(3 * width, width)
     x = xs[...]
-    for part in range(3):
-        cols = slice(part * width, (part + 1) * width)
+    middle = width // 2
+    for part in range(2):
+        cols = slice(3 * part * middle, 3 * (part + 1) * middle)
+        wait_for(wqkv.at[pl.ds(part * halves, halves)], sems.at[(1, 6)[part]])
         acc = nt(x, flat[cols, :])
         if part == 0:
-            acc = acc + vec[0:1, :]
-        if part == 2:
-            acc = acc + vec[1:2, :]
-        qkv[:, cols] = acc.astype(BF)
+            bias = jnp.concatenate([vec[0:1, :], jnp.zeros((1, middle), F32)], 1)
+        else:
+            bias = jnp.concatenate([jnp.zeros((1, middle), F32), vec[1:2, :]], 1)
+        qkv[:, cols] = (acc + bias).astype(BF)
     copy(qkv, qkv_all.at[span], sems.at[3])
     lane = lax.broadcasted_iota(jnp.int32, (2 * SLOTS, 2 * HEAD_DIM), 1)
     low_half = lane < HEAD_DIM
@@ -125,11 +129,11 @@
             zero = jnp.zeros_like(k)
             k2 = jnp.concatenate([jnp.where(low_half, k, zero), jnp.where(low_half, zero, k)], 0)
             v2 = jnp.concatenate([jnp.where(low_half, v, zero), jnp.where(low_half, zero, v)], 0)
-            score = jnp.where(valid, nt(q, k2) * (HEAD_DIM**-0.5), NEG)
+            score = jnp.where(valid, nt(q * SCALE, k2), NEG)
             halves = []
             for one in (score[:, : 2 * SLOTS], score[:, 2 * SLOTS :]):
                 e = jnp.exp(one - jnp.max(one, -1, keepdims=True))
-                halves.append((e / jnp.sum(e, -1, keepdims=True)).astype(BF))
+                halves.append((e * (1.0 / jnp.sum(e, -1, keepdims=True))).astype(BF))
             both = jnp.concatenate(halves, 1)
             prob[s, p] = both
             o = nn(both, v2).astype(BF)
@@ -139,7 +143,7 @@
         copy(prob.at[s], prob_all.at[at], sems.at[4])
         return carry
 
-    lax.fori_loop(0, seqs, seq, 0)
+    lax.fori_loop(0, seqs, seq, 0, unroll=2)
     copy(mixed, mixed_all.at[span], sems.at[5])
     wait_for(xs, sems.at[2])
     wait_for(qkv, sems.at[3])
@@ -172,7 +176,7 @@
             pltpu.VMEM((r, 3 * width), BF),
             pltpu.VMEM((seqs,) + shapes[1].shape[1:], BF),
             pltpu.VMEM((r, width), BF),
-            DMA((6,)),
+            DMA((7,)),
         ],
         compiler_params=pltpu.CompilerParams(vmem_limit_bytes=LIMIT),
         cost_estimate=SLOW,
@@ -196,12 +200,21 @@
     outs, sums, refs = refs[:8], refs[8:10], refs[10:]
     y_all, act_all, dinner_all, first_all, dout_all, dbranch_all, dmix_all, y_far = outs
     vsum, bsum = sums
-    wout, wup, wdown, xs, mixed, gs, ys, act, slope, dinner, first, dout, dbranch, dmix, acc, n1, sems = refs
-    r, width = xs.shape
+    wout, wup, wdown, xs_all, mixed_in, gs_all, ys, act, slope, dinner, first, dout, dbranch, dmix, acc, n1, sems = refs
+    r, width = ys.shape
     h = r // 2
-    pull(where, first_views, pl.ds(0, 1), wout, sems.at[0])
-    pull(where, first_views, pl.ds(1, BLOCKS), wup, sems.at[1])
-    pull(where, second_views, pl.ds(0, BLOCKS), wdown, sems.at[2])
+    for t in range(subs):
+        span = pl.ds((c0 + t) * r, r)
+        start = pl.multiple_of(where[3] + (c0 + t) * h, h)
+        copy(x_all.at[span], xs_all.at[t], sems.at[3, t])
+        copy(mixed_all.at[span], mixed_in.at[t], sems.at[3, t])
+        if t == 0:
+            pull(where, first_views, pl.ds(0, 1), wout, sems.at[0, 0])
+            pull(where, first_views, pl.ds(1, BLOCKS), wup, sems.at[1, 0])
+        copy(grads.at[pl.ds(start, h)], gs_all.at[t, pl.ds(0, h)], sems.at[4, t])
+        copy(far.at[pl.ds(t * h, h)], gs_all.at[t, pl.ds(h, h)], sems.at[4, t])
+        if t == 0:
+            pull(where, second_views, pl.ds(0, BLOCKS), wdown, sems.at[2, 0])
     out_flat = wout.reshape(width, width)
     ff = BLOCKS * width
     up_flat = wup.reshape(ff, width)
@@ -218,52 +231,46 @@
         c = c0 + t
         span = pl.ds(c * r, r)
         start = pl.multiple_of(where[3] + c * h, h)
-        ins = (
-            pltpu.make_async_copy(x_all.at[span], xs, sems.at[3]),
-            pltpu.make_async_copy(mixed_all.at[span], mixed, sems.at[3]),
-            pltpu.make_async_copy(grads.at[pl.ds(start, h)], gs.at[pl.ds(0, h)], sems.at[4]),
-            pltpu.make_async_copy(far.at[pl.ds(t * h, h)], gs.at[pl.ds(h, h)], sems.at[4]),
-        )
-        for one in ins:
-            one.start()
-        wait_for(xs, sems.at[3])
-        wait_for(mixed, sems.at[3])
+        xs, mixed, gs = xs_all.at[t], mixed_in.at[t], gs_all.at[t]
+        wait_for(xs, sems.at[3, t])
+        wait_for(mixed, sems.at[3, t])
         if t == 0:
-            wait_for(wout, sems.at[0])
+            wait_for(wout, sems.at[0, 0])
         sum1 = xs[...].astype(F32) + nt(mixed[...], out_flat[...]) + vec[2:3, :]
         hat, r1 = normed(sum1)
         n1[...] = hat
         top = hat * vec[4:5, :] + vec[5:6, :]
         if t:
             for ref in (act, dinner, first, dout, dbranch, dmix, ys):
-                wait_for(ref, sems.at[5])
+                wait_for(ref, sems.at[5, 0])
         first[...] = top.astype(BF)
-        copy(first, first_all.at[span], sems.at[5])
+        copy(first, first_all.at[span], sems.at[5, 0])
         acc[...] = top + vec[3:4, :]
         if t == 0:
-            wait_for(wup, sems.at[1])
-            wait_for(wdown, sems.at[2])
+            wait_for(wup, sems.at[1, 0])
         for b in range(BLOCKS):
             cols = slice(b * width, (b + 1) * width)
             inner = nt(first[...], up_block(b)) + bup[b : b + 1, :]
             phi = 0.5 + 0.5 * lax.erf(inner * (2**-0.5))
             low = (inner * phi).astype(BF)
             act[:, cols] = low
-            copy(act.at[:, cols], act_all.at[span, cols], sems.at[5])
+            copy(act.at[:, cols], act_all.at[span, cols], sems.at[5, 0])
             slope[:, cols] = (phi + inner * (jnp.exp(-0.5 * inner * inner) * 0.3989422804014327)).astype(BF)
+            if t == 0 and b == 0:
+                wait_for(wdown, sems.at[2, 0])
             acc[...] += nt(low, down_block(b))
         n2, r2 = normed(acc[...])
         ys[...] = (n2 * vec[6:7, :] + vec[7:8, :]).astype(BF)
-        copy(ys.at[pl.ds(0, h)], y_all.at[pl.ds(start, h)], sems.at[5])
-        copy(ys.at[pl.ds(h, h)], y_far.at[pl.ds((skip + t) * h, h)], sems.at[5])
-        wait_for(gs, sems.at[4])
+        copy(ys.at[pl.ds(0, h)], y_all.at[pl.ds(start, h)], sems.at[5, 0])
+        copy(ys.at[pl.ds(h, h)], y_far.at[pl.ds((skip + t) * h, h)], sems.at[5, 0])
+        wait_for(gs, sems.at[4, t])
         g = gs[...].astype(F32)
         sums_of = [None] * 6
         sums_of[4] = colsum(g * n2)
         sums_of[5] = colsum(g)
         dz2 = norm_back(g * vec[6:7, :], n2, r2)
         dout[...] = dz2.astype(BF)
-        copy(dout, dout_all.at[span], sems.at[5])
+        copy(dout, dout_all.at[span], sems.at[5, 0])
         sums_of[1] = colsum(dz2)
         acc[...] = dz2
         for b in range(BLOCKS):
@@ -273,7 +280,7 @@
             bsum[0:1, cols] = part if t == 0 else bsum[0:1, cols] + part
             low = grad.astype(BF)
             dinner[:, cols] = low
-            copy(dinner.at[:, cols], dinner_all.at[span, cols], sems.at[5])
+            copy(dinner.at[:, cols], dinner_all.at[span, cols], sems.at[5, 0])
             acc[...] += nn(low, up_block(b))
         d = acc[...]
         hat = n1[...]
@@ -283,13 +290,13 @@
         sums_of[0] = colsum(dz1)
         low = dz1.astype(BF)
         dbranch[...] = low
-        copy(dbranch, dbranch_all.at[span], sems.at[5])
+        copy(dbranch, dbranch_all.at[span], sems.at[5, 0])
         dmix[...] = nn(low, out_flat[...]).astype(BF)
-        copy(dmix, dmix_all.at[span], sems.at[5])
+        copy(dmix, dmix_all.at[span], sems.at[5, 0])
         for i, part in enumerate(sums_of):
             vsum[i : i + 1, :] = part if t == 0 else vsum[i : i + 1, :] + part
     for ref in (act, dinner, first, dout, dbranch, dmix, ys):
-        wait_for(ref, sems.at[5])
+        wait_for(ref, sems.at[5, 0])
 
 
 def feed(c0, subs, skip, y_rows, sides, where, grads, far, x_all, mixed_all, vec, bup, pieces, before, tokens):
@@ -316,9 +323,9 @@
             pltpu.VMEM((groups, 4, 1, thin, width), BF),
             pltpu.VMEM((groups, 4, BLOCKS, thin, width), BF),
             pltpu.VMEM((groups, 4, BLOCKS, thin, width), BF),
-            pltpu.VMEM((r, width), BF),
-            pltpu.VMEM((r, width), BF),
-            pltpu.VMEM((r, width), BF),
+            pltpu.VMEM((subs, r, width), BF),
+            pltpu.VMEM((subs, r, width), BF),
+            pltpu.VMEM((subs, r, width), BF),
             pltpu.VMEM((r, width), BF),
             pltpu.VMEM((r, ff), BF),
             pltpu.VMEM((r, ff), BF),
@@ -329,7 +336,7 @@
             pltpu.VMEM((r, width), BF),
             pltpu.VMEM((r, width), F32),
             pltpu.VMEM((r, width), F32),
-            DMA((6,)),
+            DMA((6, subs)),
         ],
         compiler_params=pltpu.CompilerParams(vmem_limit_bytes=LIMIT),
         cost_estimate=QUICK,
@@ -338,21 +345,23 @@
 
 
 def back_kernel(c0, skip, where, qkv_all, prob_all, dbranch_all, dmix_all, *refs):
-    views, refs = proj_views(refs[:2]), refs[-13:]
-    dx_all, dqkv_all, dx_far, vsum, wqkv, qkv, prob, dbranch, dmix, dqkv, dxs, dxf, sems = refs
+    views, refs = proj_views(refs[:2]), refs[-14:]
+    dx_all, dqkv_all, dx_far, vsum, wqkv, qkv, prob, dbranch, dmix, dqkv, dxs, dxf, sems, seq_sems = refs
     r, width = dbranch.shape
     h = dx_all.shape[0] // (2 * CHUNKS)
     subs = r // (2 * h)
     seqs = h // SLOTS
     span = pl.ds(c0 * 2 * h, r)
-    copy(qkv_all.at[span], qkv, sems.at[0])
-    copy(dmix_all.at[span], dmix, sems.at[1])
-    copy(prob_all.at[pl.ds(c0 * seqs, subs * seqs)], prob, sems.at[2])
+    for t in range(subs):
+        for s in range(seqs):
+            sem = seq_sems.at[t * seqs + s]
+            for at in (2 * h * t + s * SLOTS, 2 * h * t + h + s * SLOTS):
+                rows, there = pl.ds(at, SLOTS), pl.ds(c0 * 2 * h + at, SLOTS)
+                copy(qkv_all.at[there], qkv.at[rows], sem)
+                copy(dmix_all.at[there], dmix.at[rows], sem)
+            copy(prob_all.at[(c0 + t) * seqs + s], prob.at[t * seqs + s], sem)
     pull(where, views, pl.ds(0, wqkv.shape[2]), wqkv, sems.at[3])
     copy(dbranch_all.at[span], dbranch, sems.at[4])
-    wait_for(qkv, sems.at[0])
-    wait_for(dmix, sems.at[1])
-    wait_for(prob, sems.at[2])
     lane = lax.broadcasted_iota(jnp.int32, (2 * SLOTS, 2 * HEAD_DIM), 1)
     low_half = lane < HEAD_DIM
 
@@ -379,9 +388,8 @@
                 w = wide[:, cols] * dp[:, cols]
                 halves.append((w - wide[:, cols] * jnp.sum(w, -1, keepdims=True)).astype(BF))
             ds = jnp.concatenate(halves, 1)
-            scale = HEAD_DIM**-0.5
-            dq = nn(ds, k2) * scale
-            dk = tn(ds, q) * scale
+            dq = nn(ds, k2 * SCALE)
+            dk = tn(ds, q * SCALE)
             dv = tn(both, do)
             dk = jnp.where(low_half, dk[: 2 * SLOTS], dk[2 * SLOTS :])
             dv = jnp.where(low_half, dv[: 2 * SLOTS], dv[2 * SLOTS :])
@@ -395,6 +403,10 @@
         chunk = pl.ds(t * 2 * h, 2 * h)
 
         def step(s, carry, t=t):
+            sem = seq_sems.at[t * seqs + s]
+            wait_for(qkv.at[pl.ds(0, 2 * SLOTS)], sem)
+            wait_for(dmix.at[pl.ds(0, 2 * SLOTS)], sem)
+            wait_for(prob.at[0], sem)
             seq(t, s)
             return carry
 
@@ -440,6 +452,7 @@
             pltpu.VMEM((h, width), F32),
             pltpu.VMEM((h, width), BF),
             DMA((8,)),
+            DMA((seqs,)),
         ],
         compiler_params=pltpu.CompilerParams(vmem_limit_bytes=LIMIT),
         cost_estimate=QUICK,
@@ -612,10 +625,9 @@
     one, two = held[:, :first], held[:, first:]
     one = jnp.stack([one, across(one, 0, 0, 1)])
     two = jnp.stack([two, across(two, 0, 1, 0)])
-    (one, two), early = lax.optimization_barrier(((one, two), (yield)))
     near = [one, across(one, 0, 1, 0), two, across(two, 0, 0, 1)]
     near, late = lax.optimization_barrier((near, (yield)))
-    yield near + [across(piece, 1, 0, 0) for piece in near], early[:1] + late[:1]
+    yield near + [across(piece, 1, 0, 0) for piece in near], late[:1]
 
 
 def low(values):
@@ -632,8 +644,35 @@
     ready = after([low(wide(keep[i]) + wide(came[i])) for i in (1, 2, 3)], gate_one)
     for part, (dy, dx) in zip(ready, ((0, 1), (1, 0), (1, 1))):
         held = held + wide(across(part, 0, dy, dx))
-    *_, (held,) = reduce_far(after(held, gate_two))
-    return held
+    held = after(held, gate_two)
+    for bit in range(bits_of("pair") - 2, -1, -1):
+        held, _ = halved(held, "pair", bit, held.ndim - 1)
+    depth = bits_of("mod") - 2
+    rest = held.shape[1:]
+    held = held.reshape((2,) * depth + rest)
+    for bit in range(2, bits_of("mod") - 2):
+        held, _ = halved(held, "mod", bit, depth - 1 - (bit - 2))
+    held = held.reshape((2, 2) + rest)
+    top = bits_of("mod") - 1
+    upper, inner = bit_at("mod", top), bit_at("mod", top - 1)
+
+    def slab(u, v):
+        part = lax.dynamic_index_in_dim(held, upper ^ u, 0, keepdims=False)
+        return lax.dynamic_index_in_dim(part, inner ^ v, 0, keepdims=False)
+
+    total = slab(0, 0)
+    for u, v in ((1, 0), (1, 1), (0, 1)):
+        total = total + wide(swapped(low(slab(u, v)), "mod", (u << top) | (v << (top - 1))))
+    return total
+
+
+def halved(held, axis, bit, dim):
+    size = held.shape[dim] // 2
+    mine = bit_at(axis, bit)
+    away = low(lax.dynamic_slice_in_dim(held, (1 - mine) * size, size, dim))
+    stay = lax.dynamic_slice_in_dim(held, mine * size, size, dim)
+    got = swapped(away, axis, 1 << bit)
+    return stay + wide(got), got
 
 
 def reduce_wide(keep_one, send_one, keep_two, send_two):
@@ -658,21 +697,14 @@
 
 
 def reduce_far(held):
-    def halved(held, axis, bit, dim):
-        size = held.shape[dim] // 2
-        mine = bit_at(axis, bit)
-        away = low(lax.dynamic_slice_in_dim(held, (1 - mine) * size, size, dim))
-        stay = lax.dynamic_slice_in_dim(held, mine * size, size, dim)
-        return stay + wide(swapped(away, axis, 1 << bit))
-
     for bit in range(bits_of("pair") - 2, -1, -1):
-        held = halved(held, "pair", bit, held.ndim - 1)
+        held, got = halved(held, "pair", bit, held.ndim - 1)
     depth = bits_of("mod") - 2
     rest = held.shape[1:]
     held = held.reshape((2,) * depth + rest)
     for bit in range(2, bits_of("mod")):
-        held = halved(held, "mod", bit, depth - 1 - (bit - 2))
-        yield [held.reshape((-1,) + rest)]
+        held, got = halved(held, "mod", bit, depth - 1 - (bit - 2))
+        yield [held.reshape((-1,) + rest), got]
 
 
 def settle(pieces, row, rows):
@@ -704,9 +736,10 @@
     def units(sizes):
         return [(sum(sizes[:i]), size) for i, size in enumerate(sizes)]
 
-    def over_units(array, sizes):
+    def over_units(array, sizes, gate):
         return [
-            over(lax.dynamic_slice_in_dim(array, away_start + c * chunk, n * chunk)) for c, n in units(sizes)
+            over(after(lax.dynamic_slice_in_dim(array, away_start + c * chunk, n * chunk), gate))
+            for c, n in units(sizes)
         ]
 
     line = w_qkv.shape[0]
@@ -731,10 +764,13 @@
     live = jnp.stack([live_own, parcel[first_rows.shape[0] + tall, : moved // SLOTS].astype(jnp.int32)])
 
     proj = gather_proj(proj_slab)
-    far_rows = [parcel] + over_units(rows_input, X_UNITS)[1:]
+    far_rows = [parcel]
+    for c, n in units(X_UNITS)[1:]:
+        part = lax.dynamic_slice_in_dim(rows_input, away_start + c * chunk, n * chunk)
+        far_rows.append(over(after(part, far_rows[1:2])))
     wide_steps = gather_wide(slab, came, 1 + BLOCKS)
     next(wide_steps)
-    far_grads = over_units(grad_out, FEED_UNITS)
+    far_grads = over_units(grad_out, FEED_UNITS, far_rows[1:2])
 
     tiny = settle(proj, per, small_rows).reshape(mods, small_rows, pairs, line)
     tiny = tiny.transpose(2, 0, 1, 3).reshape(pairs, mods, -1)
@@ -748,9 +784,8 @@
     for (c0, n), far in zip(units(X_UNITS), far_rows):
         for i in range(n):
             *kept, done = attend(c0 + i, i, where, live, rows_input, far, vec, proj, kept, [])
-            if c0 + i in ATTENDS_BEFORE:
-                arrived = far_rows[3:] + far_grads[:1] if c0 + i else []
-                gathered = wide_steps.send([done] + arrived)
+            if c0 + i == CHUNKS - 2:
+                gathered = wide_steps.send([done] + far_rows[3:] + far_grads[:1])
     wide_pieces, gates = gathered
     qkv_all, prob_all, mixed_all, x_all = kept
     fed, back_rows = (), []
@@ -781,7 +816,7 @@
         if c0 in (1, 3):
             tokens = wide_steps.send(done)
         if c0 == 3:
-            tokens = tokens + back_grads[:1]
+            tokens = tokens + back_grads[:2]
         out = back(
             c0, n, c0 - d0, size * chunk, where, rows, qkv_all, prob_all, dbranch_all, dmix_all, proj, backed, tokens
         )
@@ -797,10 +832,10 @@
     tiny_grad = jnp.concatenate(tiny_grad, -1)
     tiny_grad = jnp.pad(tiny_grad, ((0, 0), (0, 0), (0, 16 * line - small_size(vectors, b_up))))
     tiny_grad = tiny_grad.reshape(mods, pairs, 16, line).transpose(0, 2, 1, 3).reshape(mods, 16, width).astype(BF)
-    tokens = wide_steps.send(done) + back_grads[1:2]
+    tokens = wide_steps.send(done)
     proj_pair = proj_grads(where, dqkv_all, x_all, tiny_grad, groups, tokens)
     *gates, g_wide = wide_steps
-    g_proj = reduce_proj(*after(proj_pair, back_grads[2:3] + gates[0]), [], g_wide)[0]
+    g_proj = reduce_proj(*after(proj_pair, back_grads[2:3] + gates[0][1:]), [], g_wide[1:])
     g_wide = g_wide[0][0]
 
     for (c0, n), part in zip(units(Y_UNITS), back_rows):

time: 450 us -> 428 us (0.951)
  Pallas kernels: 234 us -> 217 us
  waiting for transfers between devices: 104 us -> 95.4 us
    ppermute x22, waiting for transfers between devices: 20 us -> 10.9 us  [across(): lax.ppermute(values, ('mod', 'pair'), [(i, i ^ mask) for i in range(count)])]
    pallas_call x3, Pallas kernels: 83.8 us -> 75.8 us  [feed(): pl.pallas_call(functools.partial(feed_kernel, c0, subs, skip, sides), out...]
    pallas_call x4, Pallas kernels: 44.2 us -> 39 us  [attend(): pl.pallas_call(functools.partial(attend_kernel, c, skip), out_shape=shape...]
    ppermute x20 -> x21, starting transfers between devices: 26.9 us -> 29.6 us  [swapped(): lax.ppermute(values, axis, [(i, i ^ mask) for i in range(lax.axis_size(ax...]
    ppermute x20 -> x21, waiting for transfers between devices: 83.8 us -> 84.5 us  [swapped(): lax.ppermute(values, axis, [(i, i ^ mask) for i in range(lax.axis_size(ax...]
  transfers between devices with their start and end apart: 42 -> 43, of which waited for: 17 -> 16; matrix products, arithmetic and copies ran while one was open for 10% -> 11% of each run, Pallas kernels for 53% -> 51%
where the time goes in v3:
time: 428 us; the launch traced here: 422 us
  Pallas kernels  217 us (51%)
  waiting for transfers between devices  95.4 us (22%)
  starting transfers between devices  49 us (11%)
  local copies, waits for them, and re-layouts  29.9 us (7%)
  other arithmetic  29.4 us (7%)
    ppermute x21, waiting for transfers between devices, swapped(): lax.ppermute(values, axis, [(i, i ^ mask) for i in range(lax.axis_size(ax...  84.5 us
    pallas_call x3, Pallas kernels, feed(): pl.pallas_call(functools.partial(feed_kernel, c0, subs, skip, sides), out...  75.8 us
    pallas_call x4, Pallas kernels, back(): pl.pallas_call(functools.partial(back_kernel, c0, skip), out_shape=(S((ro...  55 us
    pallas_call x4, Pallas kernels, attend(): pl.pallas_call(functools.partial(attend_kernel, c, skip), out_shape=shape...  39 us
    pallas_call x1, Pallas kernels, wide_grads(): pl.pallas_call(functools.partial(wide_grads_kernel, sides), grid=(BLOCKS,...  33.6 us
    ppermute x21, starting transfers between devices, swapped(): lax.ppermute(values, axis, [(i, i ^ mask) for i in range(lax.axis_size(ax...  29.6 us
    ppermute x22, starting transfers between devices, across(): lax.ppermute(values, ('mod', 'pair'), [(i, i ^ mask) for i in range(count)])  19.5 us
    pallas_call x1, Pallas kernels, proj_grads(): pl.pallas_call(proj_grads_kernel, grid=(2,), out_shape=(S(shape, BF),) *...  13.4 us
  transfers between devices with their start and end apart: 43, of which 16 were waited for; matrix products, arithmetic and copies ran while one was open for 11% of the time, Pallas kernels for 51%

profile of v3, /device:TPU:0, one launch (start us, length us, event | category | flops | bytes accessed | tf_op | source)
XLA Modules:
  0.0 422.3 jit_solution(18248063411820192799)
XLA Ops:
  3.2 4.1 collective-permute-start.4
  10.0 2.4 constant_dynamic-slice_fusion.2
  14.7 19.3 %collective-permute-done.5 = bf16[2,160,384]{2,1,0:T(8,128)(2,1)S(1)} collective-permute-done((bf16[2,160,384]{2,1,0:T(8,128)(2,1)S(1)}, bf16[2,160,384]{2,1,0:T(8,128)(2,1)S(1)}, u32[]{:S(2)}, u32[]{:S(2)}) %collective-permute-start.5) | collective-permute-done | bytes 245792 | tf_op jit(solution)/shard_map/ppermute | solution.py:583
  37.7 10.1 %collective-permute-done.2.far = bf16[488,768]{1,0:T(8,128)(2,1)S(1)} collective-permute-done((bf16[488,768]{1,0:T(8,128)(2,1)S(1)}, bf16[488,768]{1,0:T(8,128)(2,1)S(1)}, u32[]{:S(2)}, u32[]{:S(2)}) %collective-permute-start.2) | collective-permute-done | bytes 749600 | tf_op jit(solution)/shard_map/ppermute | solution.py:583
  48.4 9.4 %collective-permute-done.7 = bf16[4,160,384]{2,1,0:T(8,128)(2,1)S(1)} collective-permute-done((bf16[4,160,384]{2,1,0:T(8,128)(2,1)S(1)}, bf16[4,160,384]{2,1,0:T(8,128)(2,1)S(1)}, u32[]{:S(2)}, u32[]{:S(2)}) %collective-permute-start.7) | collective-permute-done | bytes 491552 | tf_op jit(solution)/shard_map/ppermute | solution.py:590
  58.1 4.7 %collective-permute-start = (bf16[256,768]{1,0:T(8,128)(2,1)}, bf16[256,768]{1,0:T(8,128)(2,1)}, u32[]{:S(2)}, u32[]{:S(2)}) collective-permute-start(bf16[256,768]{1,0:T(8,128)(2,1)} %get-tuple-element.206), channel_id=1, source_target_pairs={{0,16},{2,18},{4,20},{6,22},{8,24},{10,26},{12,28},{14,30},{16,0},... | collective-permute-start | bytes 1179656 | tf_op jit(solution)/shard_map/ppermute | solution.py:583
  67.9 2.5 collective-permute-start.14
  73.1 8.2 %collective-permute-done.far = bf16[256,768]{1,0:T(8,128)(2,1)} collective-permute-done((bf16[256,768]{1,0:T(8,128)(2,1)}, bf16[256,768]{1,0:T(8,128)(2,1)}, u32[]{:S(2)}, u32[]{:S(2)}) %collective-permute-start) | collective-permute-done | bytes 393248 | tf_op jit(solution)/shard_map/ppermute | solution.py:583
  81.3 2.9 collective-permute-start.3
  93.8 9.8 %attend.4 = (bf16[2048,2304]{1,0:T(8,128)(2,1)}, bf16[16,6,128,256]{3,2,1,0:T(8,128)(2,1)}, bf16[2048,768]{1,0:T(8,128)(2,1)}, bf16[2048,768]{1,0:T(8,128)(2,1)}, f32[8,128]{1,0:T(8,128)}) custom-call(s32[4]{0:T(128)} %pad_add_fusion.1.where, s32[2,16]{1,0:T(2,128)} %pad_add_fusion.live, bf16[2048,768]{1,0:T(8,128)(2,1)} %rows.7, ...), custom_call_target="tpu_custom_call" | custom-call | flops 10000000000 | bytes 30000000 | tf_op jit(solution)/shard_map/attend/pallas_call | solution.py:167
  103.6 9.6 %attend.5 = (bf16[2048,2304]{1,0:T(8,128)(2,1)}, bf16[16,6,128,256]{3,2,1,0:T(8,128)(2,1)}, bf16[2048,768]{1,0:T(8,128)(2,1)}, bf16[2048,768]{1,0:T(8,128)(2,1)}, f32[8,128]{1,0:T(8,128)}) custom-call(s32[4]{0:T(128)} %pad_add_fusion.1.where, s32[2,16]{1,0:T(2,128)} %pad_add_fusion.live, ...), custom_call_target="tpu_custom_call", output_to_operand_aliasing={{0}: (7, {}), {1}: (8, {}), {2}: (9, {}), {3}: (10, {})} | custom-call | flops 10000000000 | bytes 30000000 | tf_op jit(solution)/shard_map/attend/pallas_call | solution.py:167
  113.2 4.4 %collective-permute-done.10.far = bf16[256,768]{1,0:T(8,128)(2,1)} collective-permute-done((bf16[256,768]{1,0:T(8,128)(2,1)}, bf16[256,768]{1,0:T(8,128)(2,1)}, u32[]{:S(2)}, u32[]{:S(2)}) %collective-permute-start.10) | collective-permute-done | bytes 393248 | tf_op jit(solution)/shard_map/ppermute | solution.py:583
  117.6 9.6 %attend.6 = (bf16[2048,2304]{1,0:T(8,128)(2,1)}, bf16[16,6,128,256]{3,2,1,0:T(8,128)(2,1)}, bf16[2048,768]{1,0:T(8,128)(2,1)}, bf16[2048,768]{1,0:T(8,128)(2,1)}, f32[8,128]{1,0:T(8,128)}) custom-call(s32[4]{0:T(128)} %pad_add_fusion.1.where, s32[2,16]{1,0:T(2,128)} %pad_add_fusion.live, ...), custom_call_target="tpu_custom_call", output_to_operand_aliasing={{0}: (7, {}), {1}: (8, {}), {2}: (9, {}), {3}: (10, {})} | custom-call | flops 10000000000 | bytes 30000000 | tf_op jit(solution)/shard_map/attend/pallas_call | solution.py:167
  127.2 7.1 %collective-permute-done.16.far = bf16[256,768]{1,0:T(8,128)(2,1)} collective-permute-done((bf16[256,768]{1,0:T(8,128)(2,1)}, bf16[256,768]{1,0:T(8,128)(2,1)}, u32[]{:S(2)}, u32[]{:S(2)}) %collective-permute-start.16) | collective-permute-done | bytes 393248 | tf_op jit(solution)/shard_map/ppermute | solution.py:583
  140.5 10.0 %attend.7 = (bf16[2048,2304]{1,0:T(8,128)(2,1)}, bf16[16,6,128,256]{3,2,1,0:T(8,128)(2,1)}, bf16[2048,768]{1,0:T(8,128)(2,1)}, bf16[2048,768]{1,0:T(8,128)(2,1)}, f32[8,128]{1,0:T(8,128)}) custom-call(s32[4]{0:T(128)} %pad_add_fusion.1.where, s32[2,16]{1,0:T(2,128)} %pad_add_fusion.live, ...), custom_call_target="tpu_custom_call", output_to_operand_aliasing={{0}: (7, {}), {1}: (8, {}), {2}: (9, {}), {3}: (10, {})} | custom-call | flops 10000000000 | bytes 30000000 | tf_op jit(solution)/shard_map/attend/pallas_call | solution.py:167
  151.4 20.1 %feed.3 = (bf16[2048,768]{1,0:T(8,128)(2,1)}, bf16[2048,3072]{1,0:T(8,128)(2,1)}, bf16[2048,3072]{1,0:T(8,128)(2,1)}, bf16[2048,768]{1,0:T(8,128)(2,1)}, bf16[20...) custom-call(s32[4]{0:T(128)} %pad_add_fusion.1.where, ...), custom_call_target="tpu_custom_call" | custom-call | flops 1 | bytes 1 | tf_op jit(solution)/shard_map/feed/pallas_call | solution.py:316
  171.5 3.4 collective-permute-done.21.far
  175.7 20.1 %feed.4 = (bf16[2048,768]{1,0:T(8,128)(2,1)}, bf16[2048,3072]{1,0:T(8,128)(2,1)}, bf16[2048,3072]{1,0:T(8,128)(2,1)}, bf16[2048,768]{1,0:T(8,128)(2,1)}, bf16[20...) custom-call(s32[4]{0:T(128)} %pad_add_fusion.1.where, ...), custom_call_target="tpu_custom_call", output_to_operand_aliasing={{0}: (15, {}), {1}: (16, {}), {2}: (17, {}), {3}: (18, {}),... | custom-call | flops 1 | bytes 1 | tf_op jit(solution)/shard_map/feed/pallas_call | solution.py:316
  195.9 35.6 %feed.5 = (bf16[2048,768]{1,0:T(8,128)(2,1)}, bf16[2048,3072]{1,0:T(8,128)(2,1)}, bf16[2048,3072]{1,0:T(8,128)(2,1)}, bf16[2048,768]{1,0:T(8,128)(2,1)}, bf16[20...) custom-call(s32[4]{0:T(128)} %pad_add_fusion.1.where, ...), custom_call_target="tpu_custom_call", output_to_operand_aliasing={{0}: (15, {}), {1}: (16, {}), {2}: (17, {}), {3}: (18, {}),... | custom-call | flops 1 | bytes 1 | tf_op jit(solution)/shard_map/feed/pallas_call | solution.py:316
  231.5 2.9 collective-permute-start.23
  235.3 33.6 %wide_grads.1 = (bf16[4,4,5,48,384]{4,3,2,1,0:T(8,128)(2,1)}, bf16[4,4,5,48,384]{4,3,2,1,0:T(8,128)(2,1)}, bf16[4,4,4,48,384]{4,3,2,1,0:T(8,128)(2,1)}, bf16[4,4,4,48,384]{4,3,2,1,0:T(8,128)(2,1)}) custom-call(s32[4]{0:T(128)} %pad_add_fusion.1.where, bf16[2048,3072]{1,0:T(8,128)(2,1)} %get-tuple-element.152.dinner, ...), custom_call_target="tpu_custom_call" | custom-call | flops 1 | bytes 1 | tf_op jit(solution)/shard_map/wide_grads/pallas_call | solution.py:525
  270.3 13.9 %back.4 = (f32[2048,768]{1,0:T(8,128)}, bf16[2048,2304]{1,0:T(8,128)(2,1)}, bf16[256,768]{1,0:T(8,128)(2,1)}, f32[8,768]{1,0:T(8,128)}) custom-call(s32[4]{0:T(128)} %pad_add_fusion.1.where, bf16[2048,2304]{1,0:T(8,128)(2,1)} %get-tuple-element.146.qkv_all, bf16[16,6,128,256]{3,2,1,0:T(8,128)(2,1)} %get-tuple-element.147.prob_all, ...), custom_call_target="tpu_custom_call" | custom-call | flops 1 | bytes 1 | tf_op jit(solution)/shard_map/back/pallas_call | solution.py:439
  285.8 2.3 add_convert_fusion.refs_4_
  292.4 13.6 %back.5 = (f32[2048,768]{1,0:T(8,128)}, bf16[2048,2304]{1,0:T(8,128)(2,1)}, bf16[256,768]{1,0:T(8,128)(2,1)}, f32[8,768]{1,0:T(8,128)}) custom-call(s32[4]{0:T(128)} %pad_add_fusion.1.where, bf16[2048,2304]{1,0:T(8,128)(2,1)} %get-tuple-element.146.qkv_all, ...), custom_call_target="tpu_custom_call", output_to_operand_aliasing={{0}: (7, {}), {1}: (8, {})} | custom-call | flops 1 | bytes 1 | tf_op jit(solution)/shard_map/back/pallas_call | solution.py:439
  306.0 2.5 collective-permute-start.29
  308.5 13.6 %back.6 = (f32[2048,768]{1,0:T(8,128)}, bf16[2048,2304]{1,0:T(8,128)(2,1)}, bf16[256,768]{1,0:T(8,128)(2,1)}, f32[8,768]{1,0:T(8,128)}) custom-call(s32[4]{0:T(128)} %pad_add_fusion.1.where, bf16[2048,2304]{1,0:T(8,128)(2,1)} %get-tuple-element.146.qkv_all, ...), custom_call_target="tpu_custom_call", output_to_operand_aliasing={{0}: (7, {}), {1}: (8, {})} | custom-call | flops 1 | bytes 1 | tf_op jit(solution)/shard_map/back/pallas_call | solution.py:439
  330.2 13.9 %back.7 = (f32[2048,768]{1,0:T(8,128)}, bf16[2048,2304]{1,0:T(8,128)(2,1)}, bf16[256,768]{1,0:T(8,128)(2,1)}, f32[8,768]{1,0:T(8,128)}) custom-call(s32[4]{0:T(128)} %pad_add_fusion.1.where, bf16[2048,2304]{1,0:T(8,128)(2,1)} %get-tuple-element.146.qkv_all, ...), custom_call_target="tpu_custom_call", output_to_operand_aliasing={{0}: (7, {}), {1}: (8, {})} | custom-call | flops 1 | bytes 1 | tf_op jit(solution)/shard_map/back/pallas_call | solution.py:439
  353.6 13.4 %proj_grads.1 = (bf16[4,4,160,384]{3,2,1,0:T(8,128)(2,1)}, bf16[4,4,160,384]{3,2,1,0:T(8,128)(2,1)}) custom-call(s32[4]{0:T(128)} %pad_add_fusion.1.where, bf16[2048,2304]{1,0:T(8,128)(2,1)} %get-tuple-element.179.dqkv, bf16[2048,768]{1,0:T(8,128)(2,1)} %get-tuple-element.118.x_all.x, bf16[16,16,768]{2,1,0:T(8,128)(2,1)} %convert_element_type.265.tiny, ...), custom_call_target="tpu_custom_call" | custom-call | flops 1 | bytes 1 | tf_op jit(solution)/shard_map/proj_grads/pallas_call | solution.py:559
  382.5 15.6 %collective-permute-done.31 = bf16[256,768]{1,0:T(8,128)(2,1)S(1)} collective-permute-done((bf16[256,768]{1,0:T(8,128)(2,1)S(1)}, bf16[256,768]{1,0:T(8,128)(2,1)S(1)}, u32[]{:S(2)}, u32[]{:S(2)}) %collective-permute-start.31) | collective-permute-done | bytes 393248 | tf_op jit(solution)/shard_map/ppermute | solution.py:583
  399.0 6.1 %collective-permute-done.39 = bf16[1,1,9,48,384]{4,3,2,1,0:T(8,128)(2,1)S(1)} collective-permute-done((bf16[1,1,9,48,384]{4,3,2,1,0:T(8,128)(2,1)S(1)}, bf16[1,1,9,48,384]{4,3,2,1,0:T(8,128)(2,1)S(1)}, u32[]{:S(2)}, u32[]{:S(2)}) %collective-permute-start.39) | collective-permute-done | bytes 331808 | tf_op jit(solution)/shard_map/ppermute | solution.py:583
  407.2 2.4 collective-permute-start.41
  411.3 7.2 %collective-permute-done.40 = bf16[160,384]{1,0:T(8,128)(2,1)S(1)} collective-permute-done((bf16[160,384]{1,0:T(8,128)(2,1)S(1)}, bf16[160,384]{1,0:T(8,128)(2,1)S(1)}, u32[]{:S(2)}, u32[]{:S(2)}) %collective-permute-start.40) | collective-permute-done | bytes 122912 | tf_op jit(solution)/shard_map/ppermute | solution.py:583
  (225 shorter events, 86.1 us)
Async XLA Ops:
  12.5 35.3 %collective-permute-start.2 = (bf16[488,768]{1,0:T(8,128)(2,1)S(1)}, bf16[488,768]{1,0:T(8,128)(2,1)S(1)}, u32[]{:S(2)}, u32[]{:S(2)}) collective-permute-start(bf16[488,768]{1,0:T(8,128)(2,1)S(1)} %fusion.5), channel_id=1, source_target_pairs={{0,16},{2,18},{4,20},{6,22},{8,24},{10,26},{12,28},{14,30},{16,0},... | collective-permute-start | bytes 2248712 | tf_op jit(solution)/shard_map/ppermute | solution.py:583
  13.3 20.6 %collective-permute-start.5 = (bf16[2,160,384]{2,1,0:T(8,128)(2,1)S(1)}, bf16[2,160,384]{2,1,0:T(8,128)(2,1)S(1)}, u32[]{:S(2)}, u32[]{:S(2)}) collective-permute-start(bf16[2,160,384]{2,1,0:T(8,128)(2,1)S(1)} %pad_maximum_fusion.10), channel_id=1, source_target_pairs={{0,8},{2,10},{4,12},{6,14},{8,0},{10,2},{12,4},{14,6},{16,24},{18,... | collective-permute-start | bytes 737288 | tf_op jit(solution)/shard_map/ppermute | solution.py:583
  35.7 22.0 %collective-permute-start.7 = (bf16[4,160,384]{2,1,0:T(8,128)(2,1)S(1)}, bf16[4,160,384]{2,1,0:T(8,128)(2,1)S(1)}, u32[]{:S(2)}, u32[]{:S(2)}) collective-permute-start(bf16[4,160,384]{2,1,0:T(8,128)(2,1)S(1)} %bitcast.156), channel_id=1, source_target_pairs={{0,4},{1,5},{2,6},{3,7},{4,0},{5,1},{6,2},{7,3},{8,12},{9,13},{10,... | collective-permute-start | bytes 1474568 | tf_op jit(solution)/shard_map/ppermute | solution.py:590
  37.2 20.5 %collective-permute-start.8 = (bf16[4,160,384]{2,1,0:T(8,128)(2,1)S(1)}, bf16[4,160,384]{2,1,0:T(8,128)(2,1)S(1)}, u32[]{:S(2)}, u32[]{:S(2)}) collective-permute-start(bf16[4,160,384]{2,1,0:T(8,128)(2,1)S(1)} %bitcast.157), channel_id=1, source_target_pairs={{0,5},{1,4},{2,7},{3,6},{4,1},{5,0},{6,3},{7,2},{8,13},{9,12},{10,... | collective-permute-start | bytes 1474568 | tf_op jit(solution)/shard_map/ppermute | solution.py:590
  58.1 32.6 %collective-permute-start.9 = (bf16[4,4,160,384]{3,2,1,0:T(8,128)(2,1)S(1)}, bf16[4,4,160,384]{3,2,1,0:T(8,128)(2,1)}, u32[]{:S(2)}, u32[]{:S(2)}) collective-permute-start(bf16[4,4,160,384]{3,2,1,0:T(8,128)(2,1)S(1)} %pad_maximum_fusion.1.refs_0_), channel_id=1, source_target_pairs={{0,2},{1,3},{2,0},{3,1},{4,6},{5,7},{6,4},{7,5},{8,10},{9,11},{10,... | collective-permute-start | bytes 5898248 | tf_op jit(solution)/shard_map/ppermute | solution.py:590
  58.1 23.2 %collective-permute-start = (bf16[256,768]{1,0:T(8,128)(2,1)}, bf16[256,768]{1,0:T(8,128)(2,1)}, u32[]{:S(2)}, u32[]{:S(2)}) collective-permute-start(bf16[256,768]{1,0:T(8,128)(2,1)} %get-tuple-element.206), channel_id=1, source_target_pairs={{0,16},{2,18},{4,20},{6,22},{8,24},{10,26},{12,28},{14,30},{16,0},... | collective-permute-start | bytes 1179656 | tf_op jit(solution)/shard_map/ppermute | solution.py:583
  65.5 22.4 %collective-permute-start.12 = (bf16[4,5,48,384]{3,2,1,0:T(8,128)(2,1)}, bf16[4,5,48,384]{3,2,1,0:T(8,128)(2,1)S(1)}, u32[]{:S(2)}, u32[]{:S(2)}) collective-permute-start(bf16[4,5,48,384]{3,2,1,0:T(8,128)(2,1)} %get-tuple-element.210), channel_id=1, source_target_pairs={{0,1},{1,0},{2,3},{3,2},{4,5},{5,4},{6,7},{7,6},{8,9},{9,8},{10,11... | collective-permute-start | bytes 2211848 | tf_op jit(solution)/shard_map/ppermute | solution.py:590
  67.9 17.6 %collective-permute-start.14 = (bf16[4,4,48,384]{3,2,1,0:T(8,128)(2,1)}, bf16[4,4,48,384]{3,2,1,0:T(8,128)(2,1)}, u32[]{:S(2)}, u32[]{:S(2)}) collective-permute-start(bf16[4,4,48,384]{3,2,1,0:T(8,128)(2,1)} %get-tuple-element.208), channel_id=1, source_target_pairs={{0,4},{1,5},{2,6},{3,7},{4,0},{5,1},{6,2},{7,3},{8,12},{9,13},{10,... | collective-permute-start | bytes 1769480 | tf_op jit(solution)/shard_map/ppermute | solution.py:590
  81.3 36.3 %collective-permute-start.10 = (bf16[256,768]{1,0:T(8,128)(2,1)}, bf16[256,768]{1,0:T(8,128)(2,1)}, u32[]{:S(2)}, u32[]{:S(2)}) collective-permute-start(bf16[256,768]{1,0:T(8,128)(2,1)} %get-tuple-element.105), channel_id=1, source_target_pairs={{0,16},{2,18},{4,20},{6,22},{8,24},{10,26},{12,28},{14,30},{16,0},... | collective-permute-start | bytes 1179656 | tf_op jit(solution)/shard_map/ppermute | solution.py:583
  81.3 45.9 %collective-permute-start.3 = (bf16[256,768]{1,0:T(8,128)(2,1)}, bf16[256,768]{1,0:T(8,128)(2,1)}, u32[]{:S(2)}, u32[]{:S(2)}) collective-permute-start(bf16[256,768]{1,0:T(8,128)(2,1)} %get-tuple-element.104), channel_id=1, source_target_pairs={{0,16},{2,18},{4,20},{6,22},{8,24},{10,26},{12,28},{14,30},{16,0},... | collective-permute-start | bytes 1179656 | tf_op jit(solution)/shard_map/ppermute | solution.py:583
  85.5 48.8 %collective-permute-start.16 = (bf16[256,768]{1,0:T(8,128)(2,1)}, bf16[256,768]{1,0:T(8,128)(2,1)}, u32[]{:S(2)}, u32[]{:S(2)}) collective-permute-start(bf16[256,768]{1,0:T(8,128)(2,1)} %get-tuple-element.121), channel_id=1, source_target_pairs={{0,16},{2,18},{4,20},{6,22},{8,24},{10,26},{12,28},{14,30},{16,0},... | collective-permute-start | bytes 1179656 | tf_op jit(solution)/shard_map/ppermute | solution.py:583
  87.9 46.5 %collective-permute-start.15 = (bf16[2,4,4,48,384]{4,3,2,1,0:T(8,128)(2,1)}, bf16[2,4,4,48,384]{4,3,2,1,0:T(8,128)(2,1)}, u32[]{:S(2)}, u32[]{:S(2)}) collective-permute-start(bf16[2,4,4,48,384]{4,3,2,1,0:T(8,128)(2,1)} %pad_maximum_fusion.4.refs_2_), channel_id=1, source_target_pairs={{0,1},{1,0},{2,3},{3,2},{4,5},{5,4},{6,7},{7,6},{8,9},{9,8},{10,11... | collective-permute-start | bytes 3538952 | tf_op jit(solution)/shard_map/ppermute | solution.py:590
  90.6 43.7 %collective-permute-start.13 = (bf16[2,4,5,48,384]{4,3,2,1,0:T(8,128)(2,1)S(1)}, bf16[2,4,5,48,384]{4,3,2,1,0:T(8,128)(2,1)S(1)}, u32[]{:S(2)}, u32[]{:S(2)}) collective-permute-start(bf16[2,4,5,48,384]{4,3,2,1,0:T(8,128)(2,1)S(1)} %pad_maximum_fusion.2.refs_0_), channel_id=1, source_target_pairs={{0,4},{1,5},{2,6},{3,7},{4,0},{5,1},{6,2},{7,3},{8,12},{9,13},{10,... | collective-permute-start | bytes 4423688 | tf_op jit(solution)/shard_map/ppermute | solution.py:590
  134.5 16.9 %collective-permute-start.17 = (bf16[2,4,5,48,384]{4,3,2,1,0:T(8,128)(2,1)S(1)}, bf16[2,4,5,48,384]{4,3,2,1,0:T(8,128)(2,1)}, u32[]{:S(2)}, u32[]{:S(2)}) collective-permute-start(bf16[2,4,5,48,384]{4,3,2,1,0:T(8,128)(2,1)S(1)} %pad_maximum_fusion.2.refs_0_), channel_id=1, source_target_pairs={{0,2},{1,3},{2,0},{3,1},{4,6},{5,7},{6,4},{7,5},{8,10},{9,11},{10,... | collective-permute-start | bytes 4423688 | tf_op jit(solution)/shard_map/ppermute | solution.py:590
  135.0 16.4 %collective-permute-start.18 = (bf16[2,4,5,48,384]{4,3,2,1,0:T(8,128)(2,1)S(1)}, bf16[2,4,5,48,384]{4,3,2,1,0:T(8,128)(2,1)}, u32[]{:S(2)}, u32[]{:S(2)}) collective-permute-start(bf16[2,4,5,48,384]{4,3,2,1,0:T(8,128)(2,1)S(1)} %collective-permute-done.13.refs_1_), channel_id=1, source_target_pairs={{0,2},{1,3},{2,0},{3,1},{4,6},{5,7},{6,4},{7,5},{8,10},{9,11},{10,... | collective-permute-start | bytes 4423688 | tf_op jit(solution)/shard_map/ppermute | solution.py:590
  137.6 37.3 %collective-permute-start.21 = (bf16[256,768]{1,0:T(8,128)(2,1)}, bf16[256,768]{1,0:T(8,128)(2,1)S(1)}, u32[]{:S(2)}, u32[]{:S(2)}) collective-permute-start(bf16[256,768]{1,0:T(8,128)(2,1)} %get-tuple-element.126), channel_id=1, source_target_pairs={{0,16},{2,18},{4,20},{6,22},{8,24},{10,26},{12,28},{14,30},{16,0},... | collective-permute-start | bytes 1179656 | tf_op jit(solution)/shard_map/ppermute | solution.py:583
  138.4 57.4 %collective-permute-start.1 = (bf16[512,768]{1,0:T(8,128)(2,1)}, bf16[512,768]{1,0:T(8,128)(2,1)}, u32[]{:S(2)}, u32[]{:S(2)}) collective-permute-start(bf16[512,768]{1,0:T(8,128)(2,1)} %constant_dynamic-slice_fusion.6), channel_id=1, source_target_pairs={{0,16},{2,18},{4,20},{6,22},{8,24},{10,26},{12,28},{14,30},{16,0},... | collective-permute-start | bytes 2359304 | tf_op jit(solution)/shard_map/ppermute | solution.py:583
  195.8 38.7 %collective-permute-start.22 = (bf16[512,768]{1,0:T(8,128)(2,1)}, bf16[512,768]{1,0:T(8,128)(2,1)S(1)}, u32[]{:S(2)}, u32[]{:S(2)}) collective-permute-start(bf16[512,768]{1,0:T(8,128)(2,1)} %get-tuple-element.144), channel_id=1, source_target_pairs={{0,16},{2,18},{4,20},{6,22},{8,24},{10,26},{12,28},{14,30},{16,0},... | collective-permute-start | bytes 2359304 | tf_op jit(solution)/shard_map/ppermute | solution.py:583
  231.5 37.4 %collective-permute-start.23 = (bf16[512,768]{1,0:T(8,128)(2,1)}, bf16[512,768]{1,0:T(8,128)(2,1)S(1)}, u32[]{:S(2)}, u32[]{:S(2)}) collective-permute-start(bf16[512,768]{1,0:T(8,128)(2,1)} %get-tuple-element.145), channel_id=1, source_target_pairs={{0,16},{2,18},{4,20},{6,22},{8,24},{10,26},{12,28},{14,30},{16,0},... | collective-permute-start | bytes 2359304 | tf_op jit(solution)/shard_map/ppermute | solution.py:583
  288.2 34.4 %collective-permute-start.26 = (bf16[2,4,5,48,384]{4,3,2,1,0:T(8,128)(2,1)S(1)}, bf16[2,4,5,48,384]{4,3,2,1,0:T(8,128)(2,1)}, u32[]{:S(2)}, u32[]{:S(2)}) collective-permute-start(bf16[2,4,5,48,384]{4,3,2,1,0:T(8,128)(2,1)S(1)} %add_convert_fusion.refs_4_), channel_id=1, source_target_pairs={{0,4},{1,5},{2,6},{3,7},{4,0},{5,1},{6,2},{7,3},{8,12},{9,13},{10,... | collective-permute-start | bytes 4423688 | tf_op jit(solution)/shard_map/ppermute | solution.py:590
  291.4 30.8 %collective-permute-start.27 = (bf16[2,4,4,48,384]{4,3,2,1,0:T(8,128)(2,1)S(1)}, bf16[2,4,4,48,384]{4,3,2,1,0:T(8,128)(2,1)}, u32[]{:S(2)}, u32[]{:S(2)}) collective-permute-start(bf16[2,4,4,48,384]{4,3,2,1,0:T(8,128)(2,1)S(1)} %add_convert_fusion.1.refs_5_), channel_id=1, source_target_pairs={{0,1},{1,0},{2,3},{3,2},{4,5},{5,4},{6,7},{7,6},{8,9},{9,8},{10,11... | collective-permute-start | bytes 3538952 | tf_op jit(solution)/shard_map/ppermute | solution.py:590
  291.9 37.5 %collective-permute-start.28 = (bf16[256,768]{1,0:T(8,128)(2,1)}, bf16[256,768]{1,0:T(8,128)(2,1)S(1)}, u32[]{:S(2)}, u32[]{:S(2)}) collective-permute-start(bf16[256,768]{1,0:T(8,128)(2,1)} %get-tuple-element.174), channel_id=1, source_target_pairs={{0,16},{2,18},{4,20},{6,22},{8,24},{10,26},{12,28},{14,30},{16,0},... | collective-permute-start | bytes 1179656 | tf_op jit(solution)/shard_map/ppermute | solution.py:583
  306.0 23.3 %collective-permute-start.29 = (bf16[256,768]{1,0:T(8,128)(2,1)}, bf16[256,768]{1,0:T(8,128)(2,1)S(1)}, u32[]{:S(2)}, u32[]{:S(2)}) collective-permute-start(bf16[256,768]{1,0:T(8,128)(2,1)} %get-tuple-element.175), channel_id=1, source_target_pairs={{0,16},{2,18},{4,20},{6,22},{8,24},{10,26},{12,28},{14,30},{16,0},... | collective-permute-start | bytes 1179656 | tf_op jit(solution)/shard_map/ppermute | solution.py:583
  324.5 20.7 %collective-permute-start.32 = (bf16[4,5,48,384]{3,2,1,0:T(8,128)(2,1)S(1)}, bf16[4,5,48,384]{3,2,1,0:T(8,128)(2,1)S(1)}, u32[]{:S(2)}, u32[]{:S(2)}) collective-permute-start(bf16[4,5,48,384]{3,2,1,0:T(8,128)(2,1)S(1)} %fusion.6.refs_4_), channel_id=1, source_target_pairs={{0,1},{1,0},{2,3},{3,2},{4,5},{5,4},{6,7},{7,6},{8,9},{9,8},{10,11... | collective-permute-start | bytes 2211848 | tf_op jit(solution)/shard_map/ppermute | solution.py:590
  327.5 17.7 %collective-permute-start.33 = (bf16[4,4,48,384]{3,2,1,0:T(8,128)(2,1)S(1)}, bf16[4,4,48,384]{3,2,1,0:T(8,128)(2,1)S(1)}, u32[]{:S(2)}, u32[]{:S(2)}) collective-permute-start(bf16[4,4,48,384]{3,2,1,0:T(8,128)(2,1)S(1)} %fusion.7.refs_5_), channel_id=1, source_target_pairs={{0,4},{1,5},{2,6},{3,7},{4,0},{5,1},{6,2},{7,3},{8,12},{9,13},{10,... | collective-permute-start | bytes 1769480 | tf_op jit(solution)/shard_map/ppermute | solution.py:590
  329.3 37.7 %collective-permute-start.30 = (bf16[256,768]{1,0:T(8,128)(2,1)}, bf16[256,768]{1,0:T(8,128)(2,1)}, u32[]{:S(2)}, u32[]{:S(2)}) collective-permute-start(bf16[256,768]{1,0:T(8,128)(2,1)} %get-tuple-element.177), channel_id=1, source_target_pairs={{0,16},{2,18},{4,20},{6,22},{8,24},{10,26},{12,28},{14,30},{16,0},... | collective-permute-start | bytes 1179656 | tf_op jit(solution)/shard_map/ppermute | solution.py:583
  350.0 17.0 %collective-permute-start.34 = (bf16[2,1,9,48,384]{4,3,2,1,0:T(8,128)(2,1)}, bf16[2,1,9,48,384]{4,3,2,1,0:T(8,128)(2,1)}, u32[]{:S(2)}, u32[]{:S(2)}) collective-permute-start(bf16[2,1,9,48,384]{4,3,2,1,0:T(8,128)(2,1)} %dynamic-slice_convert_fusion), channel_id=1, source_target_pairs={{0,8},{2,10},{4,12},{6,14},{8,0},{10,2},{12,4},{14,6},{16,24},{18,... | collective-permute-start | bytes 1990664 | tf_op jit(solution)/shard_map/ppermute | solution.py:583
  370.3 27.8 %collective-permute-start.31 = (bf16[256,768]{1,0:T(8,128)(2,1)S(1)}, bf16[256,768]{1,0:T(8,128)(2,1)S(1)}, u32[]{:S(2)}, u32[]{:S(2)}) collective-permute-start(bf16[256,768]{1,0:T(8,128)(2,1)S(1)} %copy-done.30), channel_id=1, source_target_pairs={{0,16},{2,18},{4,20},{6,22},{8,24},{10,26},{12,28},{14,30},{16,0},... | collective-permute-start | bytes 1179656 | tf_op jit(solution)/shard_map/ppermute | solution.py:583
  376.8 28.4 %collective-permute-start.39 = (bf16[1,1,9,48,384]{4,3,2,1,0:T(8,128)(2,1)S(1)}, bf16[1,1,9,48,384]{4,3,2,1,0:T(8,128)(2,1)S(1)}, u32[]{:S(2)}, u32[]{:S(2)}) collective-permute-start(bf16[1,1,9,48,384]{4,3,2,1,0:T(8,128)(2,1)S(1)} %dynamic-slice_convert_fusion.1), channel_id=1, source_target_pairs={{0,16},{2,18},{4,20},{6,22},{8,24},{10,26},{12,28},{14,30},{16,0},... | collective-permute-start | bytes 995336 | tf_op jit(solution)/shard_map/ppermute | solution.py:583
  378.9 27.8 %collective-permute-start.36 = (bf16[4,160,384]{2,1,0:T(8,128)(2,1)S(1)}, bf16[4,160,384]{2,1,0:T(8,128)(2,1)S(1)}, u32[]{:S(2)}, u32[]{:S(2)}) collective-permute-start(bf16[4,160,384]{2,1,0:T(8,128)(2,1)S(1)} %get-tuple-element.194), channel_id=1, source_target_pairs={{0,1},{1,0},{2,3},{3,2},{4,5},{5,4},{6,7},{7,6},{8,9},{9,8},{10,11... | collective-permute-start | bytes 1474568 | tf_op jit(solution)/shard_map/ppermute | solution.py:590
  380.4 26.3 %collective-permute-start.37 = (bf16[4,160,384]{2,1,0:T(8,128)(2,1)S(1)}, bf16[4,160,384]{2,1,0:T(8,128)(2,1)S(1)}, u32[]{:S(2)}, u32[]{:S(2)}) collective-permute-start(bf16[4,160,384]{2,1,0:T(8,128)(2,1)S(1)} %get-tuple-element.195), channel_id=1, source_target_pairs={{0,4},{1,5},{2,6},{3,7},{4,0},{5,1},{6,2},{7,3},{8,12},{9,13},{10,... | collective-permute-start | bytes 1474568 | tf_op jit(solution)/shard_map/ppermute | solution.py:590
  381.0 25.8 %collective-permute-start.38 = (bf16[4,160,384]{2,1,0:T(8,128)(2,1)S(1)}, bf16[4,160,384]{2,1,0:T(8,128)(2,1)S(1)}, u32[]{:S(2)}, u32[]{:S(2)}) collective-permute-start(bf16[4,160,384]{2,1,0:T(8,128)(2,1)S(1)} %get-tuple-element.196), channel_id=1, source_target_pairs={{0,5},{1,4},{2,7},{3,6},{4,1},{5,0},{6,3},{7,2},{8,13},{9,12},{10,... | collective-permute-start | bytes 1474568 | tf_op jit(solution)/shard_map/ppermute | solution.py:590
  (42 other events, 401.4 us)

commit v4 on v3

--- a/solution.py
+++ b/solution.py
@@ -345,13 +345,12 @@
 
 
 def back_kernel(c0, skip, where, qkv_all, prob_all, dbranch_all, dmix_all, *refs):
-    views, refs = proj_views(refs[:2]), refs[-14:]
-    dx_all, dqkv_all, dx_far, vsum, wqkv, qkv, prob, dbranch, dmix, dqkv, dxs, dxf, sems, seq_sems = refs
-    r, width = dbranch.shape
-    h = dx_all.shape[0] // (2 * CHUNKS)
+    views, refs = proj_views(refs[:2]), refs[-12:]
+    dqkv_all, dx_far, vsum, wqkv, qkv, prob, dbranch, dmix, dqkv, dxf, sems, seq_sems = refs
+    r, width = dmix.shape
+    h = dqkv_all.shape[0] // (2 * CHUNKS)
     subs = r // (2 * h)
     seqs = h // SLOTS
-    span = pl.ds(c0 * 2 * h, r)
     for t in range(subs):
         for s in range(seqs):
             sem = seq_sems.at[t * seqs + s]
@@ -361,7 +360,9 @@
                 copy(dmix_all.at[there], dmix.at[rows], sem)
             copy(prob_all.at[(c0 + t) * seqs + s], prob.at[t * seqs + s], sem)
     pull(where, views, pl.ds(0, wqkv.shape[2]), wqkv, sems.at[3])
-    copy(dbranch_all.at[span], dbranch, sems.at[4])
+    for t in range(subs):
+        there = pl.ds((c0 + t) * 2 * h + h, h)
+        copy(dbranch_all.at[there], dbranch.at[pl.ds(t * h, h)], sems.at[4])
     lane = lax.broadcasted_iota(jnp.int32, (2 * SLOTS, 2 * HEAD_DIM), 1)
     low_half = lane < HEAD_DIM
 
@@ -416,20 +417,17 @@
             wait_for(wqkv, sems.at[3])
             wait_for(dbranch, sems.at[4])
         mine = dqkv[chunk]
-        dx = dbranch[chunk].astype(F32) + nn(mine, wqkv.reshape(3 * width, width)[...])
-        dxs[t * h : (t + 1) * h, :] = dx[:h]
-        start = pl.multiple_of(where[3] + (c0 + t) * h, h)
-        copy(dxs.at[pl.ds(t * h, h)], dx_all.at[pl.ds(start, h)], sems.at[6])
-        dxf[t * h : (t + 1) * h, :] = dx[h:].astype(BF)
+        part = slice(t * h, (t + 1) * h)
+        dx = dbranch[part].astype(F32) + nn(mine[h:], wqkv.reshape(3 * width, width)[...])
+        dxf[part, :] = dx.astype(BF)
         copy(dxf.at[pl.ds(t * h, h)], dx_far.at[pl.ds((skip + t) * h, h)], sems.at[7])
         vsum[0:1, :] += colsum(mine[:, :width].astype(F32))
         vsum[1:2, :] += colsum(mine[:, 2 * width :].astype(F32))
     wait_for(dqkv, sems.at[5])
-    wait_for(dxs, sems.at[6])
     wait_for(dxf, sems.at[7])
 
 
-def back(c0, subs, skip, dx_rows, where, rows, qkv_all, prob_all, dbranch_all, dmix_all, pieces, before, tokens):
+def back(c0, subs, skip, dx_rows, where, qkv_all, prob_all, dbranch_all, dmix_all, pieces, before, tokens):
     total, width = dbranch_all.shape
     r = subs * total // CHUNKS
     h = r // 2
@@ -438,18 +436,17 @@
     per = 3 * width // (4 * groups)
     return pl.pallas_call(
         functools.partial(back_kernel, c0, skip),
-        out_shape=(S((rows, width), F32), S((total, 3 * width), BF), S((dx_rows, width), BF), S((8, width), F32)),
+        out_shape=(S((total, 3 * width), BF), S((dx_rows, width), BF), S((8, width), F32)),
         in_specs=[SM] + [ANY] * (6 + len(before) + len(tokens)),
-        out_specs=(ANY, ANY, ANY, VM),
+        out_specs=(ANY, ANY, VM),
         input_output_aliases={7 + i: i for i in range(len(before))},
         scratch_shapes=[
             pltpu.VMEM((groups, 4, per, width), BF),
             pltpu.VMEM((r, 3 * width), BF),
             pltpu.VMEM((seqs,) + prob_all.shape[1:], BF),
-            pltpu.VMEM((r, width), BF),
+            pltpu.VMEM((h, width), BF),
             pltpu.VMEM((r, width), BF),
             pltpu.VMEM((r, 3 * width), BF),
-            pltpu.VMEM((h, width), F32),
             pltpu.VMEM((h, width), BF),
             DMA((8,)),
             DMA((seqs,)),
@@ -458,6 +455,70 @@
         cost_estimate=QUICK,
         name="back",
     )(where, qkv_all, prob_all, dbranch_all, dmix_all, *pieces, *before, *tokens)
+
+
+def finish_kernel(n_y, n_dx, where, dqkv_all, dbranch_all, *refs):
+    views = proj_views(refs[:2])
+    y_parts, dx_parts = refs[3 : 3 + n_y], refs[3 + n_y : 3 + n_y + n_dx]
+    dx_all, y_all, wqkv, dqkv, dbranch, dx, came, wider, ys, sems = refs[-10:]
+    width = dbranch.shape[2]
+    h = dbranch.shape[1]
+    moved = CHUNKS * h
+    away = moved - where[3]
+    pull(where, views, pl.ds(0, wqkv.shape[2]), wqkv, sems.at[0])
+    for c, part in enumerate(dx_parts):
+        copy(part, came.at[c], sems.at[2])
+    size = moved // n_y
+    for i, part in enumerate(y_parts):
+        copy(part, ys.at[i], sems.at[3])
+    for c in range(CHUNKS):
+        span = pl.ds(c * 2 * h, h)
+        copy(dqkv_all.at[span], dqkv.at[c], sems.at[5 + c])
+        copy(dbranch_all.at[span], dbranch.at[c], sems.at[5 + c])
+    wait_for(ys, sems.at[3])
+    for i in range(n_y):
+        copy(ys.at[i], y_all.at[pl.ds(pl.multiple_of(away + i * size, size), size)], sems.at[3])
+    wait_for(came, sems.at[2])
+    for c in range(n_dx):
+        wider[c] = came[c].astype(F32)
+        copy(wider.at[c], dx_all.at[pl.ds(pl.multiple_of(away + c * h, h), h)], sems.at[4])
+    wait_for(wqkv, sems.at[0])
+    for c in range(CHUNKS):
+        wait_for(dqkv.at[c], sems.at[5 + c])
+        wait_for(dbranch.at[c], sems.at[5 + c])
+        dx[c] = dbranch[c].astype(F32) + nn(dqkv[c], wqkv.reshape(3 * width, width)[...])
+        copy(dx.at[c], dx_all.at[pl.ds(pl.multiple_of(where[3] + c * h, h), h)], sems.at[1])
+    wait_for(ys, sems.at[3])
+    wait_for(wider, sems.at[4])
+    wait_for(dx, sems.at[1])
+
+
+def finish(where, dqkv_all, dbranch_all, pieces, result, y_parts, dx_parts, tokens):
+    total, width = dbranch_all.shape
+    h = total // (2 * CHUNKS)
+    groups = pieces[0].shape[1]
+    per = 3 * width // (4 * groups)
+    n_y, n_dx = len(y_parts), len(dx_parts)
+    return pl.pallas_call(
+        functools.partial(finish_kernel, n_y, n_dx),
+        out_shape=(S(result.shape, F32), S(result.shape, BF)),
+        in_specs=[SM] + [ANY] * (5 + n_y + n_dx + len(tokens)),
+        out_specs=(ANY, ANY),
+        input_output_aliases={5: 1},
+        scratch_shapes=[
+            pltpu.VMEM((groups, 4, per, width), BF),
+            pltpu.VMEM((CHUNKS, h, 3 * width), BF),
+            pltpu.VMEM((CHUNKS, h, width), BF),
+            pltpu.VMEM((CHUNKS, h, width), F32),
+            pltpu.VMEM((n_dx, h, width), BF),
+            pltpu.VMEM((n_dx, h, width), F32),
+            pltpu.VMEM((n_y, CHUNKS * h // n_y, width), BF),
+            DMA((5 + CHUNKS,)),
+        ],
+        compiler_params=pltpu.CompilerParams(vmem_limit_bytes=LIMIT),
+        cost_estimate=QUICK,
+        name="finish",
+    )(where, dqkv_all, dbranch_all, *pieces, result, *y_parts, *dx_parts, *tokens)
 
 
 def put(buf, where, mod, value, dims, by_pair=False):
@@ -614,8 +675,8 @@
     return lax.optimization_barrier((values, tokens))[0]
 
 
-def gather_proj(slab):
-    held = gather_far(slab)
+def gather_proj(slab, came):
+    held = gather_far(slab, came)
     near = jnp.stack([held] + [across(held, 0, dy, dx) for dy, dx in ((0, 1), (1, 0), (1, 1))])
     return [near, across(near, 1, 0, 0)]
 
@@ -642,8 +703,9 @@
     came = across(send, 1, 0, 0)
     held = wide(keep[0]) + wide(came[0])
     ready = after([low(wide(keep[i]) + wide(came[i])) for i in (1, 2, 3)], gate_one)
-    for part, (dy, dx) in zip(ready, ((0, 1), (1, 0), (1, 1))):
-        held = held + wide(across(part, 0, dy, dx))
+    got = [across(part, 0, dy, dx) for part, (dy, dx) in zip(ready, ((0, 1), (1, 0), (1, 1)))]
+    for part in got:
+        held = held + wide(part)
     held = after(held, gate_two)
     for bit in range(bits_of("pair") - 2, -1, -1):
         held, _ = halved(held, "pair", bit, held.ndim - 1)
@@ -663,7 +725,7 @@
     total = slab(0, 0)
     for u, v in ((1, 0), (1, 1), (0, 1)):
         total = total + wide(swapped(low(slab(u, v)), "mod", (u << top) | (v << (top - 1))))
-    return total
+    return total, got[:1]
 
 
 def halved(held, axis, bit, dim):
@@ -757,13 +819,14 @@
     head = jnp.pad(live_away.astype(BF)[None], ((0, 15), (0, width - moved // SLOTS)))
     folded = jnp.concatenate(jnp.split(slab.reshape(-1, line), width // line, 0), 1)
     first_rows = lax.dynamic_slice_in_dim(rows_input, away_start, X_UNITS[0] * chunk)
-    parcel = over(jnp.concatenate([first_rows, folded, head], 0))
+    proj_came = over(proj_slab)
+    parcel = over(after(jnp.concatenate([first_rows, folded, head], 0), proj_came))
     tall = folded.shape[0]
     came = parcel[first_rows.shape[0] : first_rows.shape[0] + tall]
     came = jnp.concatenate(jnp.split(came, width // line, 1), 0).reshape(slab.shape)
     live = jnp.stack([live_own, parcel[first_rows.shape[0] + tall, : moved // SLOTS].astype(jnp.int32)])
 
-    proj = gather_proj(proj_slab)
+    proj = gather_proj(proj_slab, proj_came)
     far_rows = [parcel]
     for c, n in units(X_UNITS)[1:]:
         part = lax.dynamic_slice_in_dim(rows_input, away_start + c * chunk, n * chunk)
@@ -811,20 +874,20 @@
     qv_sum, done = 0.0, None
     for c0, n in units(BACK_UNITS):
         (d0, size), = [unit for unit in units(DX_UNITS) if unit[0] <= c0 < unit[0] + unit[1]]
-        backed = backed[: 2 if c0 == d0 else 3]
+        backed = backed[: 1 if c0 == d0 else 2]
         tokens = []
         if c0 in (1, 3):
             tokens = wide_steps.send(done)
         if c0 == 3:
             tokens = tokens + back_grads[:2]
         out = back(
-            c0, n, c0 - d0, size * chunk, where, rows, qkv_all, prob_all, dbranch_all, dmix_all, proj, backed, tokens
+            c0, n, c0 - d0, size * chunk, where, qkv_all, prob_all, dbranch_all, dmix_all, proj, backed, tokens
         )
-        backed, done = out[:3], out[3]
+        backed, done = out[:2], out[2]
         if c0 + n == d0 + size:
-            back_grads.append(over(out[2]))
-        qv_sum = qv_sum + out[3]
-    input_grad, dqkv_all = backed[:2]
+            back_grads.append(over(out[1]))
+        qv_sum = qv_sum + out[2]
+    dqkv_all = backed[0]
 
     vec_grad = jnp.concatenate([qv_sum[:2], vec_sum[:6]], 0).reshape(pairs, -1, mods, vectors.shape[1])
     bup_grad = bup_sum.reshape(BLOCKS, pairs, line).transpose(1, 0, 2).reshape(pairs, -1, mods, b_up.shape[1])
@@ -835,13 +898,12 @@
     tokens = wide_steps.send(done)
     proj_pair = proj_grads(where, dqkv_all, x_all, tiny_grad, groups, tokens)
     *gates, g_wide = wide_steps
-    g_proj = reduce_proj(*after(proj_pair, back_grads[2:3] + gates[0][1:]), [], g_wide[1:])
+    g_proj, token = reduce_proj(*after(proj_pair, back_grads[2:3] + gates[0][1:]), [], g_wide[1:])
+    input_grad, result = finish(where, dqkv_all, dbranch_all, proj, result, back_rows, back_grads[:-1], token)
     g_wide = g_wide[0][0]
 
-    for (c0, n), part in zip(units(Y_UNITS), back_rows):
-        result = lax.dynamic_update_slice_in_dim(result, part, away_start + c0 * chunk, 0)
-    for (c0, n), part in zip(units(DX_UNITS), back_grads):
-        input_grad = lax.dynamic_update_slice_in_dim(input_grad, wide(part), away_start + c0 * chunk, 0)
+    last = away_start + (CHUNKS - 1) * chunk
+    input_grad = lax.dynamic_update_slice_in_dim(input_grad, wide(back_grads[-1]), last, 0)
     g_small = g_proj[per:].reshape(-1)
     return (
         result,

time: 428 us -> 424 us (level)
  waiting for transfers between devices: 95.4 us -> 84.4 us
  Pallas kernels: 217 us -> 223 us
  starting transfers between devices: 49 us -> 53.5 us
    ppermute x21, waiting for transfers between devices: 84.5 us -> 71.4 us  [swapped(): lax.ppermute(values, axis, [(i, i ^ mask) for i in range(lax.axis_size(ax...]
    pallas_call x4 -> x5, Pallas kernels: 55 us -> 60.8 us  [the longest x4 50.4 us: back(): pl.pallas_call(functools.partial(back_kernel, c0, skip), out_shape=(S((to...]
    ppermute x21, starting transfers between devices: 29.6 us -> 34.9 us  [swapped(): lax.ppermute(values, axis, [(i, i ^ mask) for i in range(lax.axis_size(ax...]
  transfers between devices with their start and end apart: 43 -> 43, of which waited for: 16 -> 12; matrix products, arithmetic and copies ran while one was open for 11% -> 10% of each run, Pallas kernels for 51% -> 53%
where the time goes in v4:
time: 424 us; the launch traced here: 418 us
  Pallas kernels  223 us (53%)
  waiting for transfers between devices  84.4 us (20%)
  starting transfers between devices  53.5 us (13%)
  local copies, waits for them, and re-layouts  28 us (7%)
  other arithmetic  27.4 us (6%)
    pallas_call x3, Pallas kernels, feed(): pl.pallas_call(functools.partial(feed_kernel, c0, subs, skip, sides), out...  75.8 us
    ppermute x21, waiting for transfers between devices, swapped(): lax.ppermute(values, axis, [(i, i ^ mask) for i in range(lax.axis_size(ax...  71.4 us
    pallas_call x4, Pallas kernels, back(): pl.pallas_call(functools.partial(back_kernel, c0, skip), out_shape=(S((to...  50.4 us
    pallas_call x4, Pallas kernels, attend(): pl.pallas_call(functools.partial(attend_kernel, c, skip), out_shape=shape...  39.1 us
    ppermute x21, starting transfers between devices, swapped(): lax.ppermute(values, axis, [(i, i ^ mask) for i in range(lax.axis_size(ax...  34.9 us
    pallas_call x1, Pallas kernels, wide_grads(): pl.pallas_call(functools.partial(wide_grads_kernel, sides), grid=(BLOCKS,...  33.6 us
    ppermute x22, starting transfers between devices, across(): lax.ppermute(values, ('mod', 'pair'), [(i, i ^ mask) for i in range(count)])  18.6 us
    pallas_call x1, Pallas kernels, proj_grads(): pl.pallas_call(proj_grads_kernel, grid=(2,), out_shape=(S(shape, BF),) *...  13.7 us
  transfers between devices with their start and end apart: 43, of which 12 were waited for; matrix products, arithmetic and copies ran while one was open for 10% of the time, Pallas kernels for 53%

profile of v4, /device:TPU:0, one launch (start us, length us, event | category | flops | bytes accessed | tf_op | source)
XLA Modules:
  0.0 418.2 jit_solution(2564114460415215475)
XLA Ops:
  3.2 4.1 collective-permute-start
  9.3 2.5 constant_dynamic-slice_fusion.3
  13.4 4.1 collective-permute-start.4
  17.5 16.8 %collective-permute-done.4 = bf16[2,160,384]{2,1,0:T(8,128)(2,1)S(1)} collective-permute-done((bf16[2,160,384]{2,1,0:T(8,128)(2,1)S(1)}, bf16[2,160,384]{2,1,0:T(8,128)(2,1)S(1)}, u32[]{:S(2)}, u32[]{:S(2)}) %collective-permute-start.4) | collective-permute-done | bytes 245792 | tf_op jit(solution)/shard_map/ppermute | solution.py:644
  38.0 10.1 %collective-permute-done.1.far = bf16[488,768]{1,0:T(8,128)(2,1)S(1)} collective-permute-done((bf16[488,768]{1,0:T(8,128)(2,1)S(1)}, bf16[488,768]{1,0:T(8,128)(2,1)S(1)}, u32[]{:S(2)}, u32[]{:S(2)}) %collective-permute-start.1) | collective-permute-done | bytes 749600 | tf_op jit(solution)/shard_map/ppermute | solution.py:644
  49.0 8.4 %collective-permute-done.6 = bf16[4,160,384]{2,1,0:T(8,128)(2,1)S(1)} collective-permute-done((bf16[4,160,384]{2,1,0:T(8,128)(2,1)S(1)}, bf16[4,160,384]{2,1,0:T(8,128)(2,1)S(1)}, u32[]{:S(2)}, u32[]{:S(2)}) %collective-permute-start.6) | collective-permute-done | bytes 491552 | tf_op jit(solution)/shard_map/ppermute | solution.py:651
  57.9 6.8 %collective-permute-start.2 = (bf16[256,768]{1,0:T(8,128)(2,1)}, bf16[256,768]{1,0:T(8,128)(2,1)}, u32[]{:S(2)}, u32[]{:S(2)}) collective-permute-start(bf16[256,768]{1,0:T(8,128)(2,1)} %get-tuple-element.202), channel_id=1, source_target_pairs={{0,16},{2,18},{4,20},{6,22},{8,24},{10,26},{12,28},{14,30},{16,0},... | collective-permute-start | bytes 1179656 | tf_op jit(solution)/shard_map/ppermute | solution.py:644
  72.0 10.2 %collective-permute-done.2.far = bf16[256,768]{1,0:T(8,128)(2,1)} collective-permute-done((bf16[256,768]{1,0:T(8,128)(2,1)}, bf16[256,768]{1,0:T(8,128)(2,1)}, u32[]{:S(2)}, u32[]{:S(2)}) %collective-permute-start.2) | collective-permute-done | bytes 393248 | tf_op jit(solution)/shard_map/ppermute | solution.py:644
  82.3 2.9 collective-permute-start.3
  94.5 9.8 %attend.4 = (bf16[2048,2304]{1,0:T(8,128)(2,1)}, bf16[16,6,128,256]{3,2,1,0:T(8,128)(2,1)}, bf16[2048,768]{1,0:T(8,128)(2,1)}, bf16[2048,768]{1,0:T(8,128)(2,1)}, f32[8,128]{1,0:T(8,128)}) custom-call(s32[4]{0:T(128)} %pad_add_fusion.1.where, s32[2,16]{1,0:T(2,128)} %pad_add_fusion.live, bf16[2048,768]{1,0:T(8,128)(2,1)} %rows.7, ...), custom_call_target="tpu_custom_call" | custom-call | flops 10000000000 | bytes 30000000 | tf_op jit(solution)/shard_map/attend/pallas_call | solution.py:167
  104.3 9.6 %attend.5 = (bf16[2048,2304]{1,0:T(8,128)(2,1)}, bf16[16,6,128,256]{3,2,1,0:T(8,128)(2,1)}, bf16[2048,768]{1,0:T(8,128)(2,1)}, bf16[2048,768]{1,0:T(8,128)(2,1)}, f32[8,128]{1,0:T(8,128)}) custom-call(s32[4]{0:T(128)} %pad_add_fusion.1.where, s32[2,16]{1,0:T(2,128)} %pad_add_fusion.live, ...), custom_call_target="tpu_custom_call", output_to_operand_aliasing={{0}: (7, {}), {1}: (8, {}), {2}: (9, {}), {3}: (10, {})} | custom-call | flops 10000000000 | bytes 30000000 | tf_op jit(solution)/shard_map/attend/pallas_call | solution.py:167
  114.0 5.4 %collective-permute-done.9.far = bf16[256,768]{1,0:T(8,128)(2,1)} collective-permute-done((bf16[256,768]{1,0:T(8,128)(2,1)}, bf16[256,768]{1,0:T(8,128)(2,1)}, u32[]{:S(2)}, u32[]{:S(2)}) %collective-permute-start.9) | collective-permute-done | bytes 393248 | tf_op jit(solution)/shard_map/ppermute | solution.py:644
  119.4 9.6 %attend.6 = (bf16[2048,2304]{1,0:T(8,128)(2,1)}, bf16[16,6,128,256]{3,2,1,0:T(8,128)(2,1)}, bf16[2048,768]{1,0:T(8,128)(2,1)}, bf16[2048,768]{1,0:T(8,128)(2,1)}, f32[8,128]{1,0:T(8,128)}) custom-call(s32[4]{0:T(128)} %pad_add_fusion.1.where, s32[2,16]{1,0:T(2,128)} %pad_add_fusion.live, ...), custom_call_target="tpu_custom_call", output_to_operand_aliasing={{0}: (7, {}), {1}: (8, {}), {2}: (9, {}), {3}: (10, {})} | custom-call | flops 10000000000 | bytes 30000000 | tf_op jit(solution)/shard_map/attend/pallas_call | solution.py:167
  129.0 7.1 %collective-permute-done.16.far = bf16[256,768]{1,0:T(8,128)(2,1)} collective-permute-done((bf16[256,768]{1,0:T(8,128)(2,1)}, bf16[256,768]{1,0:T(8,128)(2,1)}, u32[]{:S(2)}, u32[]{:S(2)}) %collective-permute-start.16) | collective-permute-done | bytes 393248 | tf_op jit(solution)/shard_map/ppermute | solution.py:644
  142.3 10.0 %attend.7 = (bf16[2048,2304]{1,0:T(8,128)(2,1)}, bf16[16,6,128,256]{3,2,1,0:T(8,128)(2,1)}, bf16[2048,768]{1,0:T(8,128)(2,1)}, bf16[2048,768]{1,0:T(8,128)(2,1)}, f32[8,128]{1,0:T(8,128)}) custom-call(s32[4]{0:T(128)} %pad_add_fusion.1.where, s32[2,16]{1,0:T(2,128)} %pad_add_fusion.live, ...), custom_call_target="tpu_custom_call", output_to_operand_aliasing={{0}: (7, {}), {1}: (8, {}), {2}: (9, {}), {3}: (10, {})} | custom-call | flops 10000000000 | bytes 30000000 | tf_op jit(solution)/shard_map/attend/pallas_call | solution.py:167
  153.2 20.1 %feed.3 = (bf16[2048,768]{1,0:T(8,128)(2,1)}, bf16[2048,3072]{1,0:T(8,128)(2,1)}, bf16[2048,3072]{1,0:T(8,128)(2,1)}, bf16[2048,768]{1,0:T(8,128)(2,1)}, bf16[20...) custom-call(s32[4]{0:T(128)} %pad_add_fusion.1.where, ...), custom_call_target="tpu_custom_call" | custom-call | flops 1 | bytes 1 | tf_op jit(solution)/shard_map/feed/pallas_call | solution.py:316
  173.3 2.7 collective-permute-done.21.far
  176.8 20.1 %feed.4 = (bf16[2048,768]{1,0:T(8,128)(2,1)}, bf16[2048,3072]{1,0:T(8,128)(2,1)}, bf16[2048,3072]{1,0:T(8,128)(2,1)}, bf16[2048,768]{1,0:T(8,128)(2,1)}, bf16[20...) custom-call(s32[4]{0:T(128)} %pad_add_fusion.1.where, ...), custom_call_target="tpu_custom_call", output_to_operand_aliasing={{0}: (15, {}), {1}: (16, {}), {2}: (17, {}), {3}: (18, {}),... | custom-call | flops 1 | bytes 1 | tf_op jit(solution)/shard_map/feed/pallas_call | solution.py:316
  197.0 35.6 %feed.5 = (bf16[2048,768]{1,0:T(8,128)(2,1)}, bf16[2048,3072]{1,0:T(8,128)(2,1)}, bf16[2048,3072]{1,0:T(8,128)(2,1)}, bf16[2048,768]{1,0:T(8,128)(2,1)}, bf16[20...) custom-call(s32[4]{0:T(128)} %pad_add_fusion.1.where, ...), custom_call_target="tpu_custom_call", output_to_operand_aliasing={{0}: (15, {}), {1}: (16, {}), {2}: (17, {}), {3}: (18, {}),... | custom-call | flops 1 | bytes 1 | tf_op jit(solution)/shard_map/feed/pallas_call | solution.py:316
  232.6 2.9 collective-permute-start.23
  236.4 33.6 %wide_grads.1 = (bf16[4,4,5,48,384]{4,3,2,1,0:T(8,128)(2,1)}, bf16[4,4,5,48,384]{4,3,2,1,0:T(8,128)(2,1)}, bf16[4,4,4,48,384]{4,3,2,1,0:T(8,128)(2,1)}, bf16[4,4,4,48,384]{4,3,2,1,0:T(8,128)(2,1)}) custom-call(s32[4]{0:T(128)} %pad_add_fusion.1.where, bf16[2048,3072]{1,0:T(8,128)(2,1)} %get-tuple-element.148.dinner, ...), custom_call_target="tpu_custom_call" | custom-call | flops 1 | bytes 1 | tf_op jit(solution)/shard_map/wide_grads/pallas_call | solution.py:586
  271.5 12.8 %back.4 = (bf16[2048,2304]{1,0:T(8,128)(2,1)}, bf16[256,768]{1,0:T(8,128)(2,1)}, f32[8,768]{1,0:T(8,128)}) custom-call(s32[4]{0:T(128)} %pad_add_fusion.1.where, bf16[2048,2304]{1,0:T(8,128)(2,1)} %get-tuple-element.117.qkv_all, bf16[16,6,128,256]{3,2,1,0:T(8,128)(2,1)} %get-tuple-element.118.prob_all, ...), custom_call_target="tpu_custom_call" | custom-call | flops 1 | bytes 1 | tf_op jit(solution)/shard_map/back/pallas_call | solution.py:437
  285.9 2.3 add_convert_fusion.refs_3_
  292.4 12.5 %back.5 = (bf16[2048,2304]{1,0:T(8,128)(2,1)}, bf16[256,768]{1,0:T(8,128)(2,1)}, f32[8,768]{1,0:T(8,128)}) custom-call(s32[4]{0:T(128)} %pad_add_fusion.1.where, bf16[2048,2304]{1,0:T(8,128)(2,1)} %get-tuple-element.117.qkv_all, bf16[16,6,128,256]{3,2,1,0:T(8,128)(2,1)} %get-tuple-element.118.prob_all, ...), custom_call_target="tpu_custom_call", output_to_operand_aliasing={{0}: (7, {})} | custom-call | flops 1 | bytes 1 | tf_op jit(solution)/shard_map/back/pallas_call | solution.py:437
  305.0 2.9 collective-permute-start.29
  307.9 12.5 %back.6 = (bf16[2048,2304]{1,0:T(8,128)(2,1)}, bf16[256,768]{1,0:T(8,128)(2,1)}, f32[8,768]{1,0:T(8,128)}) custom-call(s32[4]{0:T(128)} %pad_add_fusion.1.where, bf16[2048,2304]{1,0:T(8,128)(2,1)} %get-tuple-element.117.qkv_all, bf16[16,6,128,256]{3,2,1,0:T(8,128)(2,1)} %get-tuple-element.118.prob_all, ...), custom_call_target="tpu_custom_call", output_to_operand_aliasing={{0}: (7, {})} | custom-call | flops 1 | bytes 1 | tf_op jit(solution)/shard_map/back/pallas_call | solution.py:437
  330.8 12.5 %back.7 = (bf16[2048,2304]{1,0:T(8,128)(2,1)}, bf16[256,768]{1,0:T(8,128)(2,1)}, f32[8,768]{1,0:T(8,128)}) custom-call(s32[4]{0:T(128)} %pad_add_fusion.1.where, bf16[2048,2304]{1,0:T(8,128)(2,1)} %get-tuple-element.117.qkv_all, bf16[16,6,128,256]{3,2,1,0:T(8,128)(2,1)} %get-tuple-element.118.prob_all, ...), custom_call_target="tpu_custom_call", output_to_operand_aliasing={{0}: (7, {})} | custom-call | flops 1 | bytes 1 | tf_op jit(solution)/shard_map/back/pallas_call | solution.py:437
  349.2 2.2 collective-permute-start.33
  353.0 13.7 %proj_grads.1 = (bf16[4,4,160,384]{3,2,1,0:T(8,128)(2,1)}, bf16[4,4,160,384]{3,2,1,0:T(8,128)(2,1)}) custom-call(s32[4]{0:T(128)} %pad_add_fusion.1.where, bf16[2048,2304]{1,0:T(8,128)(2,1)} %get-tuple-element.172.dqkv.dqkv_all, bf16[2048,768]{1,0:T(8,128)(2,1)} %get-tuple-element.120.x_all.x, bf16[16,16,768]{2,1,0:T(8,128)(2,1)} %convert_element_type.252.tiny, ...), custom_call_target="tpu_custom_call" | custom-call | flops 1 | bytes 1 | tf_op jit(solution)/shard_map/proj_grads/pallas_call | solution.py:620
  370.0 2.3 collective-permute-start.36
  377.9 17.6 %collective-permute-done.39 = bf16[1,1,9,48,384]{4,3,2,1,0:T(8,128)(2,1)S(1)} collective-permute-done((bf16[1,1,9,48,384]{4,3,2,1,0:T(8,128)(2,1)S(1)}, bf16[1,1,9,48,384]{4,3,2,1,0:T(8,128)(2,1)S(1)}, u32[]{:S(2)}, u32[]{:S(2)}) %collective-permute-start.39) | collective-permute-done | bytes 331808 | tf_op jit(solution)/shard_map/ppermute | solution.py:644
  404.3 10.4 %finish.1 = (f32[2048,768]{1,0:T(8,128)}, bf16[2048,768]{1,0:T(8,128)(2,1)}) custom-call(s32[4]{0:T(128)} %pad_add_fusion.1.where, bf16[2048,2304]{1,0:T(8,128)(2,1)} %get-tuple-element.172.dqkv.dqkv_all, bf16[2048,768]{1,0:T(8,128)(2,1)} %get-tuple-element.145.dbranch_all.dbranch, ...), custom_call_target="tpu_custom_call", output_to_operand_aliasing={{1}: (5, {})} | custom-call | flops 1 | bytes 1 | tf_op jit(solution)/shard_map/finish/pallas_call | solution.py:502
  (223 shorter events, 81.9 us)
Async XLA Ops:
  13.2 34.9 %collective-permute-start.1 = (bf16[488,768]{1,0:T(8,128)(2,1)S(1)}, bf16[488,768]{1,0:T(8,128)(2,1)S(1)}, u32[]{:S(2)}, u32[]{:S(2)}) collective-permute-start(bf16[488,768]{1,0:T(8,128)(2,1)S(1)} %fusion.5), channel_id=1, source_target_pairs={{0,16},{2,18},{4,20},{6,22},{8,24},{10,26},{12,28},{14,30},{16,0},... | collective-permute-start | bytes 2248712 | tf_op jit(solution)/shard_map/ppermute | solution.py:644
  13.4 20.9 %collective-permute-start.4 = (bf16[2,160,384]{2,1,0:T(8,128)(2,1)S(1)}, bf16[2,160,384]{2,1,0:T(8,128)(2,1)S(1)}, u32[]{:S(2)}, u32[]{:S(2)}) collective-permute-start(bf16[2,160,384]{2,1,0:T(8,128)(2,1)S(1)} %pad_maximum_fusion.10), channel_id=1, source_target_pairs={{0,8},{2,10},{4,12},{6,14},{8,0},{10,2},{12,4},{14,6},{16,24},{18,... | collective-permute-start | bytes 737288 | tf_op jit(solution)/shard_map/ppermute | solution.py:644
  35.8 21.7 %collective-permute-start.6 = (bf16[4,160,384]{2,1,0:T(8,128)(2,1)S(1)}, bf16[4,160,384]{2,1,0:T(8,128)(2,1)S(1)}, u32[]{:S(2)}, u32[]{:S(2)}) collective-permute-start(bf16[4,160,384]{2,1,0:T(8,128)(2,1)S(1)} %bitcast.156), channel_id=1, source_target_pairs={{0,4},{1,5},{2,6},{3,7},{4,0},{5,1},{6,2},{7,3},{8,12},{9,13},{10,... | collective-permute-start | bytes 1474568 | tf_op jit(solution)/shard_map/ppermute | solution.py:651
  37.3 20.2 %collective-permute-start.7 = (bf16[4,160,384]{2,1,0:T(8,128)(2,1)S(1)}, bf16[4,160,384]{2,1,0:T(8,128)(2,1)S(1)}, u32[]{:S(2)}, u32[]{:S(2)}) collective-permute-start(bf16[4,160,384]{2,1,0:T(8,128)(2,1)S(1)} %bitcast.157), channel_id=1, source_target_pairs={{0,5},{1,4},{2,7},{3,6},{4,1},{5,0},{6,3},{7,2},{8,13},{9,12},{10,... | collective-permute-start | bytes 1474568 | tf_op jit(solution)/shard_map/ppermute | solution.py:651
  57.8 33.5 %collective-permute-start.8 = (bf16[4,4,160,384]{3,2,1,0:T(8,128)(2,1)S(1)}, bf16[4,4,160,384]{3,2,1,0:T(8,128)(2,1)}, u32[]{:S(2)}, u32[]{:S(2)}) collective-permute-start(bf16[4,4,160,384]{3,2,1,0:T(8,128)(2,1)S(1)} %pad_maximum_fusion.1.refs_0_), channel_id=1, source_target_pairs={{0,2},{1,3},{2,0},{3,1},{4,6},{5,7},{6,4},{7,5},{8,10},{9,11},{10,... | collective-permute-start | bytes 5898248 | tf_op jit(solution)/shard_map/ppermute | solution.py:651
  57.9 24.4 %collective-permute-start.2 = (bf16[256,768]{1,0:T(8,128)(2,1)}, bf16[256,768]{1,0:T(8,128)(2,1)}, u32[]{:S(2)}, u32[]{:S(2)}) collective-permute-start(bf16[256,768]{1,0:T(8,128)(2,1)} %get-tuple-element.202), channel_id=1, source_target_pairs={{0,16},{2,18},{4,20},{6,22},{8,24},{10,26},{12,28},{14,30},{16,0},... | collective-permute-start | bytes 1179656 | tf_op jit(solution)/shard_map/ppermute | solution.py:644
  66.2 22.4 %collective-permute-start.12 = (bf16[4,5,48,384]{3,2,1,0:T(8,128)(2,1)}, bf16[4,5,48,384]{3,2,1,0:T(8,128)(2,1)S(1)}, u32[]{:S(2)}, u32[]{:S(2)}) collective-permute-start(bf16[4,5,48,384]{3,2,1,0:T(8,128)(2,1)} %get-tuple-element.208), channel_id=1, source_target_pairs={{0,1},{1,0},{2,3},{3,2},{4,5},{5,4},{6,7},{7,6},{8,9},{9,8},{10,11... | collective-permute-start | bytes 2211848 | tf_op jit(solution)/shard_map/ppermute | solution.py:651
  68.4 18.1 %collective-permute-start.14 = (bf16[4,4,48,384]{3,2,1,0:T(8,128)(2,1)}, bf16[4,4,48,384]{3,2,1,0:T(8,128)(2,1)}, u32[]{:S(2)}, u32[]{:S(2)}) collective-permute-start(bf16[4,4,48,384]{3,2,1,0:T(8,128)(2,1)} %get-tuple-element.206), channel_id=1, source_target_pairs={{0,4},{1,5},{2,6},{3,7},{4,0},{5,1},{6,2},{7,3},{8,12},{9,13},{10,... | collective-permute-start | bytes 1769480 | tf_op jit(solution)/shard_map/ppermute | solution.py:651
  82.2 37.1 %collective-permute-start.9 = (bf16[256,768]{1,0:T(8,128)(2,1)}, bf16[256,768]{1,0:T(8,128)(2,1)}, u32[]{:S(2)}, u32[]{:S(2)}) collective-permute-start(bf16[256,768]{1,0:T(8,128)(2,1)} %get-tuple-element.104), channel_id=1, source_target_pairs={{0,16},{2,18},{4,20},{6,22},{8,24},{10,26},{12,28},{14,30},{16,0},... | collective-permute-start | bytes 1179656 | tf_op jit(solution)/shard_map/ppermute | solution.py:644
  82.3 46.8 %collective-permute-start.3 = (bf16[256,768]{1,0:T(8,128)(2,1)}, bf16[256,768]{1,0:T(8,128)(2,1)}, u32[]{:S(2)}, u32[]{:S(2)}) collective-permute-start(bf16[256,768]{1,0:T(8,128)(2,1)} %get-tuple-element.103), channel_id=1, source_target_pairs={{0,16},{2,18},{4,20},{6,22},{8,24},{10,26},{12,28},{14,30},{16,0},... | collective-permute-start | bytes 1179656 | tf_op jit(solution)/shard_map/ppermute | solution.py:644
  86.5 49.7 %collective-permute-start.16 = (bf16[256,768]{1,0:T(8,128)(2,1)}, bf16[256,768]{1,0:T(8,128)(2,1)}, u32[]{:S(2)}, u32[]{:S(2)}) collective-permute-start(bf16[256,768]{1,0:T(8,128)(2,1)} %get-tuple-element.123), channel_id=1, source_target_pairs={{0,16},{2,18},{4,20},{6,22},{8,24},{10,26},{12,28},{14,30},{16,0},... | collective-permute-start | bytes 1179656 | tf_op jit(solution)/shard_map/ppermute | solution.py:644
  88.7 47.5 %collective-permute-start.15 = (bf16[2,4,4,48,384]{4,3,2,1,0:T(8,128)(2,1)}, bf16[2,4,4,48,384]{4,3,2,1,0:T(8,128)(2,1)}, u32[]{:S(2)}, u32[]{:S(2)}) collective-permute-start(bf16[2,4,4,48,384]{4,3,2,1,0:T(8,128)(2,1)} %pad_maximum_fusion.4.refs_2_), channel_id=1, source_target_pairs={{0,1},{1,0},{2,3},{3,2},{4,5},{5,4},{6,7},{7,6},{8,9},{9,8},{10,11... | collective-permute-start | bytes 3538952 | tf_op jit(solution)/shard_map/ppermute | solution.py:651
  91.3 44.9 %collective-permute-start.13 = (bf16[2,4,5,48,384]{4,3,2,1,0:T(8,128)(2,1)S(1)}, bf16[2,4,5,48,384]{4,3,2,1,0:T(8,128)(2,1)S(1)}, u32[]{:S(2)}, u32[]{:S(2)}) collective-permute-start(bf16[2,4,5,48,384]{4,3,2,1,0:T(8,128)(2,1)S(1)} %pad_maximum_fusion.2.refs_0_), channel_id=1, source_target_pairs={{0,4},{1,5},{2,6},{3,7},{4,0},{5,1},{6,2},{7,3},{8,12},{9,13},{10,... | collective-permute-start | bytes 4423688 | tf_op jit(solution)/shard_map/ppermute | solution.py:651
  136.3 16.9 %collective-permute-start.17 = (bf16[2,4,5,48,384]{4,3,2,1,0:T(8,128)(2,1)S(1)}, bf16[2,4,5,48,384]{4,3,2,1,0:T(8,128)(2,1)}, u32[]{:S(2)}, u32[]{:S(2)}) collective-permute-start(bf16[2,4,5,48,384]{4,3,2,1,0:T(8,128)(2,1)S(1)} %pad_maximum_fusion.2.refs_0_), channel_id=1, source_target_pairs={{0,2},{1,3},{2,0},{3,1},{4,6},{5,7},{6,4},{7,5},{8,10},{9,11},{10,... | collective-permute-start | bytes 4423688 | tf_op jit(solution)/shard_map/ppermute | solution.py:651
  136.7 16.4 %collective-permute-start.18 = (bf16[2,4,5,48,384]{4,3,2,1,0:T(8,128)(2,1)S(1)}, bf16[2,4,5,48,384]{4,3,2,1,0:T(8,128)(2,1)}, u32[]{:S(2)}, u32[]{:S(2)}) collective-permute-start(bf16[2,4,5,48,384]{4,3,2,1,0:T(8,128)(2,1)S(1)} %collective-permute-done.13.refs_1_), channel_id=1, source_target_pairs={{0,2},{1,3},{2,0},{3,1},{4,6},{5,7},{6,4},{7,5},{8,10},{9,11},{10,... | collective-permute-start | bytes 4423688 | tf_op jit(solution)/shard_map/ppermute | solution.py:651
  139.3 36.7 %collective-permute-start.21 = (bf16[256,768]{1,0:T(8,128)(2,1)}, bf16[256,768]{1,0:T(8,128)(2,1)S(1)}, u32[]{:S(2)}, u32[]{:S(2)}) collective-permute-start(bf16[256,768]{1,0:T(8,128)(2,1)} %get-tuple-element.128), channel_id=1, source_target_pairs={{0,16},{2,18},{4,20},{6,22},{8,24},{10,26},{12,28},{14,30},{16,0},... | collective-permute-start | bytes 1179656 | tf_op jit(solution)/shard_map/ppermute | solution.py:644
  140.2 56.8 %collective-permute-start.10 = (bf16[512,768]{1,0:T(8,128)(2,1)}, bf16[512,768]{1,0:T(8,128)(2,1)}, u32[]{:S(2)}, u32[]{:S(2)}) collective-permute-start(bf16[512,768]{1,0:T(8,128)(2,1)} %constant_dynamic-slice_fusion.2), channel_id=1, source_target_pairs={{0,16},{2,18},{4,20},{6,22},{8,24},{10,26},{12,28},{14,30},{16,0},... | collective-permute-start | bytes 2359304 | tf_op jit(solution)/shard_map/ppermute | solution.py:644
  196.9 38.6 %collective-permute-start.22 = (bf16[512,768]{1,0:T(8,128)(2,1)}, bf16[512,768]{1,0:T(8,128)(2,1)S(1)}, u32[]{:S(2)}, u32[]{:S(2)}) collective-permute-start(bf16[512,768]{1,0:T(8,128)(2,1)} %get-tuple-element.152), channel_id=1, source_target_pairs={{0,16},{2,18},{4,20},{6,22},{8,24},{10,26},{12,28},{14,30},{16,0},... | collective-permute-start | bytes 2359304 | tf_op jit(solution)/shard_map/ppermute | solution.py:644
  232.6 37.5 %collective-permute-start.23 = (bf16[512,768]{1,0:T(8,128)(2,1)}, bf16[512,768]{1,0:T(8,128)(2,1)S(1)}, u32[]{:S(2)}, u32[]{:S(2)}) collective-permute-start(bf16[512,768]{1,0:T(8,128)(2,1)} %get-tuple-element.157), channel_id=1, source_target_pairs={{0,16},{2,18},{4,20},{6,22},{8,24},{10,26},{12,28},{14,30},{16,0},... | collective-permute-start | bytes 2359304 | tf_op jit(solution)/shard_map/ppermute | solution.py:644
  288.2 34.4 %collective-permute-start.26 = (bf16[2,4,5,48,384]{4,3,2,1,0:T(8,128)(2,1)S(1)}, bf16[2,4,5,48,384]{4,3,2,1,0:T(8,128)(2,1)}, u32[]{:S(2)}, u32[]{:S(2)}) collective-permute-start(bf16[2,4,5,48,384]{4,3,2,1,0:T(8,128)(2,1)S(1)} %add_convert_fusion.refs_3_), channel_id=1, source_target_pairs={{0,4},{1,5},{2,6},{3,7},{4,0},{5,1},{6,2},{7,3},{8,12},{9,13},{10,... | collective-permute-start | bytes 4423688 | tf_op jit(solution)/shard_map/ppermute | solution.py:651
  291.2 29.2 %collective-permute-start.27 = (bf16[2,4,4,48,384]{4,3,2,1,0:T(8,128)(2,1)S(1)}, bf16[2,4,4,48,384]{4,3,2,1,0:T(8,128)(2,1)}, u32[]{:S(2)}, u32[]{:S(2)}) collective-permute-start(bf16[2,4,4,48,384]{4,3,2,1,0:T(8,128)(2,1)S(1)} %add_convert_fusion.1.refs_4_), channel_id=1, source_target_pairs={{0,1},{1,0},{2,3},{3,2},{4,5},{5,4},{6,7},{7,6},{8,9},{9,8},{10,11... | collective-permute-start | bytes 3538952 | tf_op jit(solution)/shard_map/ppermute | solution.py:651
  292.4 37.4 %collective-permute-start.28 = (bf16[256,768]{1,0:T(8,128)(2,1)}, bf16[256,768]{1,0:T(8,128)(2,1)S(1)}, u32[]{:S(2)}, u32[]{:S(2)}) collective-permute-start(bf16[256,768]{1,0:T(8,128)(2,1)} %get-tuple-element.170), channel_id=1, source_target_pairs={{0,16},{2,18},{4,20},{6,22},{8,24},{10,26},{12,28},{14,30},{16,0},... | collective-permute-start | bytes 1179656 | tf_op jit(solution)/shard_map/ppermute | solution.py:644
  305.0 24.8 %collective-permute-start.29 = (bf16[256,768]{1,0:T(8,128)(2,1)}, bf16[256,768]{1,0:T(8,128)(2,1)S(1)}, u32[]{:S(2)}, u32[]{:S(2)}) collective-permute-start(bf16[256,768]{1,0:T(8,128)(2,1)} %get-tuple-element.171), channel_id=1, source_target_pairs={{0,16},{2,18},{4,20},{6,22},{8,24},{10,26},{12,28},{14,30},{16,0},... | collective-permute-start | bytes 1179656 | tf_op jit(solution)/shard_map/ppermute | solution.py:644
  324.5 19.9 %collective-permute-start.31 = (bf16[4,5,48,384]{3,2,1,0:T(8,128)(2,1)S(1)}, bf16[4,5,48,384]{3,2,1,0:T(8,128)(2,1)S(1)}, u32[]{:S(2)}, u32[]{:S(2)}) collective-permute-start(bf16[4,5,48,384]{3,2,1,0:T(8,128)(2,1)S(1)} %fusion.6.refs_3_), channel_id=1, source_target_pairs={{0,1},{1,0},{2,3},{3,2},{4,5},{5,4},{6,7},{7,6},{8,9},{9,8},{10,11... | collective-permute-start | bytes 2211848 | tf_op jit(solution)/shard_map/ppermute | solution.py:651
  327.4 16.9 %collective-permute-start.32 = (bf16[4,4,48,384]{3,2,1,0:T(8,128)(2,1)S(1)}, bf16[4,4,48,384]{3,2,1,0:T(8,128)(2,1)S(1)}, u32[]{:S(2)}, u32[]{:S(2)}) collective-permute-start(bf16[4,4,48,384]{3,2,1,0:T(8,128)(2,1)S(1)} %fusion.7.refs_4_), channel_id=1, source_target_pairs={{0,4},{1,5},{2,6},{3,7},{4,0},{5,1},{6,2},{7,3},{8,12},{9,13},{10,... | collective-permute-start | bytes 1769480 | tf_op jit(solution)/shard_map/ppermute | solution.py:651
  329.8 37.0 %collective-permute-start.30 = (bf16[256,768]{1,0:T(8,128)(2,1)}, bf16[256,768]{1,0:T(8,128)(2,1)}, u32[]{:S(2)}, u32[]{:S(2)}) collective-permute-start(bf16[256,768]{1,0:T(8,128)(2,1)} %get-tuple-element.174), channel_id=1, source_target_pairs={{0,16},{2,18},{4,20},{6,22},{8,24},{10,26},{12,28},{14,30},{16,0},... | collective-permute-start | bytes 1179656 | tf_op jit(solution)/shard_map/ppermute | solution.py:644
  349.2 17.6 %collective-permute-start.33 = (bf16[2,1,9,48,384]{4,3,2,1,0:T(8,128)(2,1)}, bf16[2,1,9,48,384]{4,3,2,1,0:T(8,128)(2,1)}, u32[]{:S(2)}, u32[]{:S(2)}) collective-permute-start(bf16[2,1,9,48,384]{4,3,2,1,0:T(8,128)(2,1)} %dynamic-slice_convert_fusion), channel_id=1, source_target_pairs={{0,8},{2,10},{4,12},{6,14},{8,0},{10,2},{12,4},{14,6},{16,24},{18,... | collective-permute-start | bytes 1990664 | tf_op jit(solution)/shard_map/ppermute | solution.py:644
  369.2 26.3 %collective-permute-start.39 = (bf16[1,1,9,48,384]{4,3,2,1,0:T(8,128)(2,1)S(1)}, bf16[1,1,9,48,384]{4,3,2,1,0:T(8,128)(2,1)S(1)}, u32[]{:S(2)}, u32[]{:S(2)}) collective-permute-start(bf16[1,1,9,48,384]{4,3,2,1,0:T(8,128)(2,1)S(1)} %dynamic-slice_convert_fusion.1), channel_id=1, source_target_pairs={{0,16},{2,18},{4,20},{6,22},{8,24},{10,26},{12,28},{14,30},{16,0},... | collective-permute-start | bytes 995336 | tf_op jit(solution)/shard_map/ppermute | solution.py:644
  370.0 44.7 %collective-permute-start.36 = (bf16[256,768]{1,0:T(8,128)(2,1)S(1)}, bf16[256,768]{1,0:T(8,128)(2,1)S(1)}, u32[]{:S(2)}, u32[]{:S(2)}) collective-permute-start(bf16[256,768]{1,0:T(8,128)(2,1)S(1)} %copy-done.31), channel_id=1, source_target_pairs={{0,16},{2,18},{4,20},{6,22},{8,24},{10,26},{12,28},{14,30},{16,0},... | collective-permute-start | bytes 1179656 | tf_op jit(solution)/shard_map/ppermute | solution.py:644
  374.4 23.4 %collective-permute-start.35 = (bf16[4,160,384]{2,1,0:T(8,128)(2,1)S(1)}, bf16[4,160,384]{2,1,0:T(8,128)(2,1)S(1)}, u32[]{:S(2)}, u32[]{:S(2)}) collective-permute-start(bf16[4,160,384]{2,1,0:T(8,128)(2,1)S(1)} %get-tuple-element.189), channel_id=1, source_target_pairs={{0,1},{1,0},{2,3},{3,2},{4,5},{5,4},{6,7},{7,6},{8,9},{9,8},{10,11... | collective-permute-start | bytes 1474568 | tf_op jit(solution)/shard_map/ppermute | solution.py:651
  375.9 23.3 %collective-permute-start.37 = (bf16[4,160,384]{2,1,0:T(8,128)(2,1)S(1)}, bf16[4,160,384]{2,1,0:T(8,128)(2,1)S(1)}, u32[]{:S(2)}, u32[]{:S(2)}) collective-permute-start(bf16[4,160,384]{2,1,0:T(8,128)(2,1)S(1)} %get-tuple-element.193), channel_id=1, source_target_pairs={{0,4},{1,5},{2,6},{3,7},{4,0},{5,1},{6,2},{7,3},{8,12},{9,13},{10,... | collective-permute-start | bytes 1474568 | tf_op jit(solution)/shard_map/ppermute | solution.py:651
  376.4 22.8 %collective-permute-start.38 = (bf16[4,160,384]{2,1,0:T(8,128)(2,1)S(1)}, bf16[4,160,384]{2,1,0:T(8,128)(2,1)S(1)}, u32[]{:S(2)}, u32[]{:S(2)}) collective-permute-start(bf16[4,160,384]{2,1,0:T(8,128)(2,1)S(1)} %get-tuple-element.194), channel_id=1, source_target_pairs={{0,5},{1,4},{2,7},{3,6},{4,1},{5,0},{6,3},{7,2},{8,13},{9,12},{10,... | collective-permute-start | bytes 1474568 | tf_op jit(solution)/shard_map/ppermute | solution.py:651
  (43 other events, 420.8 us)

commit v5 on v4

--- a/solution.py
+++ b/solution.py
@@ -734,7 +734,7 @@
     away = low(lax.dynamic_slice_in_dim(held, (1 - mine) * size, size, dim))
     stay = lax.dynamic_slice_in_dim(held, mine * size, size, dim)
     got = swapped(away, axis, 1 << bit)
-    return stay + wide(got), got
+    return wide(stay) + wide(got), got
 
 
 def reduce_wide(keep_one, send_one, keep_two, send_two):
@@ -753,7 +753,7 @@
     last_one, last_two = after(last, gate)
     held_one = wide(keep_one[0]) + wide(came_one[0]) + wide(back_one[0]) + wide(last_one)
     held_two = wide(keep_two[0]) + wide(came_two[0]) + wide(back_two[0]) + wide(last_two)
-    held = jnp.concatenate([held_one, held_two], 1)
+    held = jnp.concatenate([low(held_one), low(held_two)], 1)
     yield [held]
     yield from reduce_far(held)
 

time: 424 us -> 422 us (level)
    convert_element_type x5 -> x7, other arithmetic: 9.55 us -> 13.2 us  [low(): return values.astype(BF)]
  transfers between devices with their start and end apart: 43 -> 43, of which waited for: 12 -> 12; matrix products, arithmetic and copies ran while one was open for 10% -> 10% of each run, Pallas kernels for 53% -> 54%
where the time goes in v5:
time: 422 us; the launch traced here: 416 us
  Pallas kernels  223 us (53%)
  waiting for transfers between devices  84.6 us (20%)
  starting transfers between devices  53.6 us (13%)
  other arithmetic  27.5 us (7%)
  local copies, waits for them, and re-layouts  25.9 us (6%)
    pallas_call x3, Pallas kernels, feed(): pl.pallas_call(functools.partial(feed_kernel, c0, subs, skip, sides), out...  75.8 us
    ppermute x21, waiting for transfers between devices, swapped(): lax.ppermute(values, axis, [(i, i ^ mask) for i in range(lax.axis_size(ax...  71.3 us
    pallas_call x4, Pallas kernels, back(): pl.pallas_call(functools.partial(back_kernel, c0, skip), out_shape=(S((to...  50.4 us
    pallas_call x4, Pallas kernels, attend(): pl.pallas_call(functools.partial(attend_kernel, c, skip), out_shape=shape...  39.1 us
    ppermute x21, starting transfers between devices, swapped(): lax.ppermute(values, axis, [(i, i ^ mask) for i in range(lax.axis_size(ax...  35 us
    pallas_call x1, Pallas kernels, wide_grads(): pl.pallas_call(functools.partial(wide_grads_kernel, sides), grid=(BLOCKS,...  33.6 us
    ppermute x22, starting transfers between devices, across(): lax.ppermute(values, ('mod', 'pair'), [(i, i ^ mask) for i in range(count)])  18.6 us
    pallas_call x1, Pallas kernels, proj_grads(): pl.pallas_call(proj_grads_kernel, grid=(2,), out_shape=(S(shape, BF),) *...  13.8 us
  transfers between devices with their start and end apart: 43, of which 12 were waited for; matrix products, arithmetic and copies ran while one was open for 10% of the time, Pallas kernels for 54%

profile of v5, /device:TPU:0, one launch (start us, length us, event | category | flops | bytes accessed | tf_op | source)
XLA Modules:
  0.0 416.4 jit_solution(12059590593122773153)
XLA Ops:
  3.2 4.1 collective-permute-start
  9.3 2.5 constant_dynamic-slice_fusion.4
  13.4 4.1 collective-permute-start.4
  17.5 16.8 %collective-permute-done.4 = bf16[2,160,384]{2,1,0:T(8,128)(2,1)S(1)} collective-permute-done((bf16[2,160,384]{2,1,0:T(8,128)(2,1)S(1)}, bf16[2,160,384]{2,1,0:T(8,128)(2,1)S(1)}, u32[]{:S(2)}, u32[]{:S(2)}) %collective-permute-start.4) | collective-permute-done | bytes 245792 | tf_op jit(solution)/shard_map/ppermute | solution.py:644
  38.0 10.1 %collective-permute-done.1.far = bf16[488,768]{1,0:T(8,128)(2,1)S(1)} collective-permute-done((bf16[488,768]{1,0:T(8,128)(2,1)S(1)}, bf16[488,768]{1,0:T(8,128)(2,1)S(1)}, u32[]{:S(2)}, u32[]{:S(2)}) %collective-permute-start.1) | collective-permute-done | bytes 749600 | tf_op jit(solution)/shard_map/ppermute | solution.py:644
  49.0 8.4 %collective-permute-done.6 = bf16[4,160,384]{2,1,0:T(8,128)(2,1)S(1)} collective-permute-done((bf16[4,160,384]{2,1,0:T(8,128)(2,1)S(1)}, bf16[4,160,384]{2,1,0:T(8,128)(2,1)S(1)}, u32[]{:S(2)}, u32[]{:S(2)}) %collective-permute-start.6) | collective-permute-done | bytes 491552 | tf_op jit(solution)/shard_map/ppermute | solution.py:651
  57.9 6.8 %collective-permute-start.2 = (bf16[256,768]{1,0:T(8,128)(2,1)}, bf16[256,768]{1,0:T(8,128)(2,1)}, u32[]{:S(2)}, u32[]{:S(2)}) collective-permute-start(bf16[256,768]{1,0:T(8,128)(2,1)} %get-tuple-element.202), channel_id=1, source_target_pairs={{0,16},{2,18},{4,20},{6,22},{8,24},{10,26},{12,28},{14,30},{16,0},... | collective-permute-start | bytes 1179656 | tf_op jit(solution)/shard_map/ppermute | solution.py:644
  72.0 10.2 %collective-permute-done.2.far = bf16[256,768]{1,0:T(8,128)(2,1)} collective-permute-done((bf16[256,768]{1,0:T(8,128)(2,1)}, bf16[256,768]{1,0:T(8,128)(2,1)}, u32[]{:S(2)}, u32[]{:S(2)}) %collective-permute-start.2) | collective-permute-done | bytes 393248 | tf_op jit(solution)/shard_map/ppermute | solution.py:644
  82.3 2.9 collective-permute-start.3
  94.5 9.8 %attend.4 = (bf16[2048,2304]{1,0:T(8,128)(2,1)}, bf16[16,6,128,256]{3,2,1,0:T(8,128)(2,1)}, bf16[2048,768]{1,0:T(8,128)(2,1)}, bf16[2048,768]{1,0:T(8,128)(2,1)}, f32[8,128]{1,0:T(8,128)}) custom-call(s32[4]{0:T(128)} %pad_add_fusion.1.where, s32[2,16]{1,0:T(2,128)} %pad_add_fusion.live, bf16[2048,768]{1,0:T(8,128)(2,1)} %rows.7, ...), custom_call_target="tpu_custom_call" | custom-call | flops 10000000000 | bytes 30000000 | tf_op jit(solution)/shard_map/attend/pallas_call | solution.py:167
  104.3 9.6 %attend.5 = (bf16[2048,2304]{1,0:T(8,128)(2,1)}, bf16[16,6,128,256]{3,2,1,0:T(8,128)(2,1)}, bf16[2048,768]{1,0:T(8,128)(2,1)}, bf16[2048,768]{1,0:T(8,128)(2,1)}, f32[8,128]{1,0:T(8,128)}) custom-call(s32[4]{0:T(128)} %pad_add_fusion.1.where, s32[2,16]{1,0:T(2,128)} %pad_add_fusion.live, ...), custom_call_target="tpu_custom_call", output_to_operand_aliasing={{0}: (7, {}), {1}: (8, {}), {2}: (9, {}), {3}: (10, {})} | custom-call | flops 10000000000 | bytes 30000000 | tf_op jit(solution)/shard_map/attend/pallas_call | solution.py:167
  114.0 5.4 %collective-permute-done.9.far = bf16[256,768]{1,0:T(8,128)(2,1)} collective-permute-done((bf16[256,768]{1,0:T(8,128)(2,1)}, bf16[256,768]{1,0:T(8,128)(2,1)}, u32[]{:S(2)}, u32[]{:S(2)}) %collective-permute-start.9) | collective-permute-done | bytes 393248 | tf_op jit(solution)/shard_map/ppermute | solution.py:644
  119.4 9.6 %attend.6 = (bf16[2048,2304]{1,0:T(8,128)(2,1)}, bf16[16,6,128,256]{3,2,1,0:T(8,128)(2,1)}, bf16[2048,768]{1,0:T(8,128)(2,1)}, bf16[2048,768]{1,0:T(8,128)(2,1)}, f32[8,128]{1,0:T(8,128)}) custom-call(s32[4]{0:T(128)} %pad_add_fusion.1.where, s32[2,16]{1,0:T(2,128)} %pad_add_fusion.live, ...), custom_call_target="tpu_custom_call", output_to_operand_aliasing={{0}: (7, {}), {1}: (8, {}), {2}: (9, {}), {3}: (10, {})} | custom-call | flops 10000000000 | bytes 30000000 | tf_op jit(solution)/shard_map/attend/pallas_call | solution.py:167
  129.0 7.1 %collective-permute-done.16.far = bf16[256,768]{1,0:T(8,128)(2,1)} collective-permute-done((bf16[256,768]{1,0:T(8,128)(2,1)}, bf16[256,768]{1,0:T(8,128)(2,1)}, u32[]{:S(2)}, u32[]{:S(2)}) %collective-permute-start.16) | collective-permute-done | bytes 393248 | tf_op jit(solution)/shard_map/ppermute | solution.py:644
  142.2 10.0 %attend.7 = (bf16[2048,2304]{1,0:T(8,128)(2,1)}, bf16[16,6,128,256]{3,2,1,0:T(8,128)(2,1)}, bf16[2048,768]{1,0:T(8,128)(2,1)}, bf16[2048,768]{1,0:T(8,128)(2,1)}, f32[8,128]{1,0:T(8,128)}) custom-call(s32[4]{0:T(128)} %pad_add_fusion.1.where, s32[2,16]{1,0:T(2,128)} %pad_add_fusion.live, ...), custom_call_target="tpu_custom_call", output_to_operand_aliasing={{0}: (7, {}), {1}: (8, {}), {2}: (9, {}), {3}: (10, {})} | custom-call | flops 10000000000 | bytes 30000000 | tf_op jit(solution)/shard_map/attend/pallas_call | solution.py:167
  153.2 20.1 %feed.3 = (bf16[2048,768]{1,0:T(8,128)(2,1)}, bf16[2048,3072]{1,0:T(8,128)(2,1)}, bf16[2048,3072]{1,0:T(8,128)(2,1)}, bf16[2048,768]{1,0:T(8,128)(2,1)}, bf16[20...) custom-call(s32[4]{0:T(128)} %pad_add_fusion.1.where, ...), custom_call_target="tpu_custom_call" | custom-call | flops 1 | bytes 1 | tf_op jit(solution)/shard_map/feed/pallas_call | solution.py:316
  173.3 2.7 collective-permute-done.21.far
  176.7 20.1 %feed.4 = (bf16[2048,768]{1,0:T(8,128)(2,1)}, bf16[2048,3072]{1,0:T(8,128)(2,1)}, bf16[2048,3072]{1,0:T(8,128)(2,1)}, bf16[2048,768]{1,0:T(8,128)(2,1)}, bf16[20...) custom-call(s32[4]{0:T(128)} %pad_add_fusion.1.where, ...), custom_call_target="tpu_custom_call", output_to_operand_aliasing={{0}: (15, {}), {1}: (16, {}), {2}: (17, {}), {3}: (18, {}),... | custom-call | flops 1 | bytes 1 | tf_op jit(solution)/shard_map/feed/pallas_call | solution.py:316
  196.9 35.6 %feed.5 = (bf16[2048,768]{1,0:T(8,128)(2,1)}, bf16[2048,3072]{1,0:T(8,128)(2,1)}, bf16[2048,3072]{1,0:T(8,128)(2,1)}, bf16[2048,768]{1,0:T(8,128)(2,1)}, bf16[20...) custom-call(s32[4]{0:T(128)} %pad_add_fusion.1.where, ...), custom_call_target="tpu_custom_call", output_to_operand_aliasing={{0}: (15, {}), {1}: (16, {}), {2}: (17, {}), {3}: (18, {}),... | custom-call | flops 1 | bytes 1 | tf_op jit(solution)/shard_map/feed/pallas_call | solution.py:316
  232.6 2.9 collective-permute-start.23
  236.4 33.6 %wide_grads.1 = (bf16[4,4,5,48,384]{4,3,2,1,0:T(8,128)(2,1)}, bf16[4,4,5,48,384]{4,3,2,1,0:T(8,128)(2,1)}, bf16[4,4,4,48,384]{4,3,2,1,0:T(8,128)(2,1)}, bf16[4,4,4,48,384]{4,3,2,1,0:T(8,128)(2,1)}) custom-call(s32[4]{0:T(128)} %pad_add_fusion.1.where, bf16[2048,3072]{1,0:T(8,128)(2,1)} %get-tuple-element.148.dinner, ...), custom_call_target="tpu_custom_call" | custom-call | flops 1 | bytes 1 | tf_op jit(solution)/shard_map/wide_grads/pallas_call | solution.py:586
  271.4 12.8 %back.4 = (bf16[2048,2304]{1,0:T(8,128)(2,1)}, bf16[256,768]{1,0:T(8,128)(2,1)}, f32[8,768]{1,0:T(8,128)}) custom-call(s32[4]{0:T(128)} %pad_add_fusion.1.where, bf16[2048,2304]{1,0:T(8,128)(2,1)} %get-tuple-element.117.qkv_all, bf16[16,6,128,256]{3,2,1,0:T(8,128)(2,1)} %get-tuple-element.118.prob_all, ...), custom_call_target="tpu_custom_call" | custom-call | flops 1 | bytes 1 | tf_op jit(solution)/shard_map/back/pallas_call | solution.py:437
  285.8 2.3 add_convert_fusion.refs_3_
  292.4 12.5 %back.5 = (bf16[2048,2304]{1,0:T(8,128)(2,1)}, bf16[256,768]{1,0:T(8,128)(2,1)}, f32[8,768]{1,0:T(8,128)}) custom-call(s32[4]{0:T(128)} %pad_add_fusion.1.where, bf16[2048,2304]{1,0:T(8,128)(2,1)} %get-tuple-element.117.qkv_all, bf16[16,6,128,256]{3,2,1,0:T(8,128)(2,1)} %get-tuple-element.118.prob_all, ...), custom_call_target="tpu_custom_call", output_to_operand_aliasing={{0}: (7, {})} | custom-call | flops 1 | bytes 1 | tf_op jit(solution)/shard_map/back/pallas_call | solution.py:437
  304.9 2.9 collective-permute-start.29
  307.8 12.5 %back.6 = (bf16[2048,2304]{1,0:T(8,128)(2,1)}, bf16[256,768]{1,0:T(8,128)(2,1)}, f32[8,768]{1,0:T(8,128)}) custom-call(s32[4]{0:T(128)} %pad_add_fusion.1.where, bf16[2048,2304]{1,0:T(8,128)(2,1)} %get-tuple-element.117.qkv_all, bf16[16,6,128,256]{3,2,1,0:T(8,128)(2,1)} %get-tuple-element.118.prob_all, ...), custom_call_target="tpu_custom_call", output_to_operand_aliasing={{0}: (7, {})} | custom-call | flops 1 | bytes 1 | tf_op jit(solution)/shard_map/back/pallas_call | solution.py:437
  330.7 12.5 %back.7 = (bf16[2048,2304]{1,0:T(8,128)(2,1)}, bf16[256,768]{1,0:T(8,128)(2,1)}, f32[8,768]{1,0:T(8,128)}) custom-call(s32[4]{0:T(128)} %pad_add_fusion.1.where, bf16[2048,2304]{1,0:T(8,128)(2,1)} %get-tuple-element.117.qkv_all, bf16[16,6,128,256]{3,2,1,0:T(8,128)(2,1)} %get-tuple-element.118.prob_all, ...), custom_call_target="tpu_custom_call", output_to_operand_aliasing={{0}: (7, {})} | custom-call | flops 1 | bytes 1 | tf_op jit(solution)/shard_map/back/pallas_call | solution.py:437
  348.2 2.3 collective-permute-start.33
  352.0 13.8 %proj_grads.1 = (bf16[4,4,160,384]{3,2,1,0:T(8,128)(2,1)}, bf16[4,4,160,384]{3,2,1,0:T(8,128)(2,1)}) custom-call(s32[4]{0:T(128)} %pad_add_fusion.1.where, bf16[2048,2304]{1,0:T(8,128)(2,1)} %get-tuple-element.172.dqkv.dqkv_all, bf16[2048,768]{1,0:T(8,128)(2,1)} %get-tuple-element.120.x_all.x, bf16[16,16,768]{2,1,0:T(8,128)(2,1)} %convert_element_type.258.tiny, ...), custom_call_target="tpu_custom_call" | custom-call | flops 1 | bytes 1 | tf_op jit(solution)/shard_map/proj_grads/pallas_call | solution.py:620
  367.9 2.3 collective-permute-start.36
  375.9 17.5 %collective-permute-done.39 = bf16[1,1,9,48,384]{4,3,2,1,0:T(8,128)(2,1)S(1)} collective-permute-done((bf16[1,1,9,48,384]{4,3,2,1,0:T(8,128)(2,1)S(1)}, bf16[1,1,9,48,384]{4,3,2,1,0:T(8,128)(2,1)S(1)}, u32[]{:S(2)}, u32[]{:S(2)}) %collective-permute-start.39) | collective-permute-done | bytes 331808 | tf_op jit(solution)/shard_map/ppermute | solution.py:644
  402.5 10.4 %finish.1 = (f32[2048,768]{1,0:T(8,128)}, bf16[2048,768]{1,0:T(8,128)(2,1)}) custom-call(s32[4]{0:T(128)} %pad_add_fusion.1.where, bf16[2048,2304]{1,0:T(8,128)(2,1)} %get-tuple-element.172.dqkv.dqkv_all, bf16[2048,768]{1,0:T(8,128)(2,1)} %get-tuple-element.145.dbranch_all.dbranch, ...), custom_call_target="tpu_custom_call", output_to_operand_aliasing={{1}: (5, {})} | custom-call | flops 1 | bytes 1 | tf_op jit(solution)/shard_map/finish/pallas_call | solution.py:502
  (217 shorter events, 80.2 us)
Async XLA Ops:
  13.2 34.9 %collective-permute-start.1 = (bf16[488,768]{1,0:T(8,128)(2,1)S(1)}, bf16[488,768]{1,0:T(8,128)(2,1)S(1)}, u32[]{:S(2)}, u32[]{:S(2)}) collective-permute-start(bf16[488,768]{1,0:T(8,128)(2,1)S(1)} %fusion.7), channel_id=1, source_target_pairs={{0,16},{2,18},{4,20},{6,22},{8,24},{10,26},{12,28},{14,30},{16,0},... | collective-permute-start | bytes 2248712 | tf_op jit(solution)/shard_map/ppermute | solution.py:644
  13.4 20.9 %collective-permute-start.4 = (bf16[2,160,384]{2,1,0:T(8,128)(2,1)S(1)}, bf16[2,160,384]{2,1,0:T(8,128)(2,1)S(1)}, u32[]{:S(2)}, u32[]{:S(2)}) collective-permute-start(bf16[2,160,384]{2,1,0:T(8,128)(2,1)S(1)} %pad_maximum_fusion.10), channel_id=1, source_target_pairs={{0,8},{2,10},{4,12},{6,14},{8,0},{10,2},{12,4},{14,6},{16,24},{18,... | collective-permute-start | bytes 737288 | tf_op jit(solution)/shard_map/ppermute | solution.py:644
  35.8 21.7 %collective-permute-start.6 = (bf16[4,160,384]{2,1,0:T(8,128)(2,1)S(1)}, bf16[4,160,384]{2,1,0:T(8,128)(2,1)S(1)}, u32[]{:S(2)}, u32[]{:S(2)}) collective-permute-start(bf16[4,160,384]{2,1,0:T(8,128)(2,1)S(1)} %bitcast.160), channel_id=1, source_target_pairs={{0,4},{1,5},{2,6},{3,7},{4,0},{5,1},{6,2},{7,3},{8,12},{9,13},{10,... | collective-permute-start | bytes 1474568 | tf_op jit(solution)/shard_map/ppermute | solution.py:651
  37.3 20.2 %collective-permute-start.7 = (bf16[4,160,384]{2,1,0:T(8,128)(2,1)S(1)}, bf16[4,160,384]{2,1,0:T(8,128)(2,1)S(1)}, u32[]{:S(2)}, u32[]{:S(2)}) collective-permute-start(bf16[4,160,384]{2,1,0:T(8,128)(2,1)S(1)} %bitcast.161), channel_id=1, source_target_pairs={{0,5},{1,4},{2,7},{3,6},{4,1},{5,0},{6,3},{7,2},{8,13},{9,12},{10,... | collective-permute-start | bytes 1474568 | tf_op jit(solution)/shard_map/ppermute | solution.py:651
  57.8 33.5 %collective-permute-start.8 = (bf16[4,4,160,384]{3,2,1,0:T(8,128)(2,1)S(1)}, bf16[4,4,160,384]{3,2,1,0:T(8,128)(2,1)}, u32[]{:S(2)}, u32[]{:S(2)}) collective-permute-start(bf16[4,4,160,384]{3,2,1,0:T(8,128)(2,1)S(1)} %pad_maximum_fusion.refs_0_), channel_id=1, source_target_pairs={{0,2},{1,3},{2,0},{3,1},{4,6},{5,7},{6,4},{7,5},{8,10},{9,11},{10,... | collective-permute-start | bytes 5898248 | tf_op jit(solution)/shard_map/ppermute | solution.py:651
  57.9 24.4 %collective-permute-start.2 = (bf16[256,768]{1,0:T(8,128)(2,1)}, bf16[256,768]{1,0:T(8,128)(2,1)}, u32[]{:S(2)}, u32[]{:S(2)}) collective-permute-start(bf16[256,768]{1,0:T(8,128)(2,1)} %get-tuple-element.202), channel_id=1, source_target_pairs={{0,16},{2,18},{4,20},{6,22},{8,24},{10,26},{12,28},{14,30},{16,0},... | collective-permute-start | bytes 1179656 | tf_op jit(solution)/shard_map/ppermute | solution.py:644
  66.2 22.5 %collective-permute-start.12 = (bf16[4,5,48,384]{3,2,1,0:T(8,128)(2,1)}, bf16[4,5,48,384]{3,2,1,0:T(8,128)(2,1)S(1)}, u32[]{:S(2)}, u32[]{:S(2)}) collective-permute-start(bf16[4,5,48,384]{3,2,1,0:T(8,128)(2,1)} %get-tuple-element.208), channel_id=1, source_target_pairs={{0,1},{1,0},{2,3},{3,2},{4,5},{5,4},{6,7},{7,6},{8,9},{9,8},{10,11... | collective-permute-start | bytes 2211848 | tf_op jit(solution)/shard_map/ppermute | solution.py:651
  68.4 18.1 %collective-permute-start.14 = (bf16[4,4,48,384]{3,2,1,0:T(8,128)(2,1)}, bf16[4,4,48,384]{3,2,1,0:T(8,128)(2,1)}, u32[]{:S(2)}, u32[]{:S(2)}) collective-permute-start(bf16[4,4,48,384]{3,2,1,0:T(8,128)(2,1)} %get-tuple-element.206), channel_id=1, source_target_pairs={{0,4},{1,5},{2,6},{3,7},{4,0},{5,1},{6,2},{7,3},{8,12},{9,13},{10,... | collective-permute-start | bytes 1769480 | tf_op jit(solution)/shard_map/ppermute | solution.py:651
  82.2 37.1 %collective-permute-start.9 = (bf16[256,768]{1,0:T(8,128)(2,1)}, bf16[256,768]{1,0:T(8,128)(2,1)}, u32[]{:S(2)}, u32[]{:S(2)}) collective-permute-start(bf16[256,768]{1,0:T(8,128)(2,1)} %get-tuple-element.104), channel_id=1, source_target_pairs={{0,16},{2,18},{4,20},{6,22},{8,24},{10,26},{12,28},{14,30},{16,0},... | collective-permute-start | bytes 1179656 | tf_op jit(solution)/shard_map/ppermute | solution.py:644
  82.3 46.8 %collective-permute-start.3 = (bf16[256,768]{1,0:T(8,128)(2,1)}, bf16[256,768]{1,0:T(8,128)(2,1)}, u32[]{:S(2)}, u32[]{:S(2)}) collective-permute-start(bf16[256,768]{1,0:T(8,128)(2,1)} %get-tuple-element.103), channel_id=1, source_target_pairs={{0,16},{2,18},{4,20},{6,22},{8,24},{10,26},{12,28},{14,30},{16,0},... | collective-permute-start | bytes 1179656 | tf_op jit(solution)/shard_map/ppermute | solution.py:644
  86.5 49.7 %collective-permute-start.16 = (bf16[256,768]{1,0:T(8,128)(2,1)}, bf16[256,768]{1,0:T(8,128)(2,1)}, u32[]{:S(2)}, u32[]{:S(2)}) collective-permute-start(bf16[256,768]{1,0:T(8,128)(2,1)} %get-tuple-element.123), channel_id=1, source_target_pairs={{0,16},{2,18},{4,20},{6,22},{8,24},{10,26},{12,28},{14,30},{16,0},... | collective-permute-start | bytes 1179656 | tf_op jit(solution)/shard_map/ppermute | solution.py:644
  88.7 47.4 %collective-permute-start.15 = (bf16[2,4,4,48,384]{4,3,2,1,0:T(8,128)(2,1)}, bf16[2,4,4,48,384]{4,3,2,1,0:T(8,128)(2,1)}, u32[]{:S(2)}, u32[]{:S(2)}) collective-permute-start(bf16[2,4,4,48,384]{4,3,2,1,0:T(8,128)(2,1)} %pad_maximum_fusion.4.refs_2_), channel_id=1, source_target_pairs={{0,1},{1,0},{2,3},{3,2},{4,5},{5,4},{6,7},{7,6},{8,9},{9,8},{10,11... | collective-permute-start | bytes 3538952 | tf_op jit(solution)/shard_map/ppermute | solution.py:651
  91.3 44.9 %collective-permute-start.13 = (bf16[2,4,5,48,384]{4,3,2,1,0:T(8,128)(2,1)S(1)}, bf16[2,4,5,48,384]{4,3,2,1,0:T(8,128)(2,1)S(1)}, u32[]{:S(2)}, u32[]{:S(2)}) collective-permute-start(bf16[2,4,5,48,384]{4,3,2,1,0:T(8,128)(2,1)S(1)} %pad_maximum_fusion.1.refs_0_), channel_id=1, source_target_pairs={{0,4},{1,5},{2,6},{3,7},{4,0},{5,1},{6,2},{7,3},{8,12},{9,13},{10,... | collective-permute-start | bytes 4423688 | tf_op jit(solution)/shard_map/ppermute | solution.py:651
  136.3 16.9 %collective-permute-start.17 = (bf16[2,4,5,48,384]{4,3,2,1,0:T(8,128)(2,1)S(1)}, bf16[2,4,5,48,384]{4,3,2,1,0:T(8,128)(2,1)}, u32[]{:S(2)}, u32[]{:S(2)}) collective-permute-start(bf16[2,4,5,48,384]{4,3,2,1,0:T(8,128)(2,1)S(1)} %pad_maximum_fusion.1.refs_0_), channel_id=1, source_target_pairs={{0,2},{1,3},{2,0},{3,1},{4,6},{5,7},{6,4},{7,5},{8,10},{9,11},{10,... | collective-permute-start | bytes 4423688 | tf_op jit(solution)/shard_map/ppermute | solution.py:651
  136.7 16.4 %collective-permute-start.18 = (bf16[2,4,5,48,384]{4,3,2,1,0:T(8,128)(2,1)S(1)}, bf16[2,4,5,48,384]{4,3,2,1,0:T(8,128)(2,1)}, u32[]{:S(2)}, u32[]{:S(2)}) collective-permute-start(bf16[2,4,5,48,384]{4,3,2,1,0:T(8,128)(2,1)S(1)} %collective-permute-done.13.refs_1_), channel_id=1, source_target_pairs={{0,2},{1,3},{2,0},{3,1},{4,6},{5,7},{6,4},{7,5},{8,10},{9,11},{10,... | collective-permute-start | bytes 4423688 | tf_op jit(solution)/shard_map/ppermute | solution.py:651
  139.3 36.7 %collective-permute-start.21 = (bf16[256,768]{1,0:T(8,128)(2,1)}, bf16[256,768]{1,0:T(8,128)(2,1)S(1)}, u32[]{:S(2)}, u32[]{:S(2)}) collective-permute-start(bf16[256,768]{1,0:T(8,128)(2,1)} %get-tuple-element.128), channel_id=1, source_target_pairs={{0,16},{2,18},{4,20},{6,22},{8,24},{10,26},{12,28},{14,30},{16,0},... | collective-permute-start | bytes 1179656 | tf_op jit(solution)/shard_map/ppermute | solution.py:644
  140.2 56.7 %collective-permute-start.10 = (bf16[512,768]{1,0:T(8,128)(2,1)}, bf16[512,768]{1,0:T(8,128)(2,1)}, u32[]{:S(2)}, u32[]{:S(2)}) collective-permute-start(bf16[512,768]{1,0:T(8,128)(2,1)} %constant_dynamic-slice_fusion.3), channel_id=1, source_target_pairs={{0,16},{2,18},{4,20},{6,22},{8,24},{10,26},{12,28},{14,30},{16,0},... | collective-permute-start | bytes 2359304 | tf_op jit(solution)/shard_map/ppermute | solution.py:644
  196.8 38.6 %collective-permute-start.22 = (bf16[512,768]{1,0:T(8,128)(2,1)}, bf16[512,768]{1,0:T(8,128)(2,1)S(1)}, u32[]{:S(2)}, u32[]{:S(2)}) collective-permute-start(bf16[512,768]{1,0:T(8,128)(2,1)} %get-tuple-element.152), channel_id=1, source_target_pairs={{0,16},{2,18},{4,20},{6,22},{8,24},{10,26},{12,28},{14,30},{16,0},... | collective-permute-start | bytes 2359304 | tf_op jit(solution)/shard_map/ppermute | solution.py:644
  232.6 37.4 %collective-permute-start.23 = (bf16[512,768]{1,0:T(8,128)(2,1)}, bf16[512,768]{1,0:T(8,128)(2,1)S(1)}, u32[]{:S(2)}, u32[]{:S(2)}) collective-permute-start(bf16[512,768]{1,0:T(8,128)(2,1)} %get-tuple-element.157), channel_id=1, source_target_pairs={{0,16},{2,18},{4,20},{6,22},{8,24},{10,26},{12,28},{14,30},{16,0},... | collective-permute-start | bytes 2359304 | tf_op jit(solution)/shard_map/ppermute | solution.py:644
  288.1 34.4 %collective-permute-start.26 = (bf16[2,4,5,48,384]{4,3,2,1,0:T(8,128)(2,1)S(1)}, bf16[2,4,5,48,384]{4,3,2,1,0:T(8,128)(2,1)}, u32[]{:S(2)}, u32[]{:S(2)}) collective-permute-start(bf16[2,4,5,48,384]{4,3,2,1,0:T(8,128)(2,1)S(1)} %add_convert_fusion.refs_3_), channel_id=1, source_target_pairs={{0,4},{1,5},{2,6},{3,7},{4,0},{5,1},{6,2},{7,3},{8,12},{9,13},{10,... | collective-permute-start | bytes 4423688 | tf_op jit(solution)/shard_map/ppermute | solution.py:651
  291.2 29.2 %collective-permute-start.27 = (bf16[2,4,4,48,384]{4,3,2,1,0:T(8,128)(2,1)S(1)}, bf16[2,4,4,48,384]{4,3,2,1,0:T(8,128)(2,1)}, u32[]{:S(2)}, u32[]{:S(2)}) collective-permute-start(bf16[2,4,4,48,384]{4,3,2,1,0:T(8,128)(2,1)S(1)} %add_convert_fusion.1.refs_4_), channel_id=1, source_target_pairs={{0,1},{1,0},{2,3},{3,2},{4,5},{5,4},{6,7},{7,6},{8,9},{9,8},{10,11... | collective-permute-start | bytes 3538952 | tf_op jit(solution)/shard_map/ppermute | solution.py:651
  292.3 37.5 %collective-permute-start.28 = (bf16[256,768]{1,0:T(8,128)(2,1)}, bf16[256,768]{1,0:T(8,128)(2,1)S(1)}, u32[]{:S(2)}, u32[]{:S(2)}) collective-permute-start(bf16[256,768]{1,0:T(8,128)(2,1)} %get-tuple-element.170), channel_id=1, source_target_pairs={{0,16},{2,18},{4,20},{6,22},{8,24},{10,26},{12,28},{14,30},{16,0},... | collective-permute-start | bytes 1179656 | tf_op jit(solution)/shard_map/ppermute | solution.py:644
  304.9 24.9 %collective-permute-start.29 = (bf16[256,768]{1,0:T(8,128)(2,1)}, bf16[256,768]{1,0:T(8,128)(2,1)S(1)}, u32[]{:S(2)}, u32[]{:S(2)}) collective-permute-start(bf16[256,768]{1,0:T(8,128)(2,1)} %get-tuple-element.171), channel_id=1, source_target_pairs={{0,16},{2,18},{4,20},{6,22},{8,24},{10,26},{12,28},{14,30},{16,0},... | collective-permute-start | bytes 1179656 | tf_op jit(solution)/shard_map/ppermute | solution.py:644
  324.4 19.9 %collective-permute-start.31 = (bf16[4,5,48,384]{3,2,1,0:T(8,128)(2,1)S(1)}, bf16[4,5,48,384]{3,2,1,0:T(8,128)(2,1)S(1)}, u32[]{:S(2)}, u32[]{:S(2)}) collective-permute-start(bf16[4,5,48,384]{3,2,1,0:T(8,128)(2,1)S(1)} %fusion.8.refs_3_), channel_id=1, source_target_pairs={{0,1},{1,0},{2,3},{3,2},{4,5},{5,4},{6,7},{7,6},{8,9},{9,8},{10,11... | collective-permute-start | bytes 2211848 | tf_op jit(solution)/shard_map/ppermute | solution.py:651
  327.3 16.9 %collective-permute-start.32 = (bf16[4,4,48,384]{3,2,1,0:T(8,128)(2,1)S(1)}, bf16[4,4,48,384]{3,2,1,0:T(8,128)(2,1)S(1)}, u32[]{:S(2)}, u32[]{:S(2)}) collective-permute-start(bf16[4,4,48,384]{3,2,1,0:T(8,128)(2,1)S(1)} %fusion.9.refs_4_), channel_id=1, source_target_pairs={{0,4},{1,5},{2,6},{3,7},{4,0},{5,1},{6,2},{7,3},{8,12},{9,13},{10,... | collective-permute-start | bytes 1769480 | tf_op jit(solution)/shard_map/ppermute | solution.py:651
  329.7 36.1 %collective-permute-start.30 = (bf16[256,768]{1,0:T(8,128)(2,1)}, bf16[256,768]{1,0:T(8,128)(2,1)}, u32[]{:S(2)}, u32[]{:S(2)}) collective-permute-start(bf16[256,768]{1,0:T(8,128)(2,1)} %get-tuple-element.174), channel_id=1, source_target_pairs={{0,16},{2,18},{4,20},{6,22},{8,24},{10,26},{12,28},{14,30},{16,0},... | collective-permute-start | bytes 1179656 | tf_op jit(solution)/shard_map/ppermute | solution.py:644
  348.2 17.6 %collective-permute-start.33 = (bf16[2,1,9,48,384]{4,3,2,1,0:T(8,128)(2,1)S(1)}, bf16[2,1,9,48,384]{4,3,2,1,0:T(8,128)(2,1)}, u32[]{:S(2)}, u32[]{:S(2)}) collective-permute-start(bf16[2,1,9,48,384]{4,3,2,1,0:T(8,128)(2,1)S(1)} %constant_dynamic-slice_fusion), channel_id=1, source_target_pairs={{0,8},{2,10},{4,12},{6,14},{8,0},{10,2},{12,4},{14,6},{16,24},{18,... | collective-permute-start | bytes 1990664 | tf_op jit(solution)/shard_map/ppermute | solution.py:644
  367.2 26.2 %collective-permute-start.39 = (bf16[1,1,9,48,384]{4,3,2,1,0:T(8,128)(2,1)S(1)}, bf16[1,1,9,48,384]{4,3,2,1,0:T(8,128)(2,1)S(1)}, u32[]{:S(2)}, u32[]{:S(2)}) collective-permute-start(bf16[1,1,9,48,384]{4,3,2,1,0:T(8,128)(2,1)S(1)} %dynamic-slice_convert_fusion), channel_id=1, source_target_pairs={{0,16},{2,18},{4,20},{6,22},{8,24},{10,26},{12,28},{14,30},{16,0},... | collective-permute-start | bytes 995336 | tf_op jit(solution)/shard_map/ppermute | solution.py:644
  367.9 45.0 %collective-permute-start.36 = (bf16[256,768]{1,0:T(8,128)(2,1)}, bf16[256,768]{1,0:T(8,128)(2,1)S(1)}, u32[]{:S(2)}, u32[]{:S(2)}) collective-permute-start(bf16[256,768]{1,0:T(8,128)(2,1)} %get-tuple-element.192), channel_id=1, source_target_pairs={{0,16},{2,18},{4,20},{6,22},{8,24},{10,26},{12,28},{14,30},{16,0},... | collective-permute-start | bytes 1179656 | tf_op jit(solution)/shard_map/ppermute | solution.py:644
  372.3 23.2 %collective-permute-start.35 = (bf16[4,160,384]{2,1,0:T(8,128)(2,1)S(1)}, bf16[4,160,384]{2,1,0:T(8,128)(2,1)S(1)}, u32[]{:S(2)}, u32[]{:S(2)}) collective-permute-start(bf16[4,160,384]{2,1,0:T(8,128)(2,1)S(1)} %get-tuple-element.189), channel_id=1, source_target_pairs={{0,1},{1,0},{2,3},{3,2},{4,5},{5,4},{6,7},{7,6},{8,9},{9,8},{10,11... | collective-permute-start | bytes 1474568 | tf_op jit(solution)/shard_map/ppermute | solution.py:651
  373.8 23.5 %collective-permute-start.37 = (bf16[4,160,384]{2,1,0:T(8,128)(2,1)S(1)}, bf16[4,160,384]{2,1,0:T(8,128)(2,1)S(1)}, u32[]{:S(2)}, u32[]{:S(2)}) collective-permute-start(bf16[4,160,384]{2,1,0:T(8,128)(2,1)S(1)} %get-tuple-element.193), channel_id=1, source_target_pairs={{0,4},{1,5},{2,6},{3,7},{4,0},{5,1},{6,2},{7,3},{8,12},{9,13},{10,... | collective-permute-start | bytes 1474568 | tf_op jit(solution)/shard_map/ppermute | solution.py:651
  374.4 23.0 %collective-permute-start.38 = (bf16[4,160,384]{2,1,0:T(8,128)(2,1)S(1)}, bf16[4,160,384]{2,1,0:T(8,128)(2,1)S(1)}, u32[]{:S(2)}, u32[]{:S(2)}) collective-permute-start(bf16[4,160,384]{2,1,0:T(8,128)(2,1)S(1)} %get-tuple-element.194), channel_id=1, source_target_pairs={{0,5},{1,4},{2,7},{3,6},{4,1},{5,0},{6,3},{7,2},{8,13},{9,12},{10,... | collective-permute-start | bytes 1474568 | tf_op jit(solution)/shard_map/ppermute | solution.py:651
  (40 other events, 390.0 us)
